TPU v7x, 256 devices: a whole 4x4x8 slice. The times are simulated.
256 devices in a mesh: panel: 2 (over core), lat: 8 (over y_hi, x), lon: 16 (over y_lo, z).
Axes of the slice: x: 4, y: 4 (y_hi: 2, y_lo: 2; y = y_hi * 2 + y_lo), z: 8, core: 2. Of those that a mesh axis runs over, the one named last changes fastest.
Arguments:
- scalars: float32 [2, 2, 24, 128, 2048], P('panel', None, None, 'lat', 'lon'), may hold values from 0.5 to 2
- vectors: float32 [2, 6, 24, 128, 2048], P('panel', None, None, 'lat', 'lon'), may hold values from -4 to 4
- corner_rows: int32 [8, 16, 16, 19], P('lat', 'lon'), may hold values from 0 to 14
- corner_cols: int32 [8, 16, 16, 19], P('lat', 'lon'), may hold values from 0 to 126
- send_weights: float32 [2, 8, 16, 16, 19], P(None, 'lat', 'lon'), may hold values from 0 to 1
- recv_source: int32 [8, 16, 592], P('lat', 'lon'), may hold values from -1 to 303, as said below
Outputs:
- scalar_rate: float32 [2, 2, 24, 128, 2048], P('panel', None, None, 'lat', 'lon')
- vector_rate: float32 [2, 6, 24, 128, 2048], P('panel', None, None, 'lat', 'lon')
Inputs may be any that keep to these rules, and one draw needn't show every extreme that they name: `recv_source`: -1 exactly at the frame cells of block (i, r) that lie inside the panel; every other entry is q * 19 + j, slot j of donor block q of the same lat row on the other panel; no (q, j) twice for one block; some block takes all 19 slots of one donor; one table serves both panels.
All inputs are finite; a program needn't handle non-finite values.
Results may differ from a plain program's by a relative error of at most 0.0003.
Values sent between devices are 32-bit elements; how exact they have to be, the bound alone decides.
No kernel may reach another device: no remote copies, remote signals or barrier semaphores. Data moves between devices by JAX's collectives and lax.ppermute only.
A program may use at most 128 MiB of HBM per device.

v0:
```python
import math

import jax
import jax.numpy as jnp
from jax import lax
from jax.sharding import PartitionSpec as P

GAMMA = 5.0 / 3.0
shell_block = 8


def swapped(block, axis, distance):
    count = lax.axis_size(axis)
    route = []
    for low in range(count):
        high = low | 1 << distance
        if high != low and high < count:
            route += [(low, high), (high, low)]
    return lax.ppermute(block, axis, route)


def with_halo(cells, sides, width):
    for axis, dim in sides:
        count = lax.axis_size(axis)
        ends = count - 1
        head = lax.slice_in_dim(cells, 0, width, axis=dim)
        tail = lax.slice_in_dim(cells, cells.shape[dim] - width, cells.shape[dim], axis=dim)
        cells = jnp.concatenate(
            [
                lax.ppermute(tail, axis, [(i, (i + 1) % count) for i in range(ends)]),
                cells,
                lax.ppermute(head, axis, [((i + 1) % count, i) for i in range(ends)]),
            ],
            axis=dim,
        )
    return cells


def spacing(n_theta, n_phi):
    step_theta = 0.5 * math.pi / n_theta
    step_phi = 1.5 * math.pi / n_phi
    step_radius = 0.6 * step_theta
    smallest = min(step_radius, 0.6 * math.sin(0.25 * math.pi - 2.0 * step_theta) * step_phi)
    return (step_theta, step_phi, step_radius, 0.3 * smallest)


def angle_at(index_vals, anchor, step_size):
    return anchor + (index_vals.astype(jnp.float32) + 0.5) * step_size


def coordinate(first_row, length, anchor, step_size):
    return angle_at(jnp.arange(length, dtype=jnp.int32) + first_row, anchor, step_size)


def crop_one(field_in):
    return field_in[..., 1:-1, 1:-1, 1:-1]


def level_geometry(coords, cut):
    radius_all, theta_all, phi_all = coords
    radius = radius_all[cut : radius_all.shape[0] - cut][:, None, None]
    theta_vals = theta_all[cut : theta_all.shape[0] - cut][None, :, None]
    phi_vals = phi_all[cut : phi_all.shape[0] - cut][None, None, :]
    sin_the = jnp.sin(theta_vals)
    cos_the = jnp.cos(theta_vals)
    return (radius, sin_the, cos_the / sin_the, phi_vals, cos_the)


def derivatives(field_in, geometry, spacings):
    radius, sin_the = (geometry[0], geometry[1])
    d_rad = (field_in[..., 2:, 1:-1, 1:-1] - field_in[..., :-2, 1:-1, 1:-1]) / (2.0 * spacings[2])
    d_the = (field_in[..., 1:-1, 2:, 1:-1] - field_in[..., 1:-1, :-2, 1:-1]) / (
        2.0 * spacings[0] * radius
    )
    d_phi = (field_in[..., 1:-1, 1:-1, 2:] - field_in[..., 1:-1, 1:-1, :-2]) / (
        2.0 * spacings[1] * radius * sin_the
    )
    return (d_rad, d_the, d_phi)


def curl_of(vector, geometry, spacings):
    d_rad, d_the, d_phi = derivatives(vector, geometry, spacings)
    middle = crop_one(vector)
    radius, cot_the = (geometry[0], geometry[2])
    return jnp.stack(
        [
            d_the[2] + middle[2] * cot_the / radius - d_phi[1],
            d_phi[0] - d_rad[2] - middle[2] / radius,
            d_rad[1] + middle[1] / radius - d_the[0],
        ]
    )


def divergence(vector, geometry, spacings):
    d_rad, d_the, d_phi = derivatives(vector, geometry, spacings)
    middle = crop_one(vector)
    radius, cot_the = (geometry[0], geometry[2])
    return d_rad[0] + 2.0 * middle[0] / radius + d_the[1] + middle[1] * cot_the / radius + d_phi[2]


def cross_product(first_vec, second_vec):
    return jnp.stack(
        [
            first_vec[1] * second_vec[2] - first_vec[2] * second_vec[1],
            first_vec[2] * second_vec[0] - first_vec[0] * second_vec[2],
            first_vec[0] * second_vec[1] - first_vec[1] * second_vec[0],
        ]
    )


def tendency(slab_state, coords, yang_flag, spacings):
    time_step = spacings[3]
    viscosity = time_step / 0.9
    gravity = 0.036 / time_step
    rotation = 0.05 / time_step
    outer = level_geometry(coords, 1)
    inner = level_geometry(coords, 2)
    velocity = slab_state[2:5]
    magnet = slab_state[5:8]
    current_one = curl_of(magnet, outer, spacings)
    vortic_one = curl_of(velocity, outer, spacings)
    expand_one = divergence(velocity, outer, spacings)
    density_one = crop_one(slab_state[0])
    pressure_one = crop_one(slab_state[1])
    velocity_one = crop_one(velocity)
    magnet_one = crop_one(magnet)
    electric_one = cross_product(velocity_one, magnet_one) - viscosity * current_one
    flux_one = density_one[None] * velocity_one
    radius, sin_the, cot_the, phi_vals, cos_the = inner
    density_zero = crop_one(density_one)
    pressure_zero = crop_one(pressure_one)
    velocity_zero = crop_one(velocity_one)
    magnet_zero = crop_one(magnet_one)
    mass_rate = -divergence(flux_one, inner, spacings)
    grad_rad, grad_the, grad_phi = derivatives(velocity_one, inner, spacings)
    advect = velocity_zero[0] * grad_rad + velocity_zero[1] * grad_the + velocity_zero[2] * grad_phi
    curvature = jnp.stack(
        [
            -(velocity_zero[1] * velocity_zero[1] + velocity_zero[2] * velocity_zero[2]) / radius,
            (velocity_zero[0] * velocity_zero[1] - velocity_zero[2] * velocity_zero[2] * cot_the)
            / radius,
            (velocity_zero[0] * velocity_zero[2] + velocity_zero[1] * velocity_zero[2] * cot_the)
            / radius,
        ]
    )
    press_grad = jnp.stack(derivatives(pressure_one, inner, spacings))
    expand_grad = jnp.stack(derivatives(expand_one, inner, spacings))
    twice_curl = curl_of(vortic_one, inner, spacings)
    out_shape = density_zero.shape
    spin_axis = jnp.stack(
        [
            jnp.broadcast_to(
                (1.0 - yang_flag) * cos_the + yang_flag * sin_the * jnp.sin(phi_vals), out_shape
            ),
            jnp.broadcast_to(
                (1.0 - yang_flag) * -sin_the + yang_flag * cos_the * jnp.sin(phi_vals), out_shape
            ),
            jnp.broadcast_to(yang_flag * jnp.cos(phi_vals), out_shape),
        ]
    )
    lorentz = cross_product(crop_one(current_one), magnet_zero)
    acceleration = (
        -(advect + curvature)
        + (lorentz - press_grad + viscosity * (4.0 / 3.0 * expand_grad - twice_curl))
        / density_zero[None]
        + 2.0 * rotation * cross_product(velocity_zero, spin_axis)
    )
    acceleration = jnp.stack(
        [acceleration[0] - gravity / (radius * radius), acceleration[1], acceleration[2]]
    )
    pressure_rate = -(
        velocity_zero[0] * press_grad[0]
        + velocity_zero[1] * press_grad[1]
        + velocity_zero[2] * press_grad[2]
    ) - GAMMA * pressure_zero * crop_one(expand_one)
    induction = curl_of(electric_one, inner, spacings)
    return (
        time_step * jnp.stack([mass_rate, pressure_rate]),
        time_step * jnp.concatenate([acceleration, induction], axis=0),
    )


def slab_rates(extended, theta_all, phi_all, yang_flag, spacings):
    shells = extended.shape[1]
    slab_count = shells // shell_block
    n_rows, n_cols = (extended.shape[2] - 4, extended.shape[3] - 4)

    def one_slab(slab_index, outputs):
        slab_start = (slab_index * shell_block).astype(jnp.int32)
        shell_ids = jnp.clip(
            slab_start - 2 + jnp.arange(shell_block + 4, dtype=jnp.int32), 0, shells - 1
        )
        slab_piece = jnp.take(extended, shell_ids, axis=1)
        radius_all = coordinate(slab_start - 2, shell_block + 4, 0.6, spacings[2])
        scalar_part, vector_part = tendency(
            slab_piece, (radius_all, theta_all, phi_all), yang_flag, spacings
        )
        return (
            lax.dynamic_update_slice_in_dim(outputs[0], scalar_part, slab_start, 1),
            lax.dynamic_update_slice_in_dim(outputs[1], vector_part, slab_start, 1),
        )

    start_vals = (
        jnp.zeros((2, shells, n_rows, n_cols), extended.dtype),
        jnp.zeros((6, shells, n_rows, n_cols), extended.dtype),
    )
    return lax.fori_loop(0, slab_count, one_slab, start_vals)


def to_cartesian(radial, polar_c, azimuth, theta_at, phi_at):
    sin_the, cos_the = (jnp.sin(theta_at), jnp.cos(theta_at))
    sin_phi, cos_phi = (jnp.sin(phi_at), jnp.cos(phi_at))
    along_x = radial * sin_the * cos_phi + polar_c * cos_the * cos_phi - azimuth * sin_phi
    along_y = radial * sin_the * sin_phi + polar_c * cos_the * sin_phi + azimuth * cos_phi
    along_z = radial * cos_the - polar_c * sin_the
    return (along_x, along_y, along_z)


def to_spherical(along_x, along_y, along_z, theta_at, phi_at):
    sin_the, cos_the = (jnp.sin(theta_at), jnp.cos(theta_at))
    sin_phi, cos_phi = (jnp.sin(phi_at), jnp.cos(phi_at))
    radial = along_x * sin_the * cos_phi + along_y * sin_the * sin_phi + along_z * cos_the
    polar_c = along_x * cos_the * cos_phi + along_y * cos_the * sin_phi - along_z * sin_the
    azimuth = -along_x * sin_phi + along_y * cos_phi
    return (radial, polar_c, azimuth)


def donor_table(own_state, theta_own, phi_own):
    shells, n_rows, n_cols = (own_state.shape[1], own_state.shape[2], own_state.shape[3])
    theta_at = theta_own[:, None]
    phi_at = phi_own[None, :]
    velocity = to_cartesian(own_state[2], own_state[3], own_state[4], theta_at, phi_at)
    magnet = to_cartesian(own_state[5], own_state[6], own_state[7], theta_at, phi_at)
    cartesian = jnp.stack(
        [
            own_state[0],
            own_state[1],
            velocity[0],
            velocity[1],
            velocity[2],
            magnet[0],
            magnet[1],
            magnet[2],
        ]
    )
    return cartesian.reshape(8 * shells, n_rows * n_cols)


def corner_terms(lookup, corner_row, corner_col, weights, n_cols):
    base_index = (corner_row * n_cols + corner_col).reshape(-1)
    weight_the = weights[0].reshape(1, -1)
    weight_phi = weights[1].reshape(1, -1)
    return [
        (1.0 - weight_the) * (1.0 - weight_phi) * jnp.take(lookup, base_index, axis=1),
        (1.0 - weight_the) * weight_phi * jnp.take(lookup, base_index + 1, axis=1),
        weight_the * (1.0 - weight_phi) * jnp.take(lookup, base_index + n_cols, axis=1),
        weight_the * weight_phi * jnp.take(lookup, base_index + n_cols + 1, axis=1),
    ]


def cycle_layout(n_rows, n_cols):
    all_cols = jnp.arange(n_cols + 4, dtype=jnp.int32)
    mid_rows = jnp.arange(n_rows, dtype=jnp.int32) + 2
    zero_row = jnp.zeros(n_cols + 4, jnp.int32)
    cycle_rows = jnp.concatenate(
        [
            zero_row,
            zero_row + 1,
            zero_row + n_rows + 2,
            zero_row + n_rows + 3,
            jnp.repeat(mid_rows, 2),
            jnp.repeat(mid_rows, 2),
        ]
    )
    pair_cols = jnp.arange(2 * n_rows, dtype=jnp.int32) % 2
    cycle_cols = jnp.concatenate(
        [all_cols, all_cols, all_cols, all_cols, pair_cols, pair_cols + n_cols + 2]
    )
    return (cycle_rows, cycle_cols)


def assemble(halo_block, cycle_vals, first_row, first_col, n_theta, n_phi, spacings):
    shells = halo_block.shape[1]
    n_rows, n_cols = (halo_block.shape[2] - 4, halo_block.shape[3] - 4)
    cycle_rows, cycle_cols = cycle_layout(n_rows, n_cols)
    grid_row = first_row - 2 + cycle_rows
    grid_col = first_col - 2 + cycle_cols
    theta_cycle = angle_at(grid_row, 0.25 * math.pi, spacings[0])[None, :]
    phi_cycle = angle_at(grid_col, -0.75 * math.pi, spacings[1])[None, :]
    values = cycle_vals.reshape(8, shells, cycle_rows.shape[0])
    velocity = to_spherical(-values[2], values[4], values[3], theta_cycle, phi_cycle)
    magnet = to_spherical(-values[5], values[7], values[6], theta_cycle, phi_cycle)
    cycle_fields = jnp.stack(
        [
            values[0],
            values[1],
            velocity[0],
            velocity[1],
            velocity[2],
            magnet[0],
            magnet[1],
            magnet[2],
        ]
    )
    outside = (grid_row < 0) | (grid_row >= n_theta) | (grid_col < 0) | (grid_col >= n_phi)
    current = halo_block[:, :, cycle_rows, cycle_cols]
    return halo_block.at[:, :, cycle_rows, cycle_cols].set(
        jnp.where(outside, cycle_fields, current)
    )


def deliver(payload):
    crossed = swapped(payload, "panel", 0)
    return lax.all_to_all(crossed, "lon", split_axis=1, concat_axis=1, tiled=True)


def body(scalars, vectors, corner_rows, corner_cols, send_weights, recv_source):
    n_rows = scalars.shape[3]
    n_cols = scalars.shape[4]
    n_theta = n_rows * lax.axis_size("lat")
    n_phi = n_cols * lax.axis_size("lon")
    spacings = spacing(n_theta, n_phi)
    lat_block = lax.axis_index("lat")
    lon_block = lax.axis_index("lon")
    yang_flag = lax.axis_index("panel").astype(jnp.float32)
    own_state = jnp.concatenate([scalars[0], vectors[0]], axis=0)
    first_row = lat_block * n_rows
    first_col = lon_block * n_cols
    lookup = donor_table(
        own_state,
        coordinate(first_row, n_rows, 0.25 * math.pi, spacings[0]),
        coordinate(first_col, n_cols, -0.75 * math.pi, spacings[1]),
    )
    corner_parts = corner_terms(
        lookup, corner_rows[0, 0], corner_cols[0, 0], send_weights[:, 0, 0], n_cols
    )
    dest_count = corner_rows.shape[2]
    slot_count = corner_rows.shape[3]
    row_width = lookup.shape[0]
    payload = jnp.concatenate(corner_parts, axis=0).reshape(4 * row_width, dest_count, slot_count)
    received = deliver(payload)
    flat_rows = received.reshape(received.shape[0], dest_count * slot_count)
    picked = jnp.take(flat_rows, jnp.maximum(recv_source[0, 0], 0), axis=1)
    cycle_vals = (
        picked[:row_width]
        + picked[row_width : 2 * row_width]
        + picked[2 * row_width : 3 * row_width]
        + picked[3 * row_width :]
    )
    halo_block = with_halo(own_state, (("lat", 2), ("lon", 3)), 2)
    extended = assemble(halo_block, cycle_vals, first_row, first_col, n_theta, n_phi, spacings)
    theta_all = coordinate(first_row - 2, n_rows + 4, 0.25 * math.pi, spacings[0])
    phi_all = coordinate(first_col - 2, n_cols + 4, -0.75 * math.pi, spacings[1])
    scalar_rate, vector_rate = slab_rates(extended, theta_all, phi_all, yang_flag, spacings)
    return (scalar_rate[None], vector_rate[None])


def solution(mesh):
    return jax.shard_map(
        body,
        mesh=mesh,
        in_specs=(
            P("panel", None, None, "lat", "lon"),
            P("panel", None, None, "lat", "lon"),
            P("lat", "lon", None, None),
            P("lat", "lon", None, None),
            P(None, "lat", "lon", None, None),
            P("lat", "lon", None),
        ),
        out_specs=(P("panel", None, None, "lat", "lon"), P("panel", None, None, "lat", "lon")),
        check_vma=False,
    )
```

profile of v0, /device:TPU:24, one launch (start us, length us, event | category | flops | bytes accessed | tf_op | source)
XLA Modules:
  0.0 220.6 jit_solution(3907057405272277067)
XLA Ops:
  3.6 1.2 fusion.83
  5.3 1.8 copy.333
  7.1 1.8 copy.316
  9.2 2.2 gather_fusion.6
  11.3 2.1 gather_fusion.5
  13.5 2.1 gather_fusion.4
  15.6 2.1 gather_fusion.3
  23.8 3.4 %collective-permute-start = (f32[8,24,2,128]{3,1,2,0:T(8,128)}, f32[8,24,2,128]{3,1,2,0:T(8,128)S(1)}, u32[]{:S(2)}, u32[]{:S(2)}) collective-permute-start(f32[8,24,2,128]{3,1,2,0:T(8,128)} %copy.326), channel_id=1, source_target_pairs={{0,16},{16,32},{32,48},{48,64},{64,80},{80,96},{96,112},{1,17},{17... | collective-permute-start | bytes 589832 | tf_op jit(solution)/shard_map/ppermute | solution.py:30
  27.9 6.0 %collective-permute-start.1 = (f32[8,24,2,128]{3,1,2,0:T(8,128)}, f32[8,24,2,128]{3,1,2,0:T(8,128)S(1)}, u32[]{:S(2)}, u32[]{:S(2)}) collective-permute-start(f32[8,24,2,128]{3,1,2,0:T(8,128)} %copy.327), channel_id=1, source_target_pairs={{16,0},{32,16},{48,32},{64,48},{80,64},{96,80},{112,96},{17,1},{33... | collective-permute-start | bytes 589832 | tf_op jit(solution)/shard_map/ppermute | solution.py:32
  37.9 2.8 %copy.321 = f32[768,16,19]{0,2,1:T(8,128)} copy(f32[768,16,19]{0,1,2:T(8,128)} %collective-permute-done.4) | data formatting | bytes 1867776 | tf_op jit(solution)/shard_map/ppermute | solution.py:19
  40.6 9.9 %all-to-all-start = ((f32[768,16,19]{0,2,1:T(8,128)}), f32[768,16,19]{0,2,1:T(8,128)}, u32[]{:S(2)}, u32[]{:S(2)}) async-start(f32[768,16,19]{0,2,1:T(8,128)} %copy.321), calls=%async_computation | async-start | bytes 2359296 | tf_op jit(solution)/shard_map/all_to_all | solution.py:314
  50.7 4.6 %copy.314 = f32[8,24,16,128]{1,0,3,2:T(8,128)} copy(f32[8,24,16,128]{3,2,1,0:T(8,128)S(1)} %pad_maximum_fusion.2) | data formatting | bytes 3145728 | tf_op jit(solution)/shard_map/concatenate | solution.py:326
  58.1 3.4 %collective-permute-start.2 = (f32[8,24,20,2]{1,0,3,2:T(8,128)S(1)}, f32[8,24,20,2]{1,0,3,2:T(8,128)S(1)}, u32[]{:S(2)}, u32[]{:S(2)}) collective-permute-start(f32[8,24,20,2]{1,0,3,2:T(8,128)S(1)} %get-tuple-element.414), channel_id=1, source_target_pairs={{0,1},{1,2},{2,3},{3,4},{4,5},{5,6},{6,7},{7,8},{8,9},{9,10},{10,1... | collective-permute-start | bytes 92168 | tf_op jit(solution)/shard_map/ppermute | solution.py:30
  61.4 4.8 %collective-permute-start.3 = (f32[8,24,20,2]{1,0,3,2:T(8,128)S(1)}, f32[8,24,20,2]{1,0,3,2:T(8,128)S(1)}, u32[]{:S(2)}, u32[]{:S(2)}) collective-permute-start(f32[8,24,20,2]{1,0,3,2:T(8,128)S(1)} %get-tuple-element.415), channel_id=1, source_target_pairs={{1,0},{2,1},{3,2},{4,3},{5,4},{6,5},{7,6},{8,7},{9,8},{10,9},{11,1... | collective-permute-start | bytes 92168 | tf_op jit(solution)/shard_map/ppermute | solution.py:32
  66.2 16.2 %collective-permute-done.2 = f32[8,24,20,2]{1,0,3,2:T(8,128)S(1)} collective-permute-done((f32[8,24,20,2]{1,0,3,2:T(8,128)S(1)}, f32[8,24,20,2]{1,0,3,2:T(8,128)S(1)}, u32[]{:S(2)}, u32[]{:S(2)}) %collective-permute-start.2) | collective-permute-done | bytes 30752 | tf_op jit(solution)/shard_map/ppermute | solution.py:30
  82.5 8.7 %pad_maximum_fusion.1 = f32[8,24,20,132]{1,0,3,2:T(8,128)} fusion(f32[8,24,20,2]{1,0,3,2:T(8,128)S(1)} %collective-permute-done.3, f32[8,24,2,128]{1,0,3,2:T(8,128)S(1)} %copy.315, f32[8,24,16,128]{1,0,3,2:T(8,128)} %copy.314, f32[8,24,2,128]{1,0,3,2:T(8,128)S(1)} %copy.313, f32[8,24,20,2]{1,0,3,2:T(8,128)S(1)} %collective-permute-done.2), kind=kLoop, calls=%fused_computation.183 | loop fusion | flops 2027520 | bytes 4055040 | tf_op jit(solution)/shard_map/concatenate | solution.py:28
  91.2 10.7 %gather_fusion.2 = f32[592,8,24]{2,1,0:T(8,128)} fusion(f32[8,24,20,132]{1,0,3,2:T(8,128)} %pad_maximum_fusion.1, s32[592]{0:T(1024)S(1)} %get-tuple-element.307), kind=kCustom, calls=%fused_computation.6 | custom fusion | bytes 914048 | tf_op jit(solution)/shard_map/gather | solution.py:306
  101.9 2.4 %copy.323 = f32[592,8,24]{0,2,1:T(8,128)S(1)} copy(f32[592,8,24]{2,1,0:T(8,128)} %gather_fusion.2) | data formatting | bytes 909312 | tf_op jit(solution)/shard_map/gather | solution.py:306
  104.3 1.4 reshape.1028
  105.7 2.6 %gather_fusion.1 = f32[592,768]{1,0:T(8,128)S(1)} fusion(f32[768,304]{0,1:T(8,128)S(1)} %reshape.1028, s32[1024]{0:T(1024)S(1)} %pad_clamp_fusion.1), kind=kCustom, calls=%fused_computation.5 | custom fusion | bytes 3639616 | tf_op jit(solution)/shard_map/jit(_take)/gather | solution.py:343
  108.4 1.9 copy.322
  110.2 1.7 select_bitcast_fusion
  112.3 2.3 %copy.324 = f32[592,8,24]{2,1,0:T(8,128)} copy(f32[592,8,24]{0,2,1:T(8,128)S(1)} %fusion.72) | data formatting | bytes 909312 | tf_op jit(solution)/shard_map/jit(_where)/select_n | solution.py:308
  114.6 61.2 %scatter_fusion = f32[8,24,20,132]{1,0,3,2:T(8,128)} fusion(f32[8,24,20,132]{1,0,3,2:T(8,128)} %pad_maximum_fusion.1, s32[592]{0:T(1024)S(1)} %get-tuple-element.308, f32[592,8,24]{2,1,0:T(8,128)} %copy.324), kind=kCustom, calls=%fused_computation.7 | custom fusion | bytes 1368704 | tf_op jit(solution)/shard_map/scatter | solution.py:307
  175.8 10.4 %copy.325 = f32[8,24,20,132]{3,0,2,1:T(8,128)} copy(f32[8,24,20,132]{1,0,3,2:T(8,128)} %scatter_fusion) | data formatting | bytes 4055040 | tf_op jit(solution)/shard_map/while | solution.py:207
  186.4 33.1 %while.17 = (s32[]{:T(128)}, f32[2,24,16,128]{3,2,1,0:T(8,128)S(1)}, f32[6,24,16,128]{3,2,1,0:T(8,128)S(1)}, f32[8,24,20,132]{3,0,2,1:T(8,128)}, f32[16]{0:T(128...) while((s32[]{:T(128)}, ...), condition=%wide.region_2.4_spmd, body=%wide.region_1.3_spmd.sunk | while | flops 6486438 | bytes 31139576 | solution.py:207
  186.7 2.8 %gather_fusion = f32[12,8,20,132]{3,1,2,0:T(8,128)S(1)} fusion(f32[8,24,20,132]{3,0,2,1:T(8,128)} %get-tuple-element.718, s32[1024]{0:T(1024)S(1)} %pad_clamp_fusion.7), kind=kCustom, calls=%fused_computation.1.clone.1 | custom fusion | bytes 2027568 | tf_op jit(solution)/shard_map/while/body/eval_jaxpr/jit(_take)/gather | solution.py:193
  190.6 2.2 %fusion.126 = (f32[3,10,18,130]{3,2,1,0:T(8,128)S(1)}, f32[3,10,18,130]{3,2,1,0:T(8,128)S(1)}, f32[3,10,18,130]{3,2,1,0:T(8,128)S(1)}, f32[3,10,18,130]{3,2,1,0:...) fusion(f32[8,12,20,132]{3,2,1,0:T(8,128)S(1)} %fusion.124, ...), kind=kLoop, calls=%fused_computation.11.clone.1 | loop fusion | flops 912600 | bytes 5710360 | tf_op jit(solution)/shard_map/while/body/eval_jaxpr/div | solution.py:72
  197.6 2.8 %gather_fusion = f32[12,8,20,132]{3,1,2,0:T(8,128)S(1)} fusion(f32[8,24,20,132]{3,0,2,1:T(8,128)} %get-tuple-element.718, s32[1024]{0:T(1024)S(1)} %pad_clamp_fusion.7), kind=kCustom, calls=%fused_computation.1.clone.1 | custom fusion | bytes 2027568 | tf_op jit(solution)/shard_map/while/body/eval_jaxpr/jit(_take)/gather | solution.py:193
  201.6 2.2 %fusion.126 = (f32[3,10,18,130]{3,2,1,0:T(8,128)S(1)}, f32[3,10,18,130]{3,2,1,0:T(8,128)S(1)}, f32[3,10,18,130]{3,2,1,0:T(8,128)S(1)}, f32[3,10,18,130]{3,2,1,0:...) fusion(f32[8,12,20,132]{3,2,1,0:T(8,128)S(1)} %fusion.124, ...), kind=kLoop, calls=%fused_computation.11.clone.1 | loop fusion | flops 912600 | bytes 5710360 | tf_op jit(solution)/shard_map/while/body/eval_jaxpr/div | solution.py:72
  208.6 2.8 %gather_fusion = f32[12,8,20,132]{3,1,2,0:T(8,128)S(1)} fusion(f32[8,24,20,132]{3,0,2,1:T(8,128)} %get-tuple-element.718, s32[1024]{0:T(1024)S(1)} %pad_clamp_fusion.7), kind=kCustom, calls=%fused_computation.1.clone.1 | custom fusion | bytes 2027568 | tf_op jit(solution)/shard_map/while/body/eval_jaxpr/jit(_take)/gather | solution.py:193
  212.5 2.2 %fusion.126 = (f32[3,10,18,130]{3,2,1,0:T(8,128)S(1)}, f32[3,10,18,130]{3,2,1,0:T(8,128)S(1)}, f32[3,10,18,130]{3,2,1,0:T(8,128)S(1)}, f32[3,10,18,130]{3,2,1,0:...) fusion(f32[8,12,20,132]{3,2,1,0:T(8,128)S(1)} %fusion.124, ...), kind=kLoop, calls=%fused_computation.11.clone.1 | loop fusion | flops 912600 | bytes 5710360 | tf_op jit(solution)/shard_map/while/body/eval_jaxpr/div | solution.py:72
  (246 shorter events, 35.5 us)
Async XLA Ops:
  0.6 4.2 %copy-start = (f32[1,6,24,16,128]{4,3,2,1,0:T(8,128)S(1)}, f32[1,6,24,16,128]{4,3,2,1,0:T(8,128)}, u32[]{:S(2)}) copy-start(f32[1,6,24,16,128]{4,3,2,1,0:T(8,128)} %param.11) | copy-start | bytes 3538948
  7.1 1.9 copy-start.8
  17.8 3.4 %copy-start.2 = (f32[304,192]{1,0:T(8,128)S(1)}, f32[304,192]{1,0:T(8,128)}, u32[]{:S(2)}) copy-start(f32[304,192]{1,0:T(8,128)} %gather_fusion.3) | copy-start | bytes 700420
  21.8 1.2 copy-start.1
  21.8 12.2 %copy-start.12 = (s32[1,1,592]{2,1,0:T(1,128)S(1)}, s32[1,1,592]{2,1,0:T(1,128)}, u32[]{:S(2)}) copy-start(s32[1,1,592]{2,1,0:T(1,128)} %param.15) | copy-start | bytes 7108
  23.0 14.9 %collective-permute-start.4 = (f32[768,16,19]{0,1,2:T(8,128)}, f32[768,16,19]{0,1,2:T(8,128)}, u32[]{:S(2)}, u32[]{:S(2)}) collective-permute-start(f32[768,16,19]{0,1,2:T(8,128)} %copy.320), channel_id=1, source_target_pairs={{0,128},{128,0},{1,129},{129,1},{2,130},{130,2},{3,131},{131,3},{4... | collective-permute-start | bytes 2801672 | tf_op jit(solution)/shard_map/ppermute | solution.py:19
  23.8 32.4 %collective-permute-start = (f32[8,24,2,128]{3,1,2,0:T(8,128)}, f32[8,24,2,128]{3,1,2,0:T(8,128)S(1)}, u32[]{:S(2)}, u32[]{:S(2)}) collective-permute-start(f32[8,24,2,128]{3,1,2,0:T(8,128)} %copy.326), channel_id=1, source_target_pairs={{0,16},{16,32},{32,48},{48,64},{64,80},{80,96},{96,112},{1,17},{17... | collective-permute-start | bytes 589832 | tf_op jit(solution)/shard_map/ppermute | solution.py:30
  27.9 28.7 %collective-permute-start.1 = (f32[8,24,2,128]{3,1,2,0:T(8,128)}, f32[8,24,2,128]{3,1,2,0:T(8,128)S(1)}, u32[]{:S(2)}, u32[]{:S(2)}) collective-permute-start(f32[8,24,2,128]{3,1,2,0:T(8,128)} %copy.327), channel_id=1, source_target_pairs={{16,0},{32,16},{48,32},{64,48},{80,64},{96,80},{112,96},{17,1},{33... | collective-permute-start | bytes 589832 | tf_op jit(solution)/shard_map/ppermute | solution.py:32
  35.6 1.5 copy-start.15
  40.6 63.7 %all-to-all-start = ((f32[768,16,19]{0,2,1:T(8,128)}), f32[768,16,19]{0,2,1:T(8,128)}, u32[]{:S(2)}, u32[]{:S(2)}) async-start(f32[768,16,19]{0,2,1:T(8,128)} %copy.321), calls=%async_computation | async-start | bytes 2359296 | tf_op jit(solution)/shard_map/all_to_all | solution.py:314
  50.7 4.9 %copy-start.16 = (f32[20]{0:T(128)S(1)}, f32[20]{0:T(128)}, u32[]{:S(2)}) copy-start(f32[20]{0:T(128)} %copy-done.15) | copy-start | bytes 244
  57.0 9.2 %copy-start.9 = (s32[592]{0:T(1024)S(1)}, s32[592]{0:T(1024)}, u32[]{:S(2)}) copy-start(s32[592]{0:T(1024)} %maximum_reduce_fusion) | copy-start | bytes 7108
  58.1 24.4 %collective-permute-start.2 = (f32[8,24,20,2]{1,0,3,2:T(8,128)S(1)}, f32[8,24,20,2]{1,0,3,2:T(8,128)S(1)}, u32[]{:S(2)}, u32[]{:S(2)}) collective-permute-start(f32[8,24,20,2]{1,0,3,2:T(8,128)S(1)} %get-tuple-element.414), channel_id=1, source_target_pairs={{0,1},{1,2},{2,3},{3,4},{4,5},{5,6},{6,7},{7,8},{8,9},{9,10},{10,1... | collective-permute-start | bytes 92168 | tf_op jit(solution)/shard_map/ppermute | solution.py:30
  61.4 21.0 %collective-permute-start.3 = (f32[8,24,20,2]{1,0,3,2:T(8,128)S(1)}, f32[8,24,20,2]{1,0,3,2:T(8,128)S(1)}, u32[]{:S(2)}, u32[]{:S(2)}) collective-permute-start(f32[8,24,20,2]{1,0,3,2:T(8,128)S(1)} %get-tuple-element.415), channel_id=1, source_target_pairs={{1,0},{2,1},{3,2},{4,3},{5,4},{6,5},{7,6},{8,7},{9,8},{10,9},{11,1... | collective-permute-start | bytes 92168 | tf_op jit(solution)/shard_map/ppermute | solution.py:32
  108.4 1.9 copy-start.13
  175.8 10.6 %copy-start.5 = (f32[16]{0:T(128)S(1)}, f32[16]{0:T(128)}, u32[]{:S(2)}) copy-start(f32[16]{0:T(128)} %get-tuple-element.681) | copy-start | bytes 196
  175.8 10.6 %copy-start.6 = (f32[16]{0:T(128)S(1)}, f32[16]{0:T(128)}, u32[]{:S(2)}) copy-start(f32[16]{0:T(128)} %get-tuple-element.682) | copy-start | bytes 196
  189.5 1.1 copy-start.11
  194.9 1.0 copy-start.14
  195.0 1.0 copy-start.10
  195.0 1.1 copy-start.18
  200.4 1.1 copy-start.11
  205.9 1.0 copy-start.14
  205.9 1.0 copy-start.10
  205.9 1.1 copy-start.18
  211.4 1.1 copy-start.11
  216.8 1.0 copy-start.7
  216.8 1.0 copy-start.14
  216.9 1.0 copy-start.10
  216.9 1.1 copy-start.18
  219.5 1.0 copy-start.3
  219.5 1.1 copy-start.4
  (3 other events, 2.8 us)
where the time goes:
time: 223 us; the launch traced here: 221 us
  local copies, waits for them, and re-layouts  131 us (59%)
  other arithmetic  43.6 us (20%)
  starting transfers between devices  27.5 us (12%)
  waiting for transfers between devices  16.3 us (7%)
    scatter x1, local copies, waits for them, and re-layouts, assemble(): halo_block.at[:, :, cycle_rows, cycle_cols]  61.2 us
    ppermute x2, waiting for transfers between devices, with_halo(): lax.ppermute(tail, axis, [(i, (i + 1) % count) for i in range(ends)])  16.2 us
    gather x2, local copies, waits for them, and re-layouts, assemble(): current = halo_block[:, :, cycle_rows, cycle_cols]  13.1 us
    ppermute x2, starting transfers between devices, with_halo(): lax.ppermute(head, axis, [((i + 1) % count, i) for i in range(ends)])  10.8 us
    while x1, local copies, waits for them, and re-layouts, slab_rates(): return lax.fori_loop(0, slab_count, one_slab, start_vals)  10.4 us
    all_to_all x1, starting transfers between devices, deliver(): lax.all_to_all(crossed, 'lon', split_axis=1, concat_axis=1, tiled=True)  9.94 us
    concatenate x1, other arithmetic, with_halo(): jnp.concatenate([lax.ppermute(tail, axis, [(i, (i + 1) % count) for i in...  8.72 us
    gather x3, local copies, waits for them, and re-layouts, one_slab(): slab_piece = jnp.take(extended, shell_ids, axis=1)  8.36 us
  transfers between devices with their start and end apart: 6, of which 1 were waited for; matrix products, arithmetic and copies ran while one was open for 17% of the time, Pallas kernels for 0%

commit v1 on v0

v1 whole, which is shorter than its diff:
```python
import math

import jax
import jax.numpy as jnp
import numpy as np
from jax import lax
from jax.experimental import pallas as pl
from jax.experimental.pallas import tpu as pltpu
from jax.sharding import PartitionSpec as P

GAMMA = 5.0 / 3.0
F32 = jnp.float32
BF16 = jnp.bfloat16
SH = 24
NR = 16
NC = 128
N_LAT = 8
N_LON = 16
CAP = 19
CHUNK = 32
EXT = NR + 4
ROW_SCALARS = 4

D_TH = 0.5 * math.pi / (NR * N_LAT)
D_PH = 1.5 * math.pi / (NC * N_LON)
D_R = 0.6 * D_TH
DT = 0.3 * min(D_R, 0.6 * math.sin(0.25 * math.pi - 2.0 * D_TH) * D_PH)
MU = DT / 0.9
GRAV = 0.036 / DT
OMEGA = 0.05 / DT


def theta_of(k):
    return 0.25 * math.pi + (k + 0.5) * D_TH


def phi_of(m):
    return -0.75 * math.pi + (m + 0.5) * D_PH


def radius_table():
    s = np.arange(SH, dtype=np.float64)
    r = 0.6 + (s + 0.5) * D_R
    ratio = np.ones(SH)
    ratio[0] = r[0] / (0.6 - 0.5 * D_R)
    ratio[-1] = r[-1] / (0.6 + (SH + 0.5) * D_R)
    cols = [1.0 / r, ratio, DT * GRAV / (r * r)]
    return np.concatenate([np.repeat(c[:, None], NC, 1) for c in cols], 0).astype(np.float32)


def row_table():
    out = np.zeros((N_LAT, EXT, ROW_SCALARS))
    for i in range(N_LAT):
        th = theta_of(i * NR - 2 + np.arange(EXT))
        out[i] = np.stack([np.sin(th), np.cos(th), np.cos(th) / np.sin(th), 1.0 / np.sin(th)], 1)
    return out.reshape(N_LAT, 1, EXT * ROW_SCALARS).astype(np.float32)


def lane_rows(shift):
    lane = (np.arange(NC) + shift) % NC
    return lane // 6, lane % 6


def theta_pack_table():
    out = np.zeros((N_LAT, 8, NC))
    for i in range(N_LAT):
        for side in range(2):
            r, _ = lane_rows(2 * side)
            th = theta_of(i * NR - 2 + np.minimum(r, EXT - 1))
            out[i, 4 * side : 4 * side + 4] = [
                np.sin(th),
                np.cos(th),
                np.cos(th) / np.sin(th),
                1.0 / np.sin(th),
            ]
    return out.astype(np.float32)


def phi_table():
    out = np.zeros((N_LON, 8, NC))
    for q in range(N_LON):
        ph = phi_of(q * NC + np.arange(NC))
        out[q, 0], out[q, 1] = np.sin(ph), np.cos(ph)
        for side in range(2):
            _, c = lane_rows(2 * side)
            ph = phi_of(q * NC + (c - 2 if side == 0 else c + NC - 4))
            out[q, 2 + 2 * side], out[q, 3 + 2 * side] = np.sin(ph), np.cos(ph)
    return out.astype(np.float32)


class Geo:
    def __init__(self, rad_ref, sin, cos, cot, isin, sphi, cphi, yang):
        self.rinv = rad_ref[0:SH, :]
        self.ratio = rad_ref[SH : 2 * SH, :]
        self.grav = rad_ref[2 * SH : 3 * SH, :]
        self.ct = self.rinv * (0.5 / D_TH)
        self.cp = self.rinv * (0.5 / D_PH) * isin
        self.cotr = self.rinv * cot
        self.n_r = (1.0 - yang) * cos + yang * (sin * sphi)
        self.n_t = (yang - 1.0) * sin + yang * (cos * sphi)
        self.n_p = yang * cphi


def lane_roll(x, shift):
    return pltpu.roll(x, shift % NC, 1)


def diff_p(x):
    return lane_roll(x, -1) - lane_roll(x, 1)


def diff_r(x, ghost, edges):
    first, last = edges
    return jnp.where(last, ghost, pltpu.roll(x, SH - 1, 0)) - jnp.where(
        first, ghost, pltpu.roll(x, 1, 0)
    )


def cross(a, b):
    return (
        a[1] * b[2] - a[2] * b[1],
        a[2] * b[0] - a[0] * b[2],
        a[0] * b[1] - a[1] * b[0],
    )


def stage_one(u, diff_t, geo, edges, full):
    rinv, ct, cp, cotr = geo.rinv, geo.ct, geo.cp, geo.cotr
    cr = 0.5 / D_R
    rho, pr = u[0], u[1]
    v, b = u[2:5], u[5:8]

    def d_r(x):
        return diff_r(x, x, edges) * cr

    def d_t(fn):
        return diff_t(fn) * ct

    def d_p(x):
        return diff_p(x) * cp

    bt_r, bp_r = d_r(b[1]), d_r(b[2])
    j_r = d_t(lambda w: w[7]) + b[2] * cotr - d_p(b[1])
    jt_ang = d_p(b[0]) - b[2] * rinv
    jp_ang = b[1] * rinv - d_t(lambda w: w[5])
    jj = (j_r, jt_ang - bp_r, bt_r + jp_ang)
    vr = [d_r(x) for x in v]
    vt = [d_t(lambda w, i=i: w[2 + i]) for i in range(3)]
    vp = [d_p(x) for x in v]
    wt_ang = vp[0] - v[2] * rinv
    wp_ang = v[1] * rinv - vt[0]
    ww = (vt[2] + v[2] * cotr - vp[1], wt_ang - vr[2], vr[1] + wp_ang)
    e_ang = 2.0 * v[0] * rinv + vt[1] + v[1] * cotr + vp[2]
    ee = vr[0] + e_ang
    vxb = cross(v, b)
    el = [vxb[i] - MU * jj[i] for i in range(3)]
    ratio = geo.ratio
    level = list(ww) + [ee] + el
    level += [
        wt_ang * ratio,
        wp_ang * ratio,
        e_ang * ratio,
        vxb[1] - MU * (jt_ang * ratio),
        vxb[2] - MU * (jp_ang * ratio),
    ]
    if not full:
        return level, None, None
    fr, fp = rho * v[0], rho * v[2]
    mass = (
        d_r(fr)
        + 2.0 * fr * rinv
        + d_t(lambda w: w[0] * w[3])
        + rho * v[1] * cotr
        + d_p(fp)
    )
    gp = (d_r(pr), d_t(lambda w: w[1]), d_p(pr))
    press = -(v[0] * gp[0] + v[1] * gp[1] + v[2] * gp[2]) - GAMMA * pr * ee
    lor = cross(jj, b)
    spin = cross(v, (geo.n_r, geo.n_t, geo.n_p))
    curv = (
        -(v[1] * v[1] + v[2] * v[2]) * rinv,
        v[0] * v[1] * rinv - v[2] * v[2] * cotr,
        v[0] * v[2] * rinv + v[1] * v[2] * cotr,
    )
    irho = DT / rho
    rest = []
    for i in range(3):
        adv = v[0] * vr[i] + v[1] * vt[i] + v[2] * vp[i] + curv[i]
        x = (lor[i] - gp[i]) * irho - DT * adv + (2.0 * OMEGA * DT) * spin[i]
        rest.append(x - geo.grav if i == 0 else x)
    rest.append(irho * MU)
    return level, rest, (-DT * mass, DT * press)


def stage_two(q, diff_t, rest, geo, edges):
    rinv, ct, cp, cotr = geo.rinv, geo.ct, geo.cp, geo.cotr
    cr = 0.5 / D_R

    def d_r(i, g):
        return diff_r(q[i], q[g], edges) * cr

    def d_t(i):
        return diff_t(i) * ct

    def d_p(i):
        return diff_p(q[i]) * cp

    def curl(o, gt, gp):
        return (
            d_t(o + 2) + q[o + 2] * cotr - d_p(o + 1),
            d_p(o) - d_r(o + 2, gp) - q[o + 2] * rinv,
            d_r(o + 1, gt) + q[o + 1] * rinv - d_t(o),
        )

    cw = curl(0, 7, 8)
    grad_e = (d_r(3, 9), d_t(3), d_p(3))
    ce = curl(4, 10, 11)
    acc = [rest[i] + rest[3] * (4.0 / 3.0 * grad_e[i] - cw[i]) for i in range(3)]
    return acc + [DT * ce[i] for i in range(3)]


def shell_edges():
    s = lax.broadcasted_iota(jnp.int32, (SH, NC), 0)
    return s == 0, s == SH - 1


def load_row(sc_ref, ve_ref, f, k):
    ref, g = (sc_ref, f) if f < 2 else (ve_ref, f - 2)
    return ref[pl.ds(g * (SH * NR) + k, SH, stride=NR), :]


def store_row(sc_ref, ve_ref, f, k, val):
    ref, g = (sc_ref, f) if f < 2 else (ve_ref, f - 2)
    ref[pl.ds(g * (SH * NR) + k, SH, stride=NR), :] = val


def aligned(i):
    return i if isinstance(i, int) else pl.multiple_of(i, 8)


def tile(ref, i):
    return ref[pl.ds(aligned(i * SH), SH), :]


def put(ref, i, val):
    ref[pl.ds(aligned(i * SH), SH), :] = val


def row_geo(rad_ref, rows_ref, phi_ref, e, yang):
    sc = [rows_ref[0, e * ROW_SCALARS + j] for j in range(ROW_SCALARS)]
    return Geo(rad_ref, sc[0], sc[1], sc[2], sc[3], phi_ref[0:1, :], phi_ref[1:2, :], yang)


def rows_one(u_ref, q_ref, r_ref, depth, geo, edges, slot, full):
    def fields(at):
        return [tile(u_ref, f * depth + at) for f in range(8)]

    up, dn = fields(slot + 1), fields(slot - 1)
    level, rest, scal = stage_one(
        fields(slot), lambda fn: fn(up) - fn(dn), geo, edges, full
    )
    for i, x in enumerate(level):
        put(q_ref, i * depth + slot, x)
    if full:
        for i, x in enumerate(rest):
            put(r_ref, i * depth + slot, x)
    return scal


def rows_two(q_ref, r_ref, depth, geo, edges, slot):
    q = [tile(q_ref, i * depth + slot) for i in range(12)]

    def diff_t(i):
        return tile(q_ref, i * depth + slot + 1) - tile(q_ref, i * depth + slot - 1)

    rest = [tile(r_ref, i * depth + slot) for i in range(4)]
    return stage_two(q, diff_t, rest, geo, edges)


def donor_kernel(sc_ref, ve_ref, tab_ref, rows_ref, phi_ref, pay_ref, up_ref, dn_ref,
                 s_hi, s_lo, c_hi, c_lo):
    sphi, cphi = phi_ref[0:1, :], phi_ref[1:2, :]
    for k in range(NR):
        u = [load_row(sc_ref, ve_ref, f, k) for f in range(8)]
        for rows, ref in (((0, 1), dn_ref), ((NR - 2, NR - 1), up_ref)):
            if k in rows:
                for f in range(8):
                    put(ref, f * 2 + k - rows[0], u[f])
        sin = rows_ref[0, (k + 2) * ROW_SCALARS]
        cos = rows_ref[0, (k + 2) * ROW_SCALARS + 1]
        c = [u[0], u[1]]
        for o in (2, 5):
            flat = u[o] * sin + u[o + 1] * cos
            c += [
                flat * cphi - u[o + 2] * sphi,
                flat * sphi + u[o + 2] * cphi,
                u[o] * cos - u[o + 1] * sin,
            ]
        c = jnp.concatenate(c, axis=0)
        hi = c.astype(BF16)
        c_hi[:, k * NC : (k + 1) * NC] = hi
        c_lo[:, k * NC : (k + 1) * NC] = (c - hi.astype(F32)).astype(BF16)
    cols = jnp.transpose(tab_ref[...])
    lane = lax.broadcasted_iota(jnp.int32, (48, NC), 1).astype(F32)
    for pair in range(N_LON // 2):
        a, b, wt, wp = [
            jnp.concatenate(
                [
                    jnp.broadcast_to(cols[0:24, o : o + 1], (24, NC))
                    for o in (j * N_LON + 2 * pair, j * N_LON + 2 * pair + 1)
                ],
                axis=0,
            )
            for j in range(4)
        ]
        along = jnp.where(lane == b, 1.0 - wp, jnp.where(lane == b + 1.0, wp, 0.0))
        first, second = along * (1.0 - wt), along * wt
        for k in range(NR):
            s = jnp.where(a == float(k), first, jnp.where(a == float(k - 1), second, 0.0))
            hi = s.astype(BF16)
            s_hi[48 * pair : 48 * pair + 48, k * NC : (k + 1) * NC] = hi
            s_lo[48 * pair : 48 * pair + 48, k * NC : (k + 1) * NC] = (
                s - hi.astype(F32)
            ).astype(BF16)

    def dot(x, y):
        return lax.dot_general(
            x[...], y[...], (((1,), (1,)), ((), ())), preferred_element_type=F32
        )

    sent = dot(s_hi, c_hi) + dot(s_hi, c_lo) + dot(s_lo, c_hi)
    for t in range(N_LON):
        pay_ref[t, 0:24, :] = sent[24 * t : 24 * t + 24, 0:NC]
        part = sent[24 * t : 24 * t + 24, NC : NC + 64]
        pay_ref[t, 24:32, :] = jnp.zeros((8, NC), F32)
        pay_ref[t, 19:29, 0:64] = part[0:10]
        pay_ref[t, 19:28, 64:128] = part[10:19]


def pack_kernel(sc_ref, ve_ref, top_ref, bot_ref, left_ref, right_ref):
    lane = lax.broadcasted_iota(jnp.int32, (SH, NC), 1)
    for f in range(8):
        left = jnp.zeros((SH, NC), F32)
        right = jnp.zeros((SH, NC), F32)
        for e in range(EXT):
            if e < 2:
                x = tile(top_ref, f * 2 + e)
            elif e >= NR + 2:
                x = tile(bot_ref, f * 2 + e - NR - 2)
            else:
                x = load_row(sc_ref, ve_ref, f, e - 2)
            x = lane_roll(x, 6 * e + 2)
            base = 6 * e
            left = jnp.where((lane >= base + 2) & (lane < base + 6), x, left)
            if e == 0:
                right = jnp.where((lane >= NC - 2) | (lane < 2), x, right)
            else:
                right = jnp.where((lane >= base - 2) & (lane < base + 2), x, right)
        put(left_ref, f, left)
        put(right_ref, f, right)


def main_kernel(sc_ref, ve_ref, top_ref, bot_ref, rad_ref, rows_ref, phi_ref, osc_ref, ove_ref,
                u_ref, q_ref, r_ref):
    yang = lax.axis_index("panel").astype(F32)
    edges = shell_edges()
    for f in range(8):
        for e in range(EXT):
            if e < 2:
                x = tile(top_ref, f * 2 + e)
            elif e >= NR + 2:
                x = tile(bot_ref, f * 2 + e - NR - 2)
            else:
                x = load_row(sc_ref, ve_ref, f, e - 2)
            put(u_ref, f * EXT + e, x)

    def one(e, full):
        geo = row_geo(rad_ref, rows_ref, phi_ref, e, yang)
        return rows_one(u_ref, q_ref, r_ref, EXT, geo, edges, e, full)

    one(1, False)
    one(NR + 2, False)

    @pl.loop(2, NR + 2)
    def _(e):
        scal = one(e, True)
        for i in range(2):
            store_row(osc_ref, ove_ref, i, e - 2, scal[i])

    @pl.loop(2, NR + 2)
    def _(e):
        geo = row_geo(rad_ref, rows_ref, phi_ref, e, yang)
        vec = rows_two(q_ref, r_ref, EXT, geo, edges, e)
        for i in range(6):
            store_row(osc_ref, ove_ref, 2 + i, e - 2, vec[i])


def to_spherical(x, y, z, sin, cos, sphi, cphi):
    flat = x * cphi + y * sphi
    return [flat * sin + z * cos, flat * cos - z * sin, y * cphi - x * sphi]


def border_fields(w, sin, cos, sphi, cphi):
    out = [w[0], w[1]]
    for o in (2, 5):
        out += to_spherical(-w[o], w[o + 2], w[o + 1], sin, cos, sphi, cphi)
    return out


STRIP = 6


def edge_kernel(sc_ref, ve_ref, top_ref, bot_ref, left_ref, right_ref, fromleft_ref, fromright_ref,
                don_ref, idx_ref, rad_ref, rows_ref, thp_ref, phi_ref, isc_ref, ive_ref,
                osc_ref, ove_ref, bord_ref, u_ref, q_ref, r_ref):
    yang = lax.axis_index("panel").astype(F32)
    lat = lax.axis_index("lat")
    lon = lax.axis_index("lon")
    edges = shell_edges()
    row_edge = (lat == 0) | (lat == N_LAT - 1)
    col_edge = (lon == 0) | (lon == N_LON - 1)
    wide = 4 * NC

    @pl.when(row_edge | col_edge)
    def _():
        recv = jnp.transpose(don_ref[...])
        hi = recv.astype(BF16)
        lo = (recv - hi.astype(F32)).astype(BF16)
        g = idx_ref[0:1, :]
        donor, slot = idx_ref[1:2, :], idx_ref[2:3, :]
        at = lax.broadcasted_iota(jnp.int32, (N_LON * CHUNK, wide), 0)
        here = jnp.where(g >= 0, donor * CHUNK + slot, -1)
        low = jnp.where((g >= 0) & (slot < 10), donor * CHUNK + 19 + slot, -1)
        high = jnp.where((g >= 0) & (slot >= 10), donor * CHUNK + 9 + slot, -1)

        def pick(where, lo_row, hi_row):
            hot = jnp.where(at == where, 1.0, 0.0).astype(BF16)
            return jnp.dot(hi[lo_row:hi_row], hot, preferred_element_type=F32) + jnp.dot(
                lo[lo_row:hi_row], hot, preferred_element_type=F32
            )

        bord_ref[0:NC, :] = pick(here, 0, NC)
        bord_ref[NC : NC + 64, :] = pick(low, 0, 64) + pick(high, 64, NC)

    def border(col, sin, cos, sphi, cphi):
        w = [bord_ref[f * SH : f * SH + SH, col * NC : (col + 1) * NC] for f in range(8)]
        return border_fields(w, sin, cos, sphi, cphi)

    def scalars_at(e):
        return [rows_ref[0, e * ROW_SCALARS + j] for j in range(ROW_SCALARS)]

    lane = lax.broadcasted_iota(jnp.int32, (SH, NC), 1)
    place = lane % 6
    merged = None
    for side in range(2):
        own_ref, other_ref = (
            (left_ref, fromleft_ref) if side == 0 else (right_ref, fromright_ref)
        )
        theirs = (place < 2) if side == 0 else ((place == 2) | (place == 3))
        th = [thp_ref[4 * side + j : 4 * side + j + 1, :] for j in range(4)]
        ph = [phi_ref[2 + 2 * side + j : 3 + 2 * side + j, :] for j in range(2)]
        g = jnp.broadcast_to(idx_ref[0:1, (2 + side) * NC : (3 + side) * NC], (SH, NC))
        donated = border(2 + side, th[0], th[1], ph[0], ph[1])
        u = []
        for f in range(8):
            x = jnp.where(theirs, tile(other_ref, f), tile(own_ref, f))
            u.append(jnp.where(g >= 0, donated[f], x))
        geo = Geo(rad_ref, th[0], th[1], th[2], th[3], ph[0], ph[1], yang)

        def diff_six(x):
            return lane_roll(x, -6) - lane_roll(x, 6)

        level, rest, scal = stage_one(u, lambda fn: diff_six(fn(u)), geo, edges, True)
        vec = stage_two(level, lambda i: diff_six(level[i]), rest, geo, edges)
        vals = list(scal) + vec
        if side == 0:
            merged = vals
        else:
            merged = [jnp.where(place < 2, y, x) for x, y in zip(merged, vals)]
    edge_lane = (lane < 2) | (lane >= NC - 2)
    for f in range(8):
        for k in range(NR):
            x = lane_roll(merged[f], -(6 * (k + 2) + 2))
            old = load_row(isc_ref, ive_ref, f, k)
            store_row(osc_ref, ove_ref, f, k, jnp.where(edge_lane, x, old))

    def merge_row(f, k, val):
        old = load_row(osc_ref, ove_ref, f, k)
        store_row(osc_ref, ove_ref, f, k, jnp.where(edge_lane, old, val))

    @pl.when(row_edge)
    def _():
        top = lat == 0
        e0 = jnp.where(top, 0, NR - 2)
        for i in range(2):
            sc = scalars_at(jnp.where(top, i, NR + 2 + i))
            w = border(i, sc[0], sc[1], phi_ref[0:1, :], phi_ref[1:2, :])
            for f in range(8):
                put(u_ref, f * STRIP + jnp.where(top, i, 4 + i), w[f])
        for j in range(4):
            for f in range(8):
                x = load_row(sc_ref, ve_ref, f, jnp.where(top, j, NR - 4 + j))
                put(u_ref, f * STRIP + jnp.where(top, 2 + j, j), x)

        def geo_at(slot):
            return row_geo(rad_ref, rows_ref, phi_ref, e0 + slot, yang)

        for slot in (1, 2, 3, 4):
            full = slot in (2, 3)
            scal = rows_one(u_ref, q_ref, r_ref, STRIP, geo_at(slot), edges, slot, full)
            if full:
                for i in range(2):
                    merge_row(i, e0 + slot - 2, scal[i])
        for slot in (2, 3):
            vec = rows_two(q_ref, r_ref, STRIP, geo_at(slot), edges, slot)
            for i in range(6):
                merge_row(2 + i, e0 + slot - 2, vec[i])


VM = pl.BlockSpec(memory_space=pltpu.VMEM)
SM = pl.BlockSpec(memory_space=pltpu.SMEM)


def call(kernel, n_in, smem, outs, scratch, name, flops, aliases=None):
    return pl.pallas_call(
        kernel,
        out_shape=[jax.ShapeDtypeStruct(s, F32) for s in outs],
        in_specs=[SM if i in smem else VM for i in range(n_in)],
        out_specs=[VM] * len(outs),
        scratch_shapes=scratch,
        input_output_aliases=aliases or {},
        name=name,
        compiler_params=pltpu.CompilerParams(vmem_limit_bytes=48 * 1024 * 1024),
        cost_estimate=pl.CostEstimate(flops=flops, bytes_accessed=3000000, transcendentals=0),
    )


def shifted(x, axis, step):
    n = lax.axis_size(axis)
    return lax.ppermute(x, axis, [(i, (i + step) % n) for i in range(n)])


def frame_places(recv, lat):
    top = jnp.stack([recv[2 : NC + 2], recv[NC + 6 : 2 * NC + 6]])
    at = 2 * (NC + 4)
    bottom = jnp.stack([recv[at + 2 : at + NC + 2], recv[at + NC + 6 : at + 2 * NC + 6]])
    strip = jnp.where(lat == 0, top, bottom)
    mid = 4 * (NC + 4)
    rows = [recv[i * (NC + 4) : (i + 1) * (NC + 4)] for i in range(4)]

    def side(cut, sides, pad):
        body = jnp.pad(sides.reshape(NR, 2), ((0, 0), pad), constant_values=-1)
        edge = jnp.stack([r[cut] for r in rows])
        return jnp.concatenate([edge[:2], body, edge[2:]]).reshape(-1)

    left = side(slice(0, 6), recv[mid : mid + 2 * NR], (0, 4))
    right = side(slice(NC - 2, NC + 4), recv[mid + 2 * NR : mid + 4 * NR], (4, 0))
    none = jnp.full((NC - 6 * EXT,), -1, jnp.int32)
    left = jnp.concatenate([left, none])
    right = jnp.concatenate([right[2:], none, right[:2]])
    g = jnp.concatenate([strip.reshape(-1), left, right])
    return jnp.pad(jnp.stack([g, g // CAP, g % CAP]), ((0, 5), (0, 0)))


def body(scalars, vectors, corner_rows, corner_cols, send_weights, recv_source):
    lat, lon = lax.axis_index("lat"), lax.axis_index("lon")
    sc = scalars.reshape(2 * SH * NR, NC)
    ve = vectors.reshape(6 * SH * NR, NC)
    rad = jnp.asarray(radius_table())
    rows = lax.dynamic_index_in_dim(jnp.asarray(row_table()), lat, 0, False)
    thp = lax.dynamic_index_in_dim(jnp.asarray(theta_pack_table()), lat, 0, False)
    phi = lax.dynamic_index_in_dim(jnp.asarray(phi_table()), lon, 0, False)
    tab = jnp.concatenate(
        [
            corner_rows[0, 0].astype(F32),
            corner_cols[0, 0].astype(F32),
            send_weights[0, 0, 0],
            send_weights[1, 0, 0],
        ]
    )
    tab = jnp.pad(tab, ((0, NC - 4 * N_LON), (0, NC - CAP)))
    halo = (8 * 2 * SH, NC)
    pack = (8 * SH, NC)

    pay, up, dn = call(
        donor_kernel, 5, (3,), [(N_LON, CHUNK, NC), halo, halo],
        [
            pltpu.VMEM((24 * N_LON, NR * NC), BF16),
            pltpu.VMEM((24 * N_LON, NR * NC), BF16),
            pltpu.VMEM((8 * SH, NR * NC), BF16),
            pltpu.VMEM((8 * SH, NR * NC), BF16),
        ],
        "donor", 400000000,
    )(sc, ve, tab, rows, phi)
    pay = lax.ppermute(pay, "panel", [(0, 1), (1, 0)])
    don = lax.all_to_all(pay, "lon", 0, 0, tiled=True).reshape(N_LON * CHUNK, NC)
    top = shifted(up, "lat", 1)
    bot = shifted(dn, "lat", -1)
    left, right = call(pack_kernel, 4, (), [pack, pack], [], "packs", 1000000)(sc, ve, top, bot)
    from_left = shifted(right, "lon", 1)
    from_right = shifted(left, "lon", -1)
    osc, ove = call(
        main_kernel, 7, (5,), [sc.shape, ve.shape],
        [
            pltpu.VMEM((8 * EXT * SH, NC), F32),
            pltpu.VMEM((12 * EXT * SH, NC), F32),
            pltpu.VMEM((4 * EXT * SH, NC), F32),
        ],
        "interior", 30000000,
    )(sc, ve, top, bot, rad, rows, phi)
    osc, ove = call(
        edge_kernel, 16, (11,), [sc.shape, ve.shape],
        [
            pltpu.VMEM((8 * SH, 4 * NC), F32),
            pltpu.VMEM((8 * STRIP * SH, NC), F32),
            pltpu.VMEM((12 * STRIP * SH, NC), F32),
            pltpu.VMEM((4 * STRIP * SH, NC), F32),
        ],
        "edges", 10000000,
    )(sc, ve, top, bot, left, right, from_left, from_right, don,
      frame_places(recv_source[0, 0], lat), rad, rows, thp, phi, osc, ove)
    return osc.reshape(scalars.shape), ove.reshape(vectors.shape)


def solution(mesh):
    return jax.shard_map(
        body,
        mesh=mesh,
        in_specs=(
            P("panel", None, None, "lat", "lon"),
            P("panel", None, None, "lat", "lon"),
            P("lat", "lon", None, None),
            P("lat", "lon", None, None),
            P(None, "lat", "lon", None, None),
            P("lat", "lon", None),
        ),
        out_specs=(P("panel", None, None, "lat", "lon"), P("panel", None, None, "lat", "lon")),
        check_vma=False,
    )
```

time: 223 us -> 50.5 us (0.23)
  the two profiles are of different devices: /device:TPU:24 before, /device:TPU:1 now
where the time goes in v1:
time: 50.5 us; the launch traced here: 49.8 us
  starting transfers between devices  20.2 us (40%)
  local copies, waits for them, and re-layouts  15.2 us (30%)
  Pallas kernels  13.4 us (27%)
  between operations  0.78 us (2%)
    unnamed x34, local copies, waits for them, and re-layouts  10.4 us
    ppermute x4, starting transfers between devices, shifted(): return lax.ppermute(x, axis, [(i, (i + step) % n) for i in range(n)])  9.65 us
    all_to_all x1, starting transfers between devices, body(): lax.all_to_all(pay, 'lon', 0, 0, tiled=True).reshape(N_LON * CHUNK, NC)  7.71 us
    pallas_call x1, Pallas kernels, body(): call(main_kernel, 7, (5,), [sc.shape, ve.shape], [pltpu.VMEM((8 * EXT * S...  5.04 us
    pallas_call x1, Pallas kernels, body(): call(edge_kernel, 16, (11,), [sc.shape, ve.shape], [pltpu.VMEM((8 * SH, 4...  4.5 us
    pallas_call x1, Pallas kernels, body(): call(donor_kernel, 5, (3,), [(N_LON, CHUNK, NC), halo, halo], [pltpu.VMEM...  3.25 us
    ppermute x1, starting transfers between devices, body(): pay = lax.ppermute(pay, 'panel', [(0, 1), (1, 0)])  2.85 us
  transfers between devices with their start and end apart: 6, of which 0 were waited for; matrix products, arithmetic and copies ran while one was open for 5% of the time, Pallas kernels for 11%

profile of v1, /device:TPU:1, one launch (start us, length us, event | category | flops | bytes accessed | tf_op | source)
XLA Modules:
  0.0 49.8 jit_solution(13573430637907759897)
XLA Ops:
  0.6 0.8 %copy.30 = s32[1,1,16,19]{2,3,1,0:T(8,128)S(1)} copy(s32[1,1,16,19]{3,2,1,0:T(8,128)} %param.12) | data formatting | bytes 2432 | tf_op args[2]
  1.4 0.8 %copy.31 = s32[1,1,16,19]{2,3,1,0:T(8,128)S(1)} copy(s32[1,1,16,19]{3,2,1,0:T(8,128)} %param.13) | data formatting | bytes 2432 | tf_op args[3]
  2.2 0.7 %fusion.1 = (f32[1,1,1,16,19]{4,3,2,1,0:T(8,128)S(1)}, f32[1,1,1,16,19]{4,3,2,1,0:T(8,128)S(1)}) fusion(f32[2,1,1,16,19]{4,3,2,1,0:T(8,128)} %param.14), kind=kLoop, calls=%fused_computation.27 | loop fusion | bytes 4864 | tf_op jit(solution)/shard_map/slice | solution.py:577
  3.2 0.1 copy.34
  3.3 0.7 %fusion.rows_ref = f32[1,80]{1,0:T(1,128)S(1)} fusion(f32[8,1,80]{2,1,0:T(1,128)} %constant.57.clone, s32[]{:T(128)S(6)} %select_n.60), kind=kLoop, calls=%fused_computation.10 | loop fusion | bytes 644 | tf_op jit(solution)/shard_map/jit(dynamic_index_in_dim)/squeeze | solution.py:570
  3.9 0.7 %dynamic-slice_bitcast_fusion.1.phi_ref = f32[8,128]{1,0:T(8,128)S(1)} fusion(f32[16,8,128]{2,1,0:T(8,128)} %constant.59.clone, s32[]{:T(128)S(6)} %select_n.61), kind=kLoop, calls=%fused_computation.7 | loop fusion | bytes 8196 | tf_op jit(solution)/shard_map/jit(dynamic_index_in_dim)/squeeze | solution.py:572
  4.6 1.3 %copy-done = f32[1,6,24,16,128]{4,3,2,1,0:T(8,128)S(1)} copy-done((f32[1,6,24,16,128]{4,3,2,1,0:T(8,128)S(1)}, f32[1,6,24,16,128]{4,3,2,1,0:T(8,128)}, u32[]{:S(2)}) %copy-start) | copy-done | bytes 1179672
  5.9 1.0 %copy-done.2 = f32[1,2,24,16,128]{4,3,2,1,0:T(8,128)S(1)} copy-done((f32[1,2,24,16,128]{4,3,2,1,0:T(8,128)S(1)}, f32[1,2,24,16,128]{4,3,2,1,0:T(8,128)}, u32[]{:S(2)}) %copy-start.2) | copy-done | bytes 393240
  6.9 3.3 %donor.1 = (f32[16,32,128]{2,1,0:T(8,128)S(1)}, f32[384,128]{1,0:T(8,128)S(1)}, f32[384,128]{1,0:T(8,128)S(1)}) custom-call(f32[768,128]{1,0:T(8,128)S(1)} %bitcast.53, f32[2304,128]{1,0:T(8,128)S(1)} %bitcast.49, f32[128,128]{1,0:T(8,128)S(1)} %pad.16.tab_ref, f32[1,80]{1,0:T(1,128)S(1)} %fusion.rows_ref, f32[8,128]{1,0:T(8,128)S(1)} %dynamic-slice_bitcast_fusion.1.phi_ref), custom_call_target="tpu_custom_call" | custom-call | flops 400000000 | bytes 3000000 | tf_op jit(solution)/shard_map/donor/pallas_call | solution.py:585
  10.2 2.1 %collective-permute-start = (f32[384,128]{1,0:T(8,128)S(1)}, f32[384,128]{1,0:T(8,128)S(1)}, u32[]{:S(2)}, u32[]{:S(2)}) collective-permute-start(f32[384,128]{1,0:T(8,128)S(1)} %get-tuple-element.11), channel_id=1, source_target_pairs={{0,16},{16,32},{32,48},{48,64},{64,80},{80,96},{96,112},{112,0},{1... | collective-permute-start | bytes 589832 | tf_op jit(solution)/shard_map/ppermute | solution.py:540
  12.3 4.0 %collective-permute-start.1 = (f32[384,128]{1,0:T(8,128)S(1)}, f32[384,128]{1,0:T(8,128)S(1)}, u32[]{:S(2)}, u32[]{:S(2)}) collective-permute-start(f32[384,128]{1,0:T(8,128)S(1)} %get-tuple-element.12), channel_id=1, source_target_pairs={{0,112},{16,0},{32,16},{48,32},{64,48},{80,64},{96,80},{112,96},{1... | collective-permute-start | bytes 589832 | tf_op jit(solution)/shard_map/ppermute | solution.py:540
  16.3 2.9 %collective-permute-start.4 = (f32[16,32,128]{2,1,0:T(8,128)S(1)}, f32[16,32,128]{2,1,0:T(8,128)}, u32[]{:S(2)}, u32[]{:S(2)}) collective-permute-start(f32[16,32,128]{2,1,0:T(8,128)S(1)} %get-tuple-element.15), channel_id=1, source_target_pairs={{0,128},{128,0},{1,129},{129,1},{2,130},{130,2},{3,131},{131,3},{4... | collective-permute-start | bytes 786440 | tf_op jit(solution)/shard_map/ppermute | solution.py:595
  19.5 0.2 concatenate.55
  19.7 0.1 reshape.334
  19.9 0.2 concatenate.54
  20.1 0.1 reshape.332
  20.3 0.1 concatenate.62
  20.4 7.7 %all-to-all-start = ((f32[16,32,128]{2,1,0:T(8,128)}), f32[16,32,128]{2,1,0:T(8,128)S(1)}, u32[]{:S(2)}, u32[]{:S(2)}) async-start(f32[16,32,128]{2,1,0:T(8,128)} %collective-permute-done.4), calls=%async_computation | async-start | bytes 524288 | tf_op jit(solution)/shard_map/all_to_all | solution.py:596
  28.3 0.6 %pad.19.idx_ref = s32[8,512]{1,0:T(8,128)} pad(s32[3,512]{1,0:T(4,128)S(1)} %pad_add_fusion, s32[]{:T(128)} %constant.49.clone.1), padding=0_5x0_0 | pad | bytes 22532 | tf_op jit(solution)/shard_map/jit(_pad)/pad | solution.py:562
  28.9 0.6 %packs.1 = (f32[192,128]{1,0:T(8,128)S(1)}, f32[192,128]{1,0:T(8,128)S(1)}) custom-call(f32[768,128]{1,0:T(8,128)S(1)} %bitcast.54, f32[2304,128]{1,0:T(8,128)S(1)} %bitcast.50, f32[384,128]{1,0:T(8,128)S(1)} %collective-permute-done.top_ref, f32[384,128]{1,0:T(8,128)S(1)} %collective-permute-done.1.bot_ref), custom_call_target="tpu_custom_call" | custom-call | flops 1000000 | bytes 3000000 | tf_op jit(solution)/shard_map/packs/pallas_call | solution.py:599
  29.6 3.6 %collective-permute-start.3 = (f32[192,128]{1,0:T(8,128)S(1)}, f32[192,128]{1,0:T(8,128)S(1)}, u32[]{:S(2)}, u32[]{:S(2)}) collective-permute-start(f32[192,128]{1,0:T(8,128)S(1)} %get-tuple-element.13.left_ref), channel_id=1, source_target_pairs={{0,15},{1,0},{2,1},{3,2},{4,3},{5,4},{6,5},{7,6},{8,7},{9,8},{10,9... | collective-permute-start | bytes 294920 | tf_op jit(solution)/shard_map/ppermute | solution.py:540
  33.1 0.7 %dynamic-slice_bitcast_fusion.thp_ref = f32[8,128]{1,0:T(8,128)S(1)} fusion(f32[8,8,128]{2,1,0:T(8,128)} %constant.58.clone, s32[]{:T(128)S(6)} %select_n.60), kind=kLoop, calls=%fused_computation.6 | loop fusion | bytes 8196 | tf_op jit(solution)/shard_map/jit(dynamic_index_in_dim)/squeeze | solution.py:571
  33.8 5.0 %interior.1 = (f32[768,128]{1,0:T(8,128)S(1)}, f32[2304,128]{1,0:T(8,128)S(1)}) custom-call(f32[768,128]{1,0:T(8,128)S(1)} %bitcast.55, f32[2304,128]{1,0:T(8,128)S(1)} %bitcast.51, f32[384,128]{1,0:T(8,128)S(1)} %collective-permute-done.top_ref, f32[384,128]{1,0:T(8,128)S(1)} %collective-permute-done.1.bot_ref, f32[72,128]{1,0:T(8,128)S(1)} %copy-done.6, ...), custom_call_target="tpu_custom_call" | custom-call | flops 30000000 | bytes 3000000 | tf_op jit(solution)/shard_map/interior/pallas_call | solution.py:602
  38.9 0.7 %copy-done.4 = f32[768,128]{1,0:T(8,128)} copy-done((f32[768,128]{1,0:T(8,128)}, f32[768,128]{1,0:T(8,128)S(1)}, u32[]{:S(2)}) %copy-start.4) | copy-done | bytes 393240
  39.6 0.6 %copy-done.9 = f32[192,128]{1,0:T(8,128)} copy-done((f32[192,128]{1,0:T(8,128)}, f32[192,128]{1,0:T(8,128)S(1)}, u32[]{:S(2)}) %copy-start.9) | copy-done | bytes 98328
  40.3 0.6 %copy-done.11 = f32[192,128]{1,0:T(8,128)} copy-done((f32[192,128]{1,0:T(8,128)}, f32[192,128]{1,0:T(8,128)S(1)}, u32[]{:S(2)}) %copy-start.11) | copy-done | bytes 98328
  40.9 1.0 %copy-done.5 = f32[768,128]{1,0:T(8,128)S(1)} copy-done((f32[768,128]{1,0:T(8,128)S(1)}, f32[768,128]{1,0:T(8,128)}, u32[]{:S(2)}) %copy-start.5) | copy-done | bytes 393240
  41.9 0.9 %copy-done.8 = f32[192,128]{1,0:T(8,128)S(1)} copy-done((f32[192,128]{1,0:T(8,128)S(1)}, f32[192,128]{1,0:T(8,128)}, u32[]{:S(2)}) %copy-start.8) | copy-done | bytes 98328
  42.8 0.9 %copy-done.10 = f32[192,128]{1,0:T(8,128)S(1)} copy-done((f32[192,128]{1,0:T(8,128)S(1)}, f32[192,128]{1,0:T(8,128)}, u32[]{:S(2)}) %copy-start.10) | copy-done | bytes 98328
  43.7 0.9 %copy-done.12 = f32[192,128]{1,0:T(8,128)S(1)} copy-done((f32[192,128]{1,0:T(8,128)S(1)}, f32[192,128]{1,0:T(8,128)}, u32[]{:S(2)}) %copy-start.12) | copy-done | bytes 98328
  44.6 0.7 %copy-done.13 = s32[8,512]{1,0:T(8,128)S(1)} copy-done((s32[8,512]{1,0:T(8,128)S(1)}, s32[8,512]{1,0:T(8,128)}, u32[]{:S(2)}) %copy-start.13) | copy-done | bytes 16408
  45.3 4.5 %edges.1 = (f32[768,128]{1,0:T(8,128)}, f32[2304,128]{1,0:T(8,128)}) custom-call(f32[768,128]{1,0:T(8,128)S(1)} %bitcast.56, f32[2304,128]{1,0:T(8,128)S(1)} %bitcast.52, f32[384,128]{1,0:T(8,128)S(1)} %collective-permute-done.top_ref, f32[384,128]{1,0:T(8,128)S(1)} %collective-permute-done.1.bot_ref, f32[192,128]{1,0:T(8,128)S(1)} %get-tuple-element.13.left_ref, ...), custom_call_target="tpu_custom_call" | custom-call | flops 10000000 | bytes 3000000 | tf_op jit(solution)/shard_map/edges/pallas_call | solution.py:611
  (49 shorter events, 1.1 us)
Async XLA Ops:
  0.6 18.5 %copy-start.14 = (s32[1,1,592]{2,1,0:T(1,128)S(1)}, s32[1,1,592]{2,1,0:T(1,128)}, u32[]{:S(2)}) copy-start(s32[1,1,592]{2,1,0:T(1,128)} %param.15) | copy-start | bytes 7108
  4.6 1.3 %copy-start = (f32[1,6,24,16,128]{4,3,2,1,0:T(8,128)S(1)}, f32[1,6,24,16,128]{4,3,2,1,0:T(8,128)}, u32[]{:S(2)}) copy-start(f32[1,6,24,16,128]{4,3,2,1,0:T(8,128)} %param.11) | copy-start | bytes 3538948
  5.9 1.0 %copy-start.2 = (f32[1,2,24,16,128]{4,3,2,1,0:T(8,128)S(1)}, f32[1,2,24,16,128]{4,3,2,1,0:T(8,128)}, u32[]{:S(2)}) copy-start(f32[1,2,24,16,128]{4,3,2,1,0:T(8,128)} %param.10) | copy-start | bytes 1179652
  6.9 22.0 %copy-start.1 = (f32[1,6,24,16,128]{4,3,2,1,0:T(8,128)S(1)}, f32[1,6,24,16,128]{4,3,2,1,0:T(8,128)}, u32[]{:S(2)}) copy-start(f32[1,6,24,16,128]{4,3,2,1,0:T(8,128)} %param.11) | copy-start | bytes 3538948
  6.9 22.0 %copy-start.3 = (f32[1,2,24,16,128]{4,3,2,1,0:T(8,128)S(1)}, f32[1,2,24,16,128]{4,3,2,1,0:T(8,128)}, u32[]{:S(2)}) copy-start(f32[1,2,24,16,128]{4,3,2,1,0:T(8,128)} %param.10) | copy-start | bytes 1179652
  10.2 18.7 %collective-permute-start = (f32[384,128]{1,0:T(8,128)S(1)}, f32[384,128]{1,0:T(8,128)S(1)}, u32[]{:S(2)}, u32[]{:S(2)}) collective-permute-start(f32[384,128]{1,0:T(8,128)S(1)} %get-tuple-element.11), channel_id=1, source_target_pairs={{0,16},{16,32},{32,48},{48,64},{64,80},{80,96},{96,112},{112,0},{1... | collective-permute-start | bytes 589832 | tf_op jit(solution)/shard_map/ppermute | solution.py:540
  12.3 16.6 %collective-permute-start.1 = (f32[384,128]{1,0:T(8,128)S(1)}, f32[384,128]{1,0:T(8,128)S(1)}, u32[]{:S(2)}, u32[]{:S(2)}) collective-permute-start(f32[384,128]{1,0:T(8,128)S(1)} %get-tuple-element.12), channel_id=1, source_target_pairs={{0,112},{16,0},{32,16},{48,32},{64,48},{80,64},{96,80},{112,96},{1... | collective-permute-start | bytes 589832 | tf_op jit(solution)/shard_map/ppermute | solution.py:540
  16.3 4.2 %collective-permute-start.4 = (f32[16,32,128]{2,1,0:T(8,128)S(1)}, f32[16,32,128]{2,1,0:T(8,128)}, u32[]{:S(2)}, u32[]{:S(2)}) collective-permute-start(f32[16,32,128]{2,1,0:T(8,128)S(1)} %get-tuple-element.15), channel_id=1, source_target_pairs={{0,128},{128,0},{1,129},{129,1},{2,130},{130,2},{3,131},{131,3},{4... | collective-permute-start | bytes 786440 | tf_op jit(solution)/shard_map/ppermute | solution.py:595
  20.4 13.4 %copy-start.6 = (f32[72,128]{1,0:T(8,128)S(1)}, f32[72,128]{1,0:T(8,128)}, u32[]{:S(2)}) copy-start(f32[72,128]{1,0:T(8,128)} %constant.56.clone.rad_ref) | copy-start | bytes 110596
  20.4 20.5 %all-to-all-start = ((f32[16,32,128]{2,1,0:T(8,128)}), f32[16,32,128]{2,1,0:T(8,128)S(1)}, u32[]{:S(2)}, u32[]{:S(2)}) async-start(f32[16,32,128]{2,1,0:T(8,128)} %collective-permute-done.4), calls=%async_computation | async-start | bytes 524288 | tf_op jit(solution)/shard_map/all_to_all | solution.py:596
  29.5 10.1 %copy-start.7 = (f32[192,128]{1,0:T(8,128)}, f32[192,128]{1,0:T(8,128)S(1)}, u32[]{:S(2)}) copy-start(f32[192,128]{1,0:T(8,128)S(1)} %get-tuple-element.14.right_ref) | copy-start | bytes 294916
  29.6 10.0 %collective-permute-start.3 = (f32[192,128]{1,0:T(8,128)S(1)}, f32[192,128]{1,0:T(8,128)S(1)}, u32[]{:S(2)}, u32[]{:S(2)}) collective-permute-start(f32[192,128]{1,0:T(8,128)S(1)} %get-tuple-element.13.left_ref), channel_id=1, source_target_pairs={{0,15},{1,0},{2,1},{3,2},{4,3},{5,4},{6,5},{7,6},{8,7},{9,8},{10,9... | collective-permute-start | bytes 294920 | tf_op jit(solution)/shard_map/ppermute | solution.py:540
  33.1 7.1 %collective-permute-start.2 = (f32[192,128]{1,0:T(8,128)S(1)}, f32[192,128]{1,0:T(8,128)S(1)}, u32[]{:S(2)}, u32[]{:S(2)}) collective-permute-start(f32[192,128]{1,0:T(8,128)S(1)} %get-tuple-element.14.right_ref), channel_id=1, source_target_pairs={{0,1},{1,2},{2,3},{3,4},{4,5},{5,6},{6,7},{7,8},{8,9},{9,10},{10,1... | collective-permute-start | bytes 294920 | tf_op jit(solution)/shard_map/ppermute | solution.py:540
  38.8 0.7 %copy-start.4 = (f32[768,128]{1,0:T(8,128)}, f32[768,128]{1,0:T(8,128)S(1)}, u32[]{:S(2)}) copy-start(f32[768,128]{1,0:T(8,128)S(1)} %get-tuple-element.16.isc_ref) | copy-start | bytes 1179652
  39.6 0.6 %copy-start.9 = (f32[192,128]{1,0:T(8,128)}, f32[192,128]{1,0:T(8,128)S(1)}, u32[]{:S(2)}) copy-start(f32[192,128]{1,0:T(8,128)S(1)} %collective-permute-done.3.fromright_ref) | copy-start | bytes 294916
  40.3 0.6 %copy-start.11 = (f32[192,128]{1,0:T(8,128)}, f32[192,128]{1,0:T(8,128)S(1)}, u32[]{:S(2)}) copy-start(f32[192,128]{1,0:T(8,128)S(1)} %collective-permute-done.2.fromleft_ref) | copy-start | bytes 294916
  40.9 1.0 %copy-start.5 = (f32[768,128]{1,0:T(8,128)S(1)}, f32[768,128]{1,0:T(8,128)}, u32[]{:S(2)}) copy-start(f32[768,128]{1,0:T(8,128)} %copy-done.4) | copy-start | bytes 1179652
  41.9 0.9 %copy-start.8 = (f32[192,128]{1,0:T(8,128)S(1)}, f32[192,128]{1,0:T(8,128)}, u32[]{:S(2)}) copy-start(f32[192,128]{1,0:T(8,128)} %copy-done.7) | copy-start | bytes 294916
  42.8 0.9 %copy-start.10 = (f32[192,128]{1,0:T(8,128)S(1)}, f32[192,128]{1,0:T(8,128)}, u32[]{:S(2)}) copy-start(f32[192,128]{1,0:T(8,128)} %copy-done.9) | copy-start | bytes 294916
  43.7 0.9 %copy-start.12 = (f32[192,128]{1,0:T(8,128)S(1)}, f32[192,128]{1,0:T(8,128)}, u32[]{:S(2)}) copy-start(f32[192,128]{1,0:T(8,128)} %copy-done.11) | copy-start | bytes 294916
  44.6 0.7 %copy-start.13 = (s32[8,512]{1,0:T(8,128)S(1)}, s32[8,512]{1,0:T(8,128)}, u32[]{:S(2)}) copy-start(s32[8,512]{1,0:T(8,128)} %pad.19.idx_ref) | copy-start | bytes 49156

commit v2 on v1

v2 whole, which is shorter than its diff:
```python
import math

import jax
import jax.numpy as jnp
import numpy as np
from jax import lax
from jax.experimental import pallas as pl
from jax.experimental.pallas import tpu as pltpu
from jax.sharding import PartitionSpec as P

GAMMA = 5.0 / 3.0
F32 = jnp.float32
BF16 = jnp.bfloat16
SH = 24
NR = 16
NC = 128
N_LAT = 8
N_LON = 16
CAP = 19
CHUNK = 32
EXT = NR + 4
ROW_SCALARS = 4

D_TH = 0.5 * math.pi / (NR * N_LAT)
D_PH = 1.5 * math.pi / (NC * N_LON)
D_R = 0.6 * D_TH
DT = 0.3 * min(D_R, 0.6 * math.sin(0.25 * math.pi - 2.0 * D_TH) * D_PH)
MU = DT / 0.9
GRAV = 0.036 / DT
OMEGA = 0.05 / DT


def theta_of(k):
    return 0.25 * math.pi + (k + 0.5) * D_TH


def phi_of(m):
    return -0.75 * math.pi + (m + 0.5) * D_PH


def lane_rows(shift):
    lane = (np.arange(NC) + shift) % NC
    return lane // 6, lane % 6


G_ROWS = 0
G_RAD = EXT * ROW_SCALARS
G_PACK = G_RAD + 3 * SH
G_FRAME = G_PACK + 8
G_PHI = G_FRAME + 16
G_ALL = G_PHI + 8


def frame_table(i):
    wide = NC + 4
    at = np.full((4, NC), -1)
    row = 0 if i == 0 else 2
    for j in range(2):
        at[j] = (row + j) * wide + 2 + np.arange(NC)
    for side in range(2):
        r, c = lane_rows(2 * side)
        for lane in range(NC):
            col = c[lane] if side == 0 else NC - 2 + c[lane]
            if r[lane] in (0, 1):
                at[2 + side, lane] = r[lane] * wide + col
            elif r[lane] in (EXT - 2, EXT - 1):
                at[2 + side, lane] = (r[lane] - NR) * wide + col
            elif r[lane] < EXT and side == 0 and c[lane] < 2:
                at[2, lane] = 4 * wide + 2 * (r[lane] - 2) + c[lane]
            elif r[lane] < EXT and side == 1 and c[lane] >= 4:
                at[3, lane] = 4 * wide + 2 * NR + 2 * (r[lane] - 2) + c[lane] - 4
    out = np.zeros((16, NC))
    out[8:] = -1
    out[0:4] = np.where(at >= 0, at % NC, 0)
    out[8:12] = np.where(at >= 0, at // NC, -1)
    return out


def lat_table():
    out = np.zeros((N_LAT, G_PHI, NC))
    s = np.arange(SH, dtype=np.float64)
    r = 0.6 + (s + 0.5) * D_R
    ratio = np.ones(SH)
    ratio[0] = r[0] / (0.6 - 0.5 * D_R)
    ratio[-1] = r[-1] / (0.6 + (SH + 0.5) * D_R)
    out[:, G_RAD:G_PACK] = np.concatenate([1.0 / r, ratio, DT * GRAV / (r * r)])[:, None]

    def four(th):
        return np.stack([np.sin(th), np.cos(th), np.cos(th) / np.sin(th), 1.0 / np.sin(th)])

    for i in range(N_LAT):
        th = theta_of(i * NR - 2 + np.arange(EXT))
        out[i, G_ROWS:G_RAD] = four(th).T.reshape(-1)[:, None]
        for side in range(2):
            rr, _ = lane_rows(2 * side)
            at = G_PACK + 4 * side
            out[i, at : at + 4] = four(theta_of(i * NR - 2 + np.minimum(rr, EXT - 1)))
        out[i, G_FRAME:G_PHI] = frame_table(i)
    return out.astype(np.float32)


def lon_table():
    out = np.zeros((N_LON, 8, NC))
    for q in range(N_LON):
        ph = phi_of(q * NC + np.arange(NC))
        out[q, 0], out[q, 1] = np.sin(ph), np.cos(ph)
        for side in range(2):
            _, c = lane_rows(2 * side)
            ph = phi_of(q * NC + (c - 2 if side == 0 else c + NC - 4))
            out[q, 2 + 2 * side], out[q, 3 + 2 * side] = np.sin(ph), np.cos(ph)
    return out.astype(np.float32)


class Geo:
    def __init__(self, geo_ref, sin, cos, cot, isin, sphi, cphi, yang):
        self.rinv = geo_ref[G_RAD : G_RAD + SH, :]
        self.ratio = geo_ref[G_RAD + SH : G_RAD + 2 * SH, :]
        self.grav = geo_ref[G_RAD + 2 * SH : G_RAD + 3 * SH, :]
        self.ct = self.rinv * (0.5 / D_TH)
        self.cp = self.rinv * (0.5 / D_PH) * isin
        self.cotr = self.rinv * cot
        self.n_r = (1.0 - yang) * cos + yang * (sin * sphi)
        self.n_t = (yang - 1.0) * sin + yang * (cos * sphi)
        self.n_p = yang * cphi


def lane_roll(x, shift):
    return pltpu.roll(x, shift % NC, 1)


def diff_p(x):
    return lane_roll(x, -1) - lane_roll(x, 1)


def diff_r(x, ghost, edges):
    first, last = edges
    return jnp.where(last, ghost, pltpu.roll(x, SH - 1, 0)) - jnp.where(
        first, ghost, pltpu.roll(x, 1, 0)
    )


def cross(a, b):
    return (
        a[1] * b[2] - a[2] * b[1],
        a[2] * b[0] - a[0] * b[2],
        a[0] * b[1] - a[1] * b[0],
    )


def stage_one(u, diff_t, geo, edges, full):
    rinv, ct, cp, cotr = geo.rinv, geo.ct, geo.cp, geo.cotr
    cr = 0.5 / D_R
    rho, pr = u[0], u[1]
    v, b = u[2:5], u[5:8]

    def d_r(x):
        return diff_r(x, x, edges) * cr

    def d_t(fn):
        return diff_t(fn) * ct

    def d_p(x):
        return diff_p(x) * cp

    bt_r, bp_r = d_r(b[1]), d_r(b[2])
    j_r = d_t(lambda w: w[7]) + b[2] * cotr - d_p(b[1])
    jt_ang = d_p(b[0]) - b[2] * rinv
    jp_ang = b[1] * rinv - d_t(lambda w: w[5])
    jj = (j_r, jt_ang - bp_r, bt_r + jp_ang)
    vr = [d_r(x) for x in v]
    vt = [d_t(lambda w, i=i: w[2 + i]) for i in range(3)]
    vp = [d_p(x) for x in v]
    wt_ang = vp[0] - v[2] * rinv
    wp_ang = v[1] * rinv - vt[0]
    ww = (vt[2] + v[2] * cotr - vp[1], wt_ang - vr[2], vr[1] + wp_ang)
    e_ang = 2.0 * v[0] * rinv + vt[1] + v[1] * cotr + vp[2]
    ee = vr[0] + e_ang
    vxb = cross(v, b)
    el = [vxb[i] - MU * jj[i] for i in range(3)]
    ratio = geo.ratio
    level = list(ww) + [ee] + el
    level += [
        wt_ang * ratio,
        wp_ang * ratio,
        e_ang * ratio,
        vxb[1] - MU * (jt_ang * ratio),
        vxb[2] - MU * (jp_ang * ratio),
    ]
    if not full:
        return level, None, None
    fr, fp = rho * v[0], rho * v[2]
    mass = (
        d_r(fr)
        + 2.0 * fr * rinv
        + d_t(lambda w: w[0] * w[3])
        + rho * v[1] * cotr
        + d_p(fp)
    )
    gp = (d_r(pr), d_t(lambda w: w[1]), d_p(pr))
    press = -(v[0] * gp[0] + v[1] * gp[1] + v[2] * gp[2]) - GAMMA * pr * ee
    lor = cross(jj, b)
    spin = cross(v, (geo.n_r, geo.n_t, geo.n_p))
    curv = (
        -(v[1] * v[1] + v[2] * v[2]) * rinv,
        v[0] * v[1] * rinv - v[2] * v[2] * cotr,
        v[0] * v[2] * rinv + v[1] * v[2] * cotr,
    )
    irho = DT / rho
    rest = []
    for i in range(3):
        adv = v[0] * vr[i] + v[1] * vt[i] + v[2] * vp[i] + curv[i]
        x = (lor[i] - gp[i]) * irho - DT * adv + (2.0 * OMEGA * DT) * spin[i]
        rest.append(x - geo.grav if i == 0 else x)
    rest.append(irho * MU)
    return level, rest, (-DT * mass, DT * press)


def stage_two(q, diff_t, rest, geo, edges):
    rinv, ct, cp, cotr = geo.rinv, geo.ct, geo.cp, geo.cotr
    cr = 0.5 / D_R

    def d_r(i, g):
        return diff_r(q[i], q[g], edges) * cr

    def d_t(i):
        return diff_t(i) * ct

    def d_p(i):
        return diff_p(q[i]) * cp

    def curl(o, gt, gp):
        return (
            d_t(o + 2) + q[o + 2] * cotr - d_p(o + 1),
            d_p(o) - d_r(o + 2, gp) - q[o + 2] * rinv,
            d_r(o + 1, gt) + q[o + 1] * rinv - d_t(o),
        )

    cw = curl(0, 7, 8)
    grad_e = (d_r(3, 9), d_t(3), d_p(3))
    ce = curl(4, 10, 11)
    acc = [rest[i] + rest[3] * (4.0 / 3.0 * grad_e[i] - cw[i]) for i in range(3)]
    return acc + [DT * ce[i] for i in range(3)]


def shell_edges():
    s = lax.broadcasted_iota(jnp.int32, (SH, NC), 0)
    return s == 0, s == SH - 1


def aligned(i):
    return i if isinstance(i, int) else pl.multiple_of(i, 8)


def tile(ref, i):
    return ref[pl.ds(aligned(i * SH), SH), :]


def put(ref, i, val):
    ref[pl.ds(aligned(i * SH), SH), :] = val


def row_values(geo_ref, e):
    return [geo_ref[pl.ds(e * ROW_SCALARS + j, 1), :] for j in range(ROW_SCALARS)]


def row_geo(geo_ref, e, yang):
    return Geo(
        geo_ref, *row_values(geo_ref, e), geo_ref[G_PHI : G_PHI + 1, :],
        geo_ref[G_PHI + 1 : G_PHI + 2, :], yang,
    )


def rows_one(fields, q_ref, r_ref, depth, geo, edges, slot, full):
    up, dn = fields(1), fields(-1)
    level, rest, scal = stage_one(fields(0), lambda fn: fn(up) - fn(dn), geo, edges, full)
    for i, x in enumerate(level):
        put(q_ref, i * depth + slot, x)
    if full:
        for i, x in enumerate(rest):
            put(r_ref, i * depth + slot, x)
    return scal


def rows_two(q_ref, r_ref, depth, geo, edges, slot):
    q = [tile(q_ref, i * depth + slot) for i in range(12)]

    def diff_t(i):
        return tile(q_ref, i * depth + slot + 1) - tile(q_ref, i * depth + slot - 1)

    rest = [tile(r_ref, i * depth + slot) for i in range(4)]
    return stage_two(q, diff_t, rest, geo, edges)


def native_row(f, k):
    return pl.ds(f * (SH * NR) + k, SH, stride=NR)


def donor_kernel(sc_hbm, ve_hbm, cr_hbm, cc_hbm, sw_hbm, rs_hbm, lat_hbm, lon_hbm,
                 pay_ref, up_ref, dn_ref, own_ref, geo_ref, idx_ref,
                 blk, cr, cc, sw, rs, tab, s_hi, s_lo, c_hi, c_lo, sems):
    lat, lon = lax.axis_index("lat"), lax.axis_index("lon")
    n_sc = 2 * SH * NR
    moves = [
        (cr_hbm.at[0, 0], cr),
        (cc_hbm.at[0, 0], cc),
        (sw_hbm.at[:, 0, 0], sw),
        (rs_hbm, rs),
        (lat_hbm.at[lat], geo_ref.at[0:G_PHI]),
        (lon_hbm.at[lon], geo_ref.at[G_PHI:G_ALL]),
        (sc_hbm, blk.at[0:n_sc]),
        (ve_hbm, blk.at[n_sc : 4 * n_sc]),
    ]
    copies = [pltpu.make_async_copy(a, b, sems.at[i]) for i, (a, b) in enumerate(moves)]
    for c in copies:
        c.start()
    tab[...] = jnp.zeros((NC, NC), F32)
    for c in copies[:3]:
        c.wait()
    tab[0:16, 0:CAP] = cr[...].astype(F32)
    tab[16:32, 0:CAP] = cc[...].astype(F32)
    tab[32:48, 0:CAP] = sw[0]
    tab[48:64, 0:CAP] = sw[1]
    cols = jnp.transpose(tab[...])
    lane = lax.broadcasted_iota(jnp.int32, (48, NC), 1).astype(F32)
    for pair in range(N_LON // 2):
        a, b, wt, wp = [
            jnp.concatenate(
                [
                    jnp.broadcast_to(cols[0:24, o : o + 1], (24, NC))
                    for o in (j * N_LON + 2 * pair, j * N_LON + 2 * pair + 1)
                ],
                axis=0,
            )
            for j in range(4)
        ]
        along = jnp.where(lane == b, 1.0 - wp, jnp.where(lane == b + 1.0, wp, 0.0))
        first, second = along * (1.0 - wt), along * wt
        for k in range(NR):
            s = jnp.where(a == float(k), first, jnp.where(a == float(k - 1), second, 0.0))
            hi = s.astype(BF16)
            s_hi[48 * pair : 48 * pair + 48, k * NC : (k + 1) * NC] = hi
            s_lo[48 * pair : 48 * pair + 48, k * NC : (k + 1) * NC] = (
                s - hi.astype(F32)
            ).astype(BF16)
    for c in copies[3:]:
        c.wait()
    at = geo_ref[G_FRAME : G_FRAME + 8, :].astype(jnp.int32)
    group = geo_ref[G_FRAME + 8 : G_FRAME + 16, :]
    g = jnp.full((8, NC), -1, jnp.int32)
    for i in range(5):
        end = min((i + 1) * NC, rs.shape[2])
        src = rs[0, :, i * NC : end]
        if end - i * NC < NC:
            src = jnp.concatenate([src, jnp.zeros((1, (i + 1) * NC - end), jnp.int32)], axis=1)
        src = jnp.broadcast_to(src, (8, NC))
        g = jnp.where(group == float(i), jnp.take_along_axis(src, at, axis=1), g)
    idx_ref[...] = g
    sphi, cphi = geo_ref[G_PHI : G_PHI + 1, :], geo_ref[G_PHI + 1 : G_PHI + 2, :]
    for k in range(NR):
        u = [blk[native_row(f, k), :] for f in range(8)]
        for f in range(8):
            put(own_ref, f * NR + k, u[f])
        for first, ref in ((0, dn_ref), (NR - 2, up_ref)):
            if k - first in (0, 1):
                for f in range(8):
                    put(ref, f * 2 + k - first, u[f])
        sin, cos = row_values(geo_ref, k + 2)[:2]
        c = [u[0], u[1]]
        for o in (2, 5):
            flat = u[o] * sin + u[o + 1] * cos
            c += [
                flat * cphi - u[o + 2] * sphi,
                flat * sphi + u[o + 2] * cphi,
                u[o] * cos - u[o + 1] * sin,
            ]
        c = jnp.concatenate(c, axis=0)
        hi = c.astype(BF16)
        c_hi[:, k * NC : (k + 1) * NC] = hi
        c_lo[:, k * NC : (k + 1) * NC] = (c - hi.astype(F32)).astype(BF16)

    def dot(x, y):
        return lax.dot_general(
            x[...], y[...], (((1,), (1,)), ((), ())), preferred_element_type=F32
        )

    sent = dot(s_hi, c_hi) + dot(s_hi, c_lo) + dot(s_lo, c_hi)
    for t in range(N_LON):
        pay_ref[t, 0:24, :] = sent[24 * t : 24 * t + 24, 0:NC]
        part = sent[24 * t : 24 * t + 24, NC : NC + 64]
        pay_ref[t, 24:32, :] = jnp.zeros((8, NC), F32)
        pay_ref[t, 19:29, 0:64] = part[0:10]
        pay_ref[t, 19:28, 64:128] = part[10:19]


def row_of(own_ref, top_ref, bot_ref, f, e):
    if isinstance(e, int) and e < 2:
        return tile(top_ref, f * 2 + e)
    if isinstance(e, int) and e >= NR + 2:
        return tile(bot_ref, f * 2 + e - NR - 2)
    return tile(own_ref, f * NR + e - 2)


def pack_kernel(own_ref, top_ref, bot_ref, left_ref, right_ref):
    lane = lax.broadcasted_iota(jnp.int32, (SH, NC), 1)
    for f in range(8):
        left = jnp.zeros((SH, NC), F32)
        right = jnp.zeros((SH, NC), F32)
        for e in range(EXT):
            x = lane_roll(row_of(own_ref, top_ref, bot_ref, f, e), 6 * e + 2)
            base = 6 * e
            left = jnp.where((lane >= base + 2) & (lane < base + 6), x, left)
            if e == 0:
                right = jnp.where((lane >= NC - 2) | (lane < 2), x, right)
            else:
                right = jnp.where((lane >= base - 2) & (lane < base + 2), x, right)
        put(left_ref, f, left)
        put(right_ref, f, right)


def main_kernel(own_ref, top_ref, bot_ref, geo_ref, out_ref, q_ref, r_ref):
    yang = lax.axis_index("panel").astype(F32)
    edges = shell_edges()

    def one(e, full):
        def fields(step):
            return [row_of(own_ref, top_ref, bot_ref, f, e + step) for f in range(8)]

        geo = row_geo(geo_ref, e, yang)
        scal = rows_one(fields, q_ref, r_ref, EXT, geo, edges, e, full)
        if full:
            for i in range(2):
                put(out_ref, i * NR + e - 2, scal[i])

    one(1, False)
    one(2, True)
    one(NR + 1, True)
    one(NR + 2, False)

    @pl.loop(3, NR + 1)
    def _(e):
        one(e, True)

    @pl.loop(2, NR + 2)
    def _(e):
        vec = rows_two(q_ref, r_ref, EXT, row_geo(geo_ref, e, yang), edges, e)
        for i in range(6):
            put(out_ref, (2 + i) * NR + e - 2, vec[i])


def to_spherical(x, y, z, sin, cos, sphi, cphi):
    flat = x * cphi + y * sphi
    return [flat * sin + z * cos, flat * cos - z * sin, y * cphi - x * sphi]


def border_fields(w, sin, cos, sphi, cphi):
    out = [w[0], w[1]]
    for o in (2, 5):
        out += to_spherical(-w[o], w[o + 2], w[o + 1], sin, cos, sphi, cphi)
    return out


STRIP = 6


def edge_kernel(own_ref, left_hbm, right_hbm, fromleft_hbm, fromright_hbm,
                don_ref, idx_ref, geo_ref, int_ref, osc_hbm, ove_hbm,
                out_ref, pack_ref, bord_ref, u_ref, q_ref, r_ref, sems):
    yang = lax.axis_index("panel").astype(F32)
    lat = lax.axis_index("lat")
    lon = lax.axis_index("lon")
    edges = shell_edges()
    row_edge = (lat == 0) | (lat == N_LAT - 1)
    col_edge = (lon == 0) | (lon == N_LON - 1)
    per = SH * NR
    fetches = [
        pltpu.make_async_copy(src, pack_ref.at[i], sems.at[8 + i])
        for i, src in enumerate((left_hbm, fromleft_hbm, right_hbm, fromright_hbm))
    ]
    for c in fetches:
        c.start()

    @pl.when(row_edge | col_edge)
    def _():
        recv = jnp.transpose(don_ref[...])
        hi = recv.astype(BF16)
        lo = (recv - hi.astype(F32)).astype(BF16)
        at = lax.broadcasted_iota(jnp.int32, (N_LON * CHUNK, NC), 0)
        for col in range(4):
            g = idx_ref[col : col + 1, :]
            donor = jnp.floor((g.astype(F32) + 0.5) * (1.0 / CAP)).astype(jnp.int32)
            slot = g - donor * CAP
            first = donor * CHUNK + slot
            here = jnp.where(g >= 0, first, -1)
            low = jnp.where((g >= 0) & (slot < 10), first + 19, -1)
            high = jnp.where((g >= 0) & (slot >= 10), first + 9, -1)

            def pick(where, lo_row, hi_row):
                hot = jnp.where(at == where, 1.0, 0.0).astype(BF16)
                return jnp.dot(hi[lo_row:hi_row], hot, preferred_element_type=F32) + jnp.dot(
                    lo[lo_row:hi_row], hot, preferred_element_type=F32
                )

            here_at = slice(col * NC, (col + 1) * NC)
            bord_ref[0:NC, here_at] = pick(here, 0, NC)
            bord_ref[NC : NC + 64, here_at] = pick(low, 0, 64) + pick(high, 64, NC)

    def border(col, sin, cos, sphi, cphi):
        w = [bord_ref[f * SH : f * SH + SH, col * NC : (col + 1) * NC] for f in range(8)]
        return border_fields(w, sin, cos, sphi, cphi)

    for c in fetches:
        c.wait()
    lane = lax.broadcasted_iota(jnp.int32, (SH, NC), 1)
    place = lane % 6
    merged = None
    for side in range(2):
        own, other = pack_ref.at[2 * side], pack_ref.at[2 * side + 1]
        theirs = (place < 2) if side == 0 else ((place == 2) | (place == 3))
        at = G_PACK + 4 * side
        th = [geo_ref[at + j : at + j + 1, :] for j in range(4)]
        at = G_PHI + 2 + 2 * side
        ph = [geo_ref[at + j : at + j + 1, :] for j in range(2)]
        g = jnp.broadcast_to(idx_ref[2 + side : 3 + side, :], (SH, NC))
        donated = border(2 + side, th[0], th[1], ph[0], ph[1])
        u = []
        for f in range(8):
            x = jnp.where(theirs, tile(other, f), tile(own, f))
            u.append(jnp.where(g >= 0, donated[f], x))
        geo = Geo(geo_ref, *th, *ph, yang)

        def diff_six(x):
            return lane_roll(x, -6) - lane_roll(x, 6)

        level, rest, scal = stage_one(u, lambda fn: diff_six(fn(u)), geo, edges, True)
        vec = stage_two(level, lambda i: diff_six(level[i]), rest, geo, edges)
        vals = list(scal) + vec
        if side == 0:
            merged = vals
        else:
            merged = [jnp.where(place < 2, y, x) for x, y in zip(merged, vals)]
    for f in range(8):
        put(u_ref, 8 * STRIP + f, merged[f])

    @pl.when(row_edge)
    def _():
        top = lat == 0
        e0 = jnp.where(top, 0, NR - 2)
        for i in range(2):
            sc = row_values(geo_ref, jnp.where(top, i, NR + 2 + i))
            phi = [geo_ref[G_PHI + j : G_PHI + j + 1, :] for j in range(2)]
            w = border(i, sc[0], sc[1], phi[0], phi[1])
            for f in range(8):
                put(u_ref, f * STRIP + jnp.where(top, i, 4 + i), w[f])
        for j in range(4):
            for f in range(8):
                x = tile(own_ref, f * NR + jnp.where(top, j, NR - 4 + j))
                put(u_ref, f * STRIP + jnp.where(top, 2 + j, j), x)

        for slot in (1, 2, 3, 4):
            def fields(step, slot=slot):
                return [tile(u_ref, f * STRIP + slot + step) for f in range(8)]

            full = slot in (2, 3)
            geo = row_geo(geo_ref, e0 + slot, yang)
            scal = rows_one(fields, q_ref, r_ref, STRIP, geo, edges, slot, full)
            if full:
                for i in range(2):
                    put(r_ref, (4 + i) * STRIP + slot, scal[i])
        for slot in (2, 3):
            vec = rows_two(q_ref, r_ref, STRIP, row_geo(geo_ref, e0 + slot, yang), edges, slot)
            for i in range(6):
                put(r_ref, (6 + i) * STRIP + slot, vec[i])

    edge_lane = (lane < 2) | (lane >= NC - 2)
    sends = []
    for f in range(8):
        cols = tile(u_ref, 8 * STRIP + f)
        for k in range(NR):
            x = lane_roll(cols, -(6 * (k + 2) + 2))
            out_ref[native_row(f, k), :] = jnp.where(edge_lane, x, tile(int_ref, f * NR + k))

        @pl.when(row_edge)
        def _(f=f):
            k0 = jnp.where(lat == 0, 0, NR - 2)
            for j in range(2):
                at = native_row(f, k0 + j)
                val = tile(r_ref, (4 + f) * STRIP + 2 + j)
                out_ref[at, :] = jnp.where(edge_lane, out_ref[at, :], val)

        dst = osc_hbm.at[pl.ds(f * per, per)] if f < 2 else ove_hbm.at[pl.ds((f - 2) * per, per)]
        sends.append(pltpu.make_async_copy(out_ref.at[pl.ds(f * per, per)], dst, sems.at[f]))
        sends[-1].start()
    for c in sends:
        c.wait()


VM = pl.BlockSpec(memory_space=pltpu.VMEM)
HBM = pl.BlockSpec(memory_space=pltpu.HBM)


def call(kernel, ins, outs, scratch, name, flops, mib):
    return pl.pallas_call(
        kernel,
        out_shape=[jax.ShapeDtypeStruct(s, t) for s, t, _ in outs],
        in_specs=ins,
        out_specs=[o[2] for o in outs],
        scratch_shapes=scratch,
        name=name,
        compiler_params=pltpu.CompilerParams(vmem_limit_bytes=mib * 1024 * 1024),
        cost_estimate=pl.CostEstimate(flops=flops, bytes_accessed=100000, transcendentals=0),
    )


def rows(n):
    return pltpu.VMEM((n * SH, NC), F32)


def shifted(x, axis, step):
    n = lax.axis_size(axis)
    return lax.ppermute(x, axis, [(i, (i + step) % n) for i in range(n)])


def body(scalars, vectors, corner_rows, corner_cols, send_weights, recv_source):
    sc = scalars.reshape(2 * SH * NR, NC)
    ve = vectors.reshape(6 * SH * NR, NC)
    halo = ((8 * 2 * SH, NC), F32, VM)
    pack = ((8 * SH, NC), F32, VM)
    block = ((8 * NR * SH, NC), F32, VM)
    table = pltpu.VMEM((N_LON, CAP), jnp.int32)

    def in_hbm(*arrays):
        return [pltpu.with_memory_space_constraint(a, pltpu.HBM) for a in arrays]

    pay, up, dn, own, geo, idx = call(
        donor_kernel, [HBM] * 8,
        [
            ((N_LON, CHUNK, NC), F32, VM), halo, halo, block,
            ((G_ALL, NC), F32, VM), ((8, NC), jnp.int32, VM),
        ],
        [
            rows(8 * NR), table, table,
            pltpu.VMEM((2, N_LON, CAP), F32),
            pltpu.VMEM((1, 1, 592), jnp.int32),
            pltpu.VMEM((NC, NC), F32),
            pltpu.VMEM((24 * N_LON, NR * NC), BF16),
            pltpu.VMEM((24 * N_LON, NR * NC), BF16),
            pltpu.VMEM((8 * SH, NR * NC), BF16),
            pltpu.VMEM((8 * SH, NR * NC), BF16),
            pltpu.SemaphoreType.DMA((8,)),
        ],
        "donor", 400000000, 20,
    )(*in_hbm(sc, ve, corner_rows, corner_cols, send_weights, recv_source,
              jnp.asarray(lat_table()), jnp.asarray(lon_table())))
    pay = lax.ppermute(pay, "panel", [(0, 1), (1, 0)])
    don = lax.all_to_all(pay, "lon", 0, 0, tiled=True).reshape(N_LON * CHUNK, NC)
    top = shifted(up, "lat", 1)
    bot = shifted(dn, "lat", -1)
    left, right = call(pack_kernel, [VM] * 3, [pack, pack], [], "packs", 50000000000, 12)(
        own, top, bot
    )
    from_left = shifted(right, "lon", 1)
    from_right = shifted(left, "lon", -1)
    (inner,) = call(
        main_kernel, [VM] * 4, [block], [rows(12 * EXT), rows(4 * EXT)],
        "interior", 300000, 16,
    )(own, top, bot, geo)
    osc, ove = call(
        edge_kernel, [VM] + [HBM] * 4 + [VM] * 4,
        [(sc.shape, F32, HBM), (ve.shape, F32, HBM)],
        [
            rows(8 * NR),
            pltpu.VMEM((4, 8 * SH, NC), F32),
            pltpu.VMEM((8 * SH, 4 * NC), F32),
            rows(8 * STRIP + 8), rows(12 * STRIP), rows(12 * STRIP),
            pltpu.SemaphoreType.DMA((12,)),
        ],
        "edges", 10000000, 16,
    )(own, *in_hbm(left, right, from_left, from_right), don, idx, geo, inner)
    return osc.reshape(scalars.shape), ove.reshape(vectors.shape)


def solution(mesh):
    return jax.shard_map(
        body,
        mesh=mesh,
        in_specs=(
            P("panel", None, None, "lat", "lon"),
            P("panel", None, None, "lat", "lon"),
            P("lat", "lon", None, None),
            P("lat", "lon", None, None),
            P(None, "lat", "lon", None, None),
            P("lat", "lon", None),
        ),
        out_specs=(P("panel", None, None, "lat", "lon"), P("panel", None, None, "lat", "lon")),
        check_vma=False,
    )
```

time: 50.5 us -> 35.8 us (0.71)
  the two profiles are of different devices: /device:TPU:1 before, /device:TPU:8 now
where the time goes in v2:
time: 35.8 us; the launch traced here: 35.2 us
  starting transfers between devices  18.4 us (51%)
  Pallas kernels  12.1 us (34%)
  local copies, waits for them, and re-layouts  2.63 us (7%)
  waiting for transfers between devices  1.28 us (4%)
  between operations  0.71 us (2%)
    all_to_all x1, starting transfers between devices, body(): lax.all_to_all(pay, 'lon', 0, 0, tiled=True).reshape(N_LON * CHUNK, NC)  9.94 us
    ppermute x4, starting transfers between devices, shifted(): return lax.ppermute(x, axis, [(i, (i + step) % n) for i in range(n)])  8.39 us
    pallas_call x1, Pallas kernels, body(): call(edge_kernel, [VM] + [HBM] * 4 + [VM] * 4, [(sc.shape, F32, HBM), (ve...  3.93 us
    pallas_call x1, Pallas kernels, body(): call(donor_kernel, [HBM] * 8, [((N_LON, CHUNK, NC), F32, VM), halo, halo,...  3.92 us
    pallas_call x1, Pallas kernels, body(): call(main_kernel, [VM] * 4, [block], [rows(12 * EXT), rows(4 * EXT)], 'in...  3.69 us
    unnamed x14, local copies, waits for them, and re-layouts  2.63 us
    ppermute x4, waiting for transfers between devices, shifted(): return lax.ppermute(x, axis, [(i, (i + step) % n) for i in range(n)])  1.28 us
  transfers between devices with their start and end apart: 6, of which 2 were waited for; matrix products, arithmetic and copies ran while one was open for 0% of the time, Pallas kernels for 12%

profile of v2, /device:TPU:8, one launch (start us, length us, event | category | flops | bytes accessed | tf_op | source)
XLA Modules:
  0.0 35.2 jit_solution(8339365336933901541)
XLA Ops:
  0.6 3.9 %donor.1 = (f32[16,32,128]{2,1,0:T(8,128)S(1)}, f32[384,128]{1,0:T(8,128)S(1)}, f32[384,128]{1,0:T(8,128)S(1)}, f32[3072,128]{1,0:T(8,128)S(1)}, f32[184,128]{1,0:T(8,128)S(1)}, /*index=5*/s32[8,128]{1,0:T(8,128)S(1)}) custom-call(f32[768,128]{1,0:T(8,128)} %bitcast.7, f32[2304,128]{1,0:T(8,128)} %bitcast.6, s32[1,1,16,19]{3,2,1,0:T(8,128)} %cr_hbm.1, ...), custom_call_target="tpu_custom_call" | custom-call | flops 400000000 | bytes 100000 | tf_op jit(solution)/shard_map/donor/pallas_call | solution.py:634
  4.6 0.1 collective-permute-start.4
  4.7 1.6 %collective-permute-start = (f32[384,128]{1,0:T(8,128)S(1)}, f32[384,128]{1,0:T(8,128)S(1)}, u32[]{:S(2)}, u32[]{:S(2)}) collective-permute-start(f32[384,128]{1,0:T(8,128)S(1)} %get-tuple-element.13), channel_id=1, source_target_pairs={{0,16},{16,32},{32,48},{48,64},{64,80},{80,96},{96,112},{112,0},{1... | collective-permute-start | bytes 589832 | tf_op jit(solution)/shard_map/ppermute | solution.py:620
  6.2 4.1 %collective-permute-start.1 = (f32[384,128]{1,0:T(8,128)S(1)}, f32[384,128]{1,0:T(8,128)S(1)}, u32[]{:S(2)}, u32[]{:S(2)}) collective-permute-start(f32[384,128]{1,0:T(8,128)S(1)} %get-tuple-element.14), channel_id=1, source_target_pairs={{0,112},{16,0},{32,16},{48,32},{64,48},{80,64},{96,80},{112,96},{1... | collective-permute-start | bytes 589832 | tf_op jit(solution)/shard_map/ppermute | solution.py:620
  10.4 0.0 collective-permute-done.4
  10.4 9.9 %all-to-all-start = ((f32[16,32,128]{2,1,0:T(8,128)}), f32[16,32,128]{2,1,0:T(8,128)S(1)}, u32[]{:S(2)}, u32[]{:S(2)}) async-start(f32[16,32,128]{2,1,0:T(8,128)} %collective-permute-done.4), calls=%async_computation | async-start | bytes 524288 | tf_op jit(solution)/shard_map/all_to_all | solution.py:655
  20.3 0.0 collective-permute-done.top_ref
  20.3 0.0 copy-start
  20.3 0.0 collective-permute-done.1.bot_ref
  20.4 0.0 copy-start.2
  20.4 0.6 %packs.1 = (f32[192,128]{1,0:T(8,128)S(1)}, f32[192,128]{1,0:T(8,128)S(1)}) custom-call(f32[3072,128]{1,0:T(8,128)S(1)} %get-tuple-element.12.own_ref, f32[384,128]{1,0:T(8,128)S(1)} %collective-permute-done.top_ref, f32[384,128]{1,0:T(8,128)S(1)} %collective-permute-done.1.bot_ref), custom_call_target="tpu_custom_call" | custom-call | flops 49999998976 | bytes 100000 | tf_op jit(solution)/shard_map/packs/pallas_call | solution.py:658
  21.0 0.1 copy-done
  21.0 0.1 copy-done.2
  21.1 0.0 copy-start.4
  21.1 0.0 copy-start.5
  21.1 2.7 %collective-permute-start.3 = (f32[192,128]{1,0:T(8,128)S(1)}, f32[192,128]{1,0:T(8,128)S(1)}, u32[]{:S(2)}, u32[]{:S(2)}) collective-permute-start(f32[192,128]{1,0:T(8,128)S(1)} %get-tuple-element.15.left_hbm), channel_id=1, source_target_pairs={{0,15},{1,0},{2,1},{3,2},{4,3},{5,4},{6,5},{7,6},{8,7},{9,8},{10,9... | collective-permute-start | bytes 294920 | tf_op jit(solution)/shard_map/ppermute | solution.py:620
  23.8 0.0 collective-permute-start.2
  23.8 0.0 copy-start.1
  23.8 0.9 %copy-done.1 = f32[384,128]{1,0:T(8,128)S(1)} copy-done((f32[384,128]{1,0:T(8,128)S(1)}, f32[384,128]{1,0:T(8,128)}, u32[]{:S(2)}) %copy-start.1) | copy-done | bytes 196632
  24.7 0.0 copy-start.3
  24.7 0.9 %copy-done.3 = f32[384,128]{1,0:T(8,128)S(1)} copy-done((f32[384,128]{1,0:T(8,128)S(1)}, f32[384,128]{1,0:T(8,128)}, u32[]{:S(2)}) %copy-start.3) | copy-done | bytes 196632
  25.6 3.7 %interior.1.int_ref = f32[3072,128]{1,0:T(8,128)S(1)} custom-call(f32[3072,128]{1,0:T(8,128)S(1)} %get-tuple-element.12.own_ref, f32[384,128]{1,0:T(8,128)S(1)} %copy-done.1, f32[384,128]{1,0:T(8,128)S(1)} %copy-done.3, f32[184,128]{1,0:T(8,128)S(1)} %get-tuple-element.19.geo_ref), custom_call_target="tpu_custom_call" | custom-call | flops 300000 | bytes 100000 | tf_op jit(solution)/shard_map/interior/pallas_call | solution.py:663
  29.3 0.0 copy-done.4
  29.3 0.0 copy-done.5
  29.3 0.5 %collective-permute-done.3.fromright_hbm = f32[192,128]{1,0:T(8,128)S(1)} collective-permute-done((f32[192,128]{1,0:T(8,128)S(1)}, f32[192,128]{1,0:T(8,128)S(1)}, u32[]{:S(2)}, u32[]{:S(2)}) %collective-permute-start.3) | collective-permute-done | bytes 98336 | tf_op jit(solution)/shard_map/ppermute | solution.py:620
  29.9 0.0 copy-start.6
  29.9 0.6 %copy-done.6 = f32[192,128]{1,0:T(8,128)} copy-done((f32[192,128]{1,0:T(8,128)}, f32[192,128]{1,0:T(8,128)S(1)}, u32[]{:S(2)}) %copy-start.6) | copy-done | bytes 98328
  30.5 0.7 %collective-permute-done.2.fromleft_hbm = f32[192,128]{1,0:T(8,128)} collective-permute-done((f32[192,128]{1,0:T(8,128)S(1)}, f32[192,128]{1,0:T(8,128)}, u32[]{:S(2)}, u32[]{:S(2)}) %collective-permute-start.2) | collective-permute-done | bytes 98336 | tf_op jit(solution)/shard_map/ppermute | solution.py:620
  31.3 0.0 all-to-all-done
  31.3 3.9 %edges.1 = (f32[768,128]{1,0:T(8,128)}, f32[2304,128]{1,0:T(8,128)}) custom-call(f32[3072,128]{1,0:T(8,128)S(1)} %get-tuple-element.12.own_ref, f32[192,128]{1,0:T(8,128)} %copy-done.4, f32[192,128]{1,0:T(8,128)} %copy-done.5, f32[192,128]{1,0:T(8,128)} %collective-permute-done.2.fromleft_hbm, f32[192,128]{1,0:T(8,128)} %copy-done.6, ...), custom_call_target="tpu_custom_call" | custom-call | flops 10000000 | bytes 100000 | tf_op jit(solution)/shard_map/edges/pallas_call | solution.py:667
Async XLA Ops:
  4.6 5.8 %collective-permute-start.4 = (f32[16,32,128]{2,1,0:T(8,128)S(1)}, f32[16,32,128]{2,1,0:T(8,128)}, u32[]{:S(2)}, u32[]{:S(2)}) collective-permute-start(f32[16,32,128]{2,1,0:T(8,128)S(1)} %get-tuple-element.17), channel_id=1, source_target_pairs={{0,128},{128,0},{1,129},{129,1},{2,130},{130,2},{3,131},{131,3},{4... | collective-permute-start | bytes 786440 | tf_op jit(solution)/shard_map/ppermute | solution.py:654
  4.7 15.7 %collective-permute-start = (f32[384,128]{1,0:T(8,128)S(1)}, f32[384,128]{1,0:T(8,128)S(1)}, u32[]{:S(2)}, u32[]{:S(2)}) collective-permute-start(f32[384,128]{1,0:T(8,128)S(1)} %get-tuple-element.13), channel_id=1, source_target_pairs={{0,16},{16,32},{32,48},{48,64},{64,80},{80,96},{96,112},{112,0},{1... | collective-permute-start | bytes 589832 | tf_op jit(solution)/shard_map/ppermute | solution.py:620
  6.2 14.1 %collective-permute-start.1 = (f32[384,128]{1,0:T(8,128)S(1)}, f32[384,128]{1,0:T(8,128)S(1)}, u32[]{:S(2)}, u32[]{:S(2)}) collective-permute-start(f32[384,128]{1,0:T(8,128)S(1)} %get-tuple-element.14), channel_id=1, source_target_pairs={{0,112},{16,0},{32,16},{48,32},{64,48},{80,64},{96,80},{112,96},{1... | collective-permute-start | bytes 589832 | tf_op jit(solution)/shard_map/ppermute | solution.py:620
  10.4 20.9 %all-to-all-start = ((f32[16,32,128]{2,1,0:T(8,128)}), f32[16,32,128]{2,1,0:T(8,128)S(1)}, u32[]{:S(2)}, u32[]{:S(2)}) async-start(f32[16,32,128]{2,1,0:T(8,128)} %collective-permute-done.4), calls=%async_computation | async-start | bytes 524288 | tf_op jit(solution)/shard_map/all_to_all | solution.py:655
  20.3 0.7 %copy-start = (f32[384,128]{1,0:T(8,128)}, f32[384,128]{1,0:T(8,128)S(1)}, u32[]{:S(2)}) copy-start(f32[384,128]{1,0:T(8,128)S(1)} %collective-permute-done.top_ref) | copy-start | bytes 589828
  20.4 0.7 %copy-start.2 = (f32[384,128]{1,0:T(8,128)}, f32[384,128]{1,0:T(8,128)S(1)}, u32[]{:S(2)}) copy-start(f32[384,128]{1,0:T(8,128)S(1)} %collective-permute-done.1.bot_ref) | copy-start | bytes 589828
  21.1 8.2 %copy-start.4 = (f32[192,128]{1,0:T(8,128)}, f32[192,128]{1,0:T(8,128)S(1)}, u32[]{:S(2)}) copy-start(f32[192,128]{1,0:T(8,128)S(1)} %get-tuple-element.15.left_hbm) | copy-start | bytes 294916
  21.1 8.2 %copy-start.5 = (f32[192,128]{1,0:T(8,128)}, f32[192,128]{1,0:T(8,128)S(1)}, u32[]{:S(2)}) copy-start(f32[192,128]{1,0:T(8,128)S(1)} %get-tuple-element.16.right_hbm) | copy-start | bytes 294916
  21.1 8.8 %collective-permute-start.3 = (f32[192,128]{1,0:T(8,128)S(1)}, f32[192,128]{1,0:T(8,128)S(1)}, u32[]{:S(2)}, u32[]{:S(2)}) collective-permute-start(f32[192,128]{1,0:T(8,128)S(1)} %get-tuple-element.15.left_hbm), channel_id=1, source_target_pairs={{0,15},{1,0},{2,1},{3,2},{4,3},{5,4},{6,5},{7,6},{8,7},{9,8},{10,9... | collective-permute-start | bytes 294920 | tf_op jit(solution)/shard_map/ppermute | solution.py:620
  23.8 7.5 %collective-permute-start.2 = (f32[192,128]{1,0:T(8,128)S(1)}, f32[192,128]{1,0:T(8,128)}, u32[]{:S(2)}, u32[]{:S(2)}) collective-permute-start(f32[192,128]{1,0:T(8,128)S(1)} %get-tuple-element.16.right_hbm), channel_id=1, source_target_pairs={{0,1},{1,2},{2,3},{3,4},{4,5},{5,6},{6,7},{7,8},{8,9},{9,10},{10,1... | collective-permute-start | bytes 294920 | tf_op jit(solution)/shard_map/ppermute | solution.py:620
  23.8 0.9 %copy-start.1 = (f32[384,128]{1,0:T(8,128)S(1)}, f32[384,128]{1,0:T(8,128)}, u32[]{:S(2)}) copy-start(f32[384,128]{1,0:T(8,128)} %copy-done) | copy-start | bytes 589828
  24.7 0.9 %copy-start.3 = (f32[384,128]{1,0:T(8,128)S(1)}, f32[384,128]{1,0:T(8,128)}, u32[]{:S(2)}) copy-start(f32[384,128]{1,0:T(8,128)} %copy-done.2) | copy-start | bytes 589828
  29.9 0.6 %copy-start.6 = (f32[192,128]{1,0:T(8,128)}, f32[192,128]{1,0:T(8,128)S(1)}, u32[]{:S(2)}) copy-start(f32[192,128]{1,0:T(8,128)S(1)} %collective-permute-done.3.fromright_hbm) | copy-start | bytes 294916

commit v3 on v2

--- a/solution.py
+++ b/solution.py
@@ -297,7 +297,7 @@
 
 def donor_kernel(sc_hbm, ve_hbm, cr_hbm, cc_hbm, sw_hbm, rs_hbm, lat_hbm, lon_hbm,
                  pay_ref, up_ref, dn_ref, own_ref, geo_ref, idx_ref,
-                 blk, cr, cc, sw, rs, tab, s_hi, s_lo, c_hi, c_lo, sems):
+                 blk, cr, cc, sw, rs, s_hi, s_lo, c_hi, c_lo, sent_a, sent_b, sems):
     lat, lon = lax.axis_index("lat"), lax.axis_index("lon")
     n_sc = 2 * SH * NR
     moves = [
@@ -313,35 +313,20 @@
     copies = [pltpu.make_async_copy(a, b, sems.at[i]) for i, (a, b) in enumerate(moves)]
     for c in copies:
         c.start()
-    tab[...] = jnp.zeros((NC, NC), F32)
     for c in copies[:3]:
         c.wait()
-    tab[0:16, 0:CAP] = cr[...].astype(F32)
-    tab[16:32, 0:CAP] = cc[...].astype(F32)
-    tab[32:48, 0:CAP] = sw[0]
-    tab[48:64, 0:CAP] = sw[1]
-    cols = jnp.transpose(tab[...])
-    lane = lax.broadcasted_iota(jnp.int32, (48, NC), 1).astype(F32)
-    for pair in range(N_LON // 2):
-        a, b, wt, wp = [
-            jnp.concatenate(
-                [
-                    jnp.broadcast_to(cols[0:24, o : o + 1], (24, NC))
-                    for o in (j * N_LON + 2 * pair, j * N_LON + 2 * pair + 1)
-                ],
-                axis=0,
-            )
-            for j in range(4)
-        ]
+    tables = [cr[...].astype(F32), cc[...].astype(F32), sw[0], sw[1]]
+    lane = lax.broadcasted_iota(jnp.int32, (N_LON, NC), 1).astype(F32)
+    for j in range(CAP):
+        a, b, wt, wp = [jnp.broadcast_to(x[:, j : j + 1], (N_LON, NC)) for x in tables]
         along = jnp.where(lane == b, 1.0 - wp, jnp.where(lane == b + 1.0, wp, 0.0))
         first, second = along * (1.0 - wt), along * wt
+        here = slice(N_LON * j, N_LON * j + N_LON)
         for k in range(NR):
             s = jnp.where(a == float(k), first, jnp.where(a == float(k - 1), second, 0.0))
             hi = s.astype(BF16)
-            s_hi[48 * pair : 48 * pair + 48, k * NC : (k + 1) * NC] = hi
-            s_lo[48 * pair : 48 * pair + 48, k * NC : (k + 1) * NC] = (
-                s - hi.astype(F32)
-            ).astype(BF16)
+            s_hi[here, k * NC : (k + 1) * NC] = hi
+            s_lo[here, k * NC : (k + 1) * NC] = (s - hi.astype(F32)).astype(BF16)
     for c in copies[3:]:
         c.wait()
     at = geo_ref[G_FRAME : G_FRAME + 8, :].astype(jnp.int32)
@@ -384,12 +369,15 @@
         )
 
     sent = dot(s_hi, c_hi) + dot(s_hi, c_lo) + dot(s_lo, c_hi)
+    sent_a[...] = sent[:, 0:NC]
+    sent_b[:, 0:64] = sent[:, NC : NC + 64]
     for t in range(N_LON):
-        pay_ref[t, 0:24, :] = sent[24 * t : 24 * t + 24, 0:NC]
-        part = sent[24 * t : 24 * t + 24, NC : NC + 64]
+        mine = pl.ds(t, CAP, stride=N_LON)
+        part = sent_b[mine, :]
         pay_ref[t, 24:32, :] = jnp.zeros((8, NC), F32)
-        pay_ref[t, 19:29, 0:64] = part[0:10]
-        pay_ref[t, 19:28, 64:128] = part[10:19]
+        pay_ref[t, 0:CAP, :] = sent_a[mine, :]
+        pay_ref[t, 19:29, 0:64] = part[0:10, 0:64]
+        pay_ref[t, 19:28, 64:128] = part[10:19, 0:64]
 
 
 def row_of(own_ref, top_ref, bot_ref, f, e):
@@ -400,8 +388,27 @@
     return tile(own_ref, f * NR + e - 2)
 
 
-def pack_kernel(own_ref, top_ref, bot_ref, left_ref, right_ref):
+def dense(fields, first, place):
+    out = []
+    for o in range(0, 8, 3):
+        group = None
+        for j, x in enumerate(fields[o : o + 3]):
+            at = (first + 2 * j) % 6
+            x = lane_roll(x, at - first)
+            mine = (place == at) | (place == at + 1)
+            group = x if group is None else jnp.where(mine, x, group)
+        out.append(group)
+    return out
+
+
+def undense(group, first, j):
+    return lane_roll(group, first - (first + 2 * j) % 6)
+
+
+def pack_kernel(own_ref, top_ref, bot_ref, left_ref, right_ref, go_left_ref, go_right_ref):
     lane = lax.broadcasted_iota(jnp.int32, (SH, NC), 1)
+    place = lane % 6
+    lefts, rights = [], []
     for f in range(8):
         left = jnp.zeros((SH, NC), F32)
         right = jnp.zeros((SH, NC), F32)
@@ -415,9 +422,19 @@
                 right = jnp.where((lane >= base - 2) & (lane < base + 2), x, right)
         put(left_ref, f, left)
         put(right_ref, f, right)
-
-
-def main_kernel(own_ref, top_ref, bot_ref, geo_ref, out_ref, q_ref, r_ref):
+        lefts.append(left)
+        rights.append(right)
+    for i, x in enumerate(dense(lefts, 2, place)):
+        put(go_left_ref, i, x)
+    for i, x in enumerate(dense(rights, 0, place)):
+        put(go_right_ref, i, x)
+
+
+def main_kernel(own_ref, top_ref, bot_ref, geo_ref, out_hbm, near_ref, out_ref, q_ref, r_ref, sems):
+    k0 = jnp.where(lax.axis_index("lat") == 0, 0, NR - 4)
+    for f in range(8):
+        for j in range(4):
+            put(near_ref, f * 4 + j, tile(own_ref, f * NR + k0 + j))
     yang = lax.axis_index("panel").astype(F32)
     edges = shell_edges()
 
@@ -429,22 +446,34 @@
         scal = rows_one(fields, q_ref, r_ref, EXT, geo, edges, e, full)
         if full:
             for i in range(2):
-                put(out_ref, i * NR + e - 2, scal[i])
+                put(out_ref, (e - 2) * 8 + i, scal[i])
+
+    @pl.loop(3, NR + 1)
+    def _(e):
+        one(e, True)
 
     one(1, False)
     one(2, True)
     one(NR + 1, True)
     one(NR + 2, False)
 
-    @pl.loop(3, NR + 1)
-    def _(e):
-        one(e, True)
-
-    @pl.loop(2, NR + 2)
-    def _(e):
-        vec = rows_two(q_ref, r_ref, EXT, row_geo(geo_ref, e, yang), edges, e)
-        for i in range(6):
-            put(out_ref, (2 + i) * NR + e - 2, vec[i])
+    sends = []
+    for part in range(4):
+        k0 = part * (NR // 4)
+
+        @pl.loop(k0 + 2, k0 + NR // 4 + 2)
+        def _(e):
+            vec = rows_two(q_ref, r_ref, EXT, row_geo(geo_ref, e, yang), edges, e)
+            for i in range(6):
+                put(out_ref, (e - 2) * 8 + 2 + i, vec[i])
+
+        span = pl.ds(k0 * 8 * SH, NR // 4 * 8 * SH)
+        sends.append(
+            pltpu.make_async_copy(out_ref.at[span], out_hbm.at[span], sems.at[part])
+        )
+        sends[-1].start()
+    for c in sends:
+        c.wait()
 
 
 def to_spherical(x, y, z, sin, cos, sphi, cphi):
@@ -462,9 +491,9 @@
 STRIP = 6
 
 
-def edge_kernel(own_ref, left_hbm, right_hbm, fromleft_hbm, fromright_hbm,
-                don_ref, idx_ref, geo_ref, int_ref, osc_hbm, ove_hbm,
-                out_ref, pack_ref, bord_ref, u_ref, q_ref, r_ref, sems):
+def edge_kernel(near_ref, left_ref, right_ref, fromleft_ref, fromright_ref,
+                don_ref, idx_ref, geo_ref, int_hbm, osc_hbm, ove_hbm,
+                int_ref, out_ref, bord_ref, u_ref, q_ref, r_ref, sems):
     yang = lax.axis_index("panel").astype(F32)
     lat = lax.axis_index("lat")
     lon = lax.axis_index("lon")
@@ -472,13 +501,8 @@
     row_edge = (lat == 0) | (lat == N_LAT - 1)
     col_edge = (lon == 0) | (lon == N_LON - 1)
     per = SH * NR
-    fetches = [
-        pltpu.make_async_copy(src, pack_ref.at[i], sems.at[8 + i])
-        for i, src in enumerate((left_hbm, fromleft_hbm, right_hbm, fromright_hbm))
-    ]
-    for c in fetches:
-        c.start()
-
+    fetch = pltpu.make_async_copy(int_hbm, int_ref, sems.at[8])
+    fetch.start()
     @pl.when(row_edge | col_edge)
     def _():
         recv = jnp.transpose(don_ref[...])
@@ -508,13 +532,11 @@
         w = [bord_ref[f * SH : f * SH + SH, col * NC : (col + 1) * NC] for f in range(8)]
         return border_fields(w, sin, cos, sphi, cphi)
 
-    for c in fetches:
-        c.wait()
     lane = lax.broadcasted_iota(jnp.int32, (SH, NC), 1)
     place = lane % 6
     merged = None
     for side in range(2):
-        own, other = pack_ref.at[2 * side], pack_ref.at[2 * side + 1]
+        own, other = (left_ref, fromleft_ref) if side == 0 else (right_ref, fromright_ref)
         theirs = (place < 2) if side == 0 else ((place == 2) | (place == 3))
         at = G_PACK + 4 * side
         th = [geo_ref[at + j : at + j + 1, :] for j in range(4)]
@@ -524,7 +546,8 @@
         donated = border(2 + side, th[0], th[1], ph[0], ph[1])
         u = []
         for f in range(8):
-            x = jnp.where(theirs, tile(other, f), tile(own, f))
+            x = undense(tile(other, f // 3), 2 * side, f % 3)
+            x = jnp.where(theirs, x, tile(own, f))
             u.append(jnp.where(g >= 0, donated[f], x))
         geo = Geo(geo_ref, *th, *ph, yang)
 
@@ -553,7 +576,7 @@
                 put(u_ref, f * STRIP + jnp.where(top, i, 4 + i), w[f])
         for j in range(4):
             for f in range(8):
-                x = tile(own_ref, f * NR + jnp.where(top, j, NR - 4 + j))
+                x = tile(near_ref, f * 4 + j)
                 put(u_ref, f * STRIP + jnp.where(top, 2 + j, j), x)
 
         for slot in (1, 2, 3, 4):
@@ -573,11 +596,12 @@
 
     edge_lane = (lane < 2) | (lane >= NC - 2)
     sends = []
+    fetch.wait()
     for f in range(8):
         cols = tile(u_ref, 8 * STRIP + f)
         for k in range(NR):
             x = lane_roll(cols, -(6 * (k + 2) + 2))
-            out_ref[native_row(f, k), :] = jnp.where(edge_lane, x, tile(int_ref, f * NR + k))
+            out_ref[native_row(f, k), :] = jnp.where(edge_lane, x, tile(int_ref, k * 8 + f))
 
         @pl.when(row_edge)
         def _(f=f):
@@ -596,12 +620,15 @@
 
 VM = pl.BlockSpec(memory_space=pltpu.VMEM)
 HBM = pl.BlockSpec(memory_space=pltpu.HBM)
+PINNED = pl.BlockSpec(memory_space=pltpu.HBM)
 
 
 def call(kernel, ins, outs, scratch, name, flops, mib):
     return pl.pallas_call(
         kernel,
-        out_shape=[jax.ShapeDtypeStruct(s, t) for s, t, _ in outs],
+        out_shape=[
+            pltpu.HBM(s, t) if m is PINNED else jax.ShapeDtypeStruct(s, t) for s, t, m in outs
+        ],
         in_specs=ins,
         out_specs=[o[2] for o in outs],
         scratch_shapes=scratch,
@@ -641,11 +668,12 @@
             rows(8 * NR), table, table,
             pltpu.VMEM((2, N_LON, CAP), F32),
             pltpu.VMEM((1, 1, 592), jnp.int32),
-            pltpu.VMEM((NC, NC), F32),
-            pltpu.VMEM((24 * N_LON, NR * NC), BF16),
-            pltpu.VMEM((24 * N_LON, NR * NC), BF16),
+            pltpu.VMEM((CAP * N_LON, NR * NC), BF16),
+            pltpu.VMEM((CAP * N_LON, NR * NC), BF16),
             pltpu.VMEM((8 * SH, NR * NC), BF16),
             pltpu.VMEM((8 * SH, NR * NC), BF16),
+            pltpu.VMEM((CAP * N_LON, NC), F32),
+            pltpu.VMEM((CAP * N_LON, NC), F32),
             pltpu.SemaphoreType.DMA((8,)),
         ],
         "donor", 400000000, 20,
@@ -655,27 +683,28 @@
     don = lax.all_to_all(pay, "lon", 0, 0, tiled=True).reshape(N_LON * CHUNK, NC)
     top = shifted(up, "lat", 1)
     bot = shifted(dn, "lat", -1)
-    left, right = call(pack_kernel, [VM] * 3, [pack, pack], [], "packs", 50000000000, 12)(
+    thin = ((3 * SH, NC), F32, VM)
+    left, right, go_left, go_right = call(pack_kernel, [VM] * 3, [pack, pack, thin, thin], [], "packs", 50000000000, 12)(
         own, top, bot
     )
-    from_left = shifted(right, "lon", 1)
-    from_right = shifted(left, "lon", -1)
-    (inner,) = call(
-        main_kernel, [VM] * 4, [block], [rows(12 * EXT), rows(4 * EXT)],
+    from_left = shifted(go_right, "lon", 1)
+    from_right = shifted(go_left, "lon", -1)
+    inner, near = call(
+        main_kernel, [VM] * 4, [block[:2] + (PINNED,), ((8 * 4 * SH, NC), F32, VM)],
+        [rows(8 * NR), rows(12 * EXT), rows(4 * EXT), pltpu.SemaphoreType.DMA((4,))],
         "interior", 300000, 16,
     )(own, top, bot, geo)
     osc, ove = call(
-        edge_kernel, [VM] + [HBM] * 4 + [VM] * 4,
+        edge_kernel, [VM] * 8 + [HBM],
         [(sc.shape, F32, HBM), (ve.shape, F32, HBM)],
         [
-            rows(8 * NR),
-            pltpu.VMEM((4, 8 * SH, NC), F32),
+            rows(8 * NR), rows(8 * NR),
             pltpu.VMEM((8 * SH, 4 * NC), F32),
             rows(8 * STRIP + 8), rows(12 * STRIP), rows(12 * STRIP),
-            pltpu.SemaphoreType.DMA((12,)),
+            pltpu.SemaphoreType.DMA((9,)),
         ],
         "edges", 10000000, 16,
-    )(own, *in_hbm(left, right, from_left, from_right), don, idx, geo, inner)
+    )(near, left, right, from_left, from_right, don, idx, geo, *in_hbm(inner))
     return osc.reshape(scalars.shape), ove.reshape(vectors.shape)
 
 

time: 35.8 us -> 34 us (0.950)
  local copies, waits for them, and re-layouts: 2.63 us -> 0 us
  starting transfers between devices: 18.4 us -> 20 us
  waiting for transfers between devices: 1.28 us -> 0.46 us
  Pallas kernels: 12.1 us -> 12.6 us
    unnamed x14 -> x0, local copies, waits for them, and re-layouts: 2.63 us -> none
    ppermute x4, starting transfers between devices: 8.39 us -> 9.93 us  [shifted(): return lax.ppermute(x, axis, [(i, (i + step) % n) for i in range(n)])]
    ppermute x4, waiting for transfers between devices: 1.28 us -> 0.01 us  [shifted(): return lax.ppermute(x, axis, [(i, (i + step) % n) for i in range(n)])]
    pallas_call x3, Pallas kernels: 8.2 us -> 9.11 us  [the longest x1 4.55 us: body(): call(main_kernel, [VM] * 4, [block[:2] + (PINNED,), ((8 * 4 * SH, NC), F3...]
    all_to_all x1, waiting for transfers between devices: 0.01 us -> 0.45 us  [body(): lax.all_to_all(pay, 'lon', 0, 0, tiled=True).reshape(N_LON * CHUNK, NC)]
    pallas_call x1, Pallas kernels: 3.92 us -> 3.49 us  [body(): call(donor_kernel, [HBM] * 8, [((N_LON, CHUNK, NC), F32, VM), halo, halo,...]
  transfers between devices with their start and end apart: 6 -> 6, of which waited for: 2 -> 1; matrix products, arithmetic and copies ran while one was open for 0% -> 0% of each run, Pallas kernels for 12% -> 15%
where the time goes in v3:
time: 34 us; the launch traced here: 33.7 us
  starting transfers between devices  20 us (59%)
  Pallas kernels  12.6 us (37%)
  between operations  0.69 us (2%)
  waiting for transfers between devices  0.46 us (1%)
    all_to_all x1, starting transfers between devices, body(): lax.all_to_all(pay, 'lon', 0, 0, tiled=True).reshape(N_LON * CHUNK, NC)  9.94 us
    ppermute x4, starting transfers between devices, shifted(): return lax.ppermute(x, axis, [(i, (i + step) % n) for i in range(n)])  9.93 us
    pallas_call x1, Pallas kernels, body(): call(main_kernel, [VM] * 4, [block[:2] + (PINNED,), ((8 * 4 * SH, NC), F3...  4.55 us
    pallas_call x1, Pallas kernels, body(): call(edge_kernel, [VM] * 8 + [HBM], [(sc.shape, F32, HBM), (ve.shape, F32...  3.89 us
    pallas_call x1, Pallas kernels, body(): call(donor_kernel, [HBM] * 8, [((N_LON, CHUNK, NC), F32, VM), halo, halo,...  3.49 us
  transfers between devices with their start and end apart: 6, of which 1 were waited for; matrix products, arithmetic and copies ran while one was open for 0% of the time, Pallas kernels for 15%

profile of v3, /device:TPU:8, one launch (start us, length us, event | category | flops | bytes accessed | tf_op | source)
XLA Modules:
  0.0 33.7 jit_solution(772226803952064063)
XLA Ops:
  0.6 3.5 %donor.1 = (f32[16,32,128]{2,1,0:T(8,128)S(1)}, f32[384,128]{1,0:T(8,128)S(1)}, f32[384,128]{1,0:T(8,128)S(1)}, f32[3072,128]{1,0:T(8,128)S(1)}, f32[184,128]{1,0:T(8,128)S(1)}, /*index=5*/s32[8,128]{1,0:T(8,128)S(1)}) custom-call(f32[768,128]{1,0:T(8,128)} %bitcast.7, f32[2304,128]{1,0:T(8,128)} %bitcast.6, s32[1,1,16,19]{3,2,1,0:T(8,128)} %cr_hbm.1, ...), custom_call_target="tpu_custom_call" | custom-call | flops 400000000 | bytes 100000 | tf_op jit(solution)/shard_map/donor/pallas_call | solution.py:661
  4.1 0.1 collective-permute-start.4
  4.2 1.6 %collective-permute-start = (f32[384,128]{1,0:T(8,128)S(1)}, f32[384,128]{1,0:T(8,128)S(1)}, u32[]{:S(2)}, u32[]{:S(2)}) collective-permute-start(f32[384,128]{1,0:T(8,128)S(1)} %get-tuple-element.17), channel_id=1, source_target_pairs={{0,16},{16,32},{32,48},{48,64},{64,80},{80,96},{96,112},{112,0},{1... | collective-permute-start | bytes 589832 | tf_op jit(solution)/shard_map/ppermute | solution.py:647
  5.8 4.1 %collective-permute-start.1 = (f32[384,128]{1,0:T(8,128)S(1)}, f32[384,128]{1,0:T(8,128)S(1)}, u32[]{:S(2)}, u32[]{:S(2)}) collective-permute-start(f32[384,128]{1,0:T(8,128)S(1)} %get-tuple-element.18), channel_id=1, source_target_pairs={{0,112},{16,0},{32,16},{48,32},{64,48},{80,64},{96,80},{112,96},{1... | collective-permute-start | bytes 589832 | tf_op jit(solution)/shard_map/ppermute | solution.py:647
  9.9 0.0 collective-permute-done.4
  9.9 9.9 %all-to-all-start = ((f32[16,32,128]{2,1,0:T(8,128)}), f32[16,32,128]{2,1,0:T(8,128)S(1)}, u32[]{:S(2)}, u32[]{:S(2)}) async-start(f32[16,32,128]{2,1,0:T(8,128)} %collective-permute-done.4), calls=%async_computation | async-start | bytes 524288 | tf_op jit(solution)/shard_map/all_to_all | solution.py:683
  19.9 0.0 collective-permute-done.top_ref
  19.9 0.0 collective-permute-done.1.bot_ref
  19.9 0.7 %packs.1 = (f32[192,128]{1,0:T(8,128)S(1)}, f32[192,128]{1,0:T(8,128)S(1)}, f32[72,128]{1,0:T(8,128)S(1)}, f32[72,128]{1,0:T(8,128)S(1)}) custom-call(f32[3072,128]{1,0:T(8,128)S(1)} %get-tuple-element.16.own_ref, f32[384,128]{1,0:T(8,128)S(1)} %collective-permute-done.top_ref, f32[384,128]{1,0:T(8,128)S(1)} %collective-permute-done.1.bot_ref), custom_call_target="tpu_custom_call" | custom-call | flops 49999998976 | bytes 100000 | tf_op jit(solution)/shard_map/packs/pallas_call | solution.py:687
  20.6 1.5 %collective-permute-start.2 = (f32[72,128]{1,0:T(8,128)S(1)}, f32[72,128]{1,0:T(8,128)S(1)}, u32[]{:S(2)}, u32[]{:S(2)}) collective-permute-start(f32[72,128]{1,0:T(8,128)S(1)} %get-tuple-element.23), channel_id=1, source_target_pairs={{0,1},{1,2},{2,3},{3,4},{4,5},{5,6},{6,7},{7,8},{8,9},{9,10},{10,1... | collective-permute-start | bytes 110600 | tf_op jit(solution)/shard_map/ppermute | solution.py:647
  22.1 2.7 %collective-permute-start.3 = (f32[72,128]{1,0:T(8,128)S(1)}, f32[72,128]{1,0:T(8,128)S(1)}, u32[]{:S(2)}, u32[]{:S(2)}) collective-permute-start(f32[72,128]{1,0:T(8,128)S(1)} %get-tuple-element.24), channel_id=1, source_target_pairs={{0,15},{1,0},{2,1},{3,2},{4,3},{5,4},{6,5},{7,6},{8,7},{9,8},{10,9... | collective-permute-start | bytes 110600 | tf_op jit(solution)/shard_map/ppermute | solution.py:647
  24.8 4.6 %interior.1 = (f32[3072,128]{1,0:T(8,128)}, f32[768,128]{1,0:T(8,128)S(1)}) custom-call(f32[3072,128]{1,0:T(8,128)S(1)} %get-tuple-element.16.own_ref, f32[384,128]{1,0:T(8,128)S(1)} %collective-permute-done.top_ref, f32[384,128]{1,0:T(8,128)S(1)} %collective-permute-done.1.bot_ref, f32[184,128]{1,0:T(8,128)S(1)} %get-tuple-element.19.geo_ref), custom_call_target="tpu_custom_call" | custom-call | flops 300000 | bytes 100000 | tf_op jit(solution)/shard_map/interior/pallas_call | solution.py:692
  29.4 0.0 collective-permute-done.2.fromleft_ref
  29.4 0.0 collective-permute-done.3.fromright_ref
  29.4 0.4 %all-to-all-done = f32[16,32,128]{2,1,0:T(8,128)S(1)} async-done(((f32[16,32,128]{2,1,0:T(8,128)}), f32[16,32,128]{2,1,0:T(8,128)S(1)}, u32[]{:S(2)}, u32[]{:S(2)}) %all-to-all-start) | async-done | bytes 262176 | tf_op jit(solution)/shard_map/all_to_all | solution.py:683
  29.8 3.9 %edges.1 = (f32[768,128]{1,0:T(8,128)}, f32[2304,128]{1,0:T(8,128)}) custom-call(f32[768,128]{1,0:T(8,128)S(1)} %get-tuple-element.20.near_ref, f32[192,128]{1,0:T(8,128)S(1)} %get-tuple-element.21.left_ref, f32[192,128]{1,0:T(8,128)S(1)} %get-tuple-element.22.right_ref, f32[72,128]{1,0:T(8,128)S(1)} %collective-permute-done.2.fromleft_ref, ...), custom_call_target="tpu_custom_call" | custom-call | flops 10000000 | bytes 100000 | tf_op jit(solution)/shard_map/edges/pallas_call | solution.py:697
Async XLA Ops:
  4.1 5.8 %collective-permute-start.4 = (f32[16,32,128]{2,1,0:T(8,128)S(1)}, f32[16,32,128]{2,1,0:T(8,128)}, u32[]{:S(2)}, u32[]{:S(2)}) collective-permute-start(f32[16,32,128]{2,1,0:T(8,128)S(1)} %get-tuple-element.25), channel_id=1, source_target_pairs={{0,128},{128,0},{1,129},{129,1},{2,130},{130,2},{3,131},{131,3},{4... | collective-permute-start | bytes 786440 | tf_op jit(solution)/shard_map/ppermute | solution.py:682
  4.2 15.7 %collective-permute-start = (f32[384,128]{1,0:T(8,128)S(1)}, f32[384,128]{1,0:T(8,128)S(1)}, u32[]{:S(2)}, u32[]{:S(2)}) collective-permute-start(f32[384,128]{1,0:T(8,128)S(1)} %get-tuple-element.17), channel_id=1, source_target_pairs={{0,16},{16,32},{32,48},{48,64},{64,80},{80,96},{96,112},{112,0},{1... | collective-permute-start | bytes 589832 | tf_op jit(solution)/shard_map/ppermute | solution.py:647
  5.8 14.1 %collective-permute-start.1 = (f32[384,128]{1,0:T(8,128)S(1)}, f32[384,128]{1,0:T(8,128)S(1)}, u32[]{:S(2)}, u32[]{:S(2)}) collective-permute-start(f32[384,128]{1,0:T(8,128)S(1)} %get-tuple-element.18), channel_id=1, source_target_pairs={{0,112},{16,0},{32,16},{48,32},{64,48},{80,64},{96,80},{112,96},{1... | collective-permute-start | bytes 589832 | tf_op jit(solution)/shard_map/ppermute | solution.py:647
  9.9 19.9 %all-to-all-start = ((f32[16,32,128]{2,1,0:T(8,128)}), f32[16,32,128]{2,1,0:T(8,128)S(1)}, u32[]{:S(2)}, u32[]{:S(2)}) async-start(f32[16,32,128]{2,1,0:T(8,128)} %collective-permute-done.4), calls=%async_computation | async-start | bytes 524288 | tf_op jit(solution)/shard_map/all_to_all | solution.py:683
  20.6 8.8 %collective-permute-start.2 = (f32[72,128]{1,0:T(8,128)S(1)}, f32[72,128]{1,0:T(8,128)S(1)}, u32[]{:S(2)}, u32[]{:S(2)}) collective-permute-start(f32[72,128]{1,0:T(8,128)S(1)} %get-tuple-element.23), channel_id=1, source_target_pairs={{0,1},{1,2},{2,3},{3,4},{4,5},{5,6},{6,7},{7,8},{8,9},{9,10},{10,1... | collective-permute-start | bytes 110600 | tf_op jit(solution)/shard_map/ppermute | solution.py:647
  22.1 7.2 %collective-permute-start.3 = (f32[72,128]{1,0:T(8,128)S(1)}, f32[72,128]{1,0:T(8,128)S(1)}, u32[]{:S(2)}, u32[]{:S(2)}) collective-permute-start(f32[72,128]{1,0:T(8,128)S(1)} %get-tuple-element.24), channel_id=1, source_target_pairs={{0,15},{1,0},{2,1},{3,2},{4,3},{5,4},{6,5},{7,6},{8,7},{9,8},{10,9... | collective-permute-start | bytes 110600 | tf_op jit(solution)/shard_map/ppermute | solution.py:647

commit v4 on v3

--- a/solution.py
+++ b/solution.py
@@ -291,13 +291,17 @@
     return stage_two(q, diff_t, rest, geo, edges)
 
 
+def is_even(axis):
+    return lax.rem(lax.axis_index(axis), 2) == 0
+
+
 def native_row(f, k):
     return pl.ds(f * (SH * NR) + k, SH, stride=NR)
 
 
 def donor_kernel(sc_hbm, ve_hbm, cr_hbm, cc_hbm, sw_hbm, rs_hbm, lat_hbm, lon_hbm,
-                 pay_ref, up_ref, dn_ref, own_ref, geo_ref, idx_ref,
-                 blk, cr, cc, sw, rs, s_hi, s_lo, c_hi, c_lo, sent_a, sent_b, sems):
+                 pay_ref, pair_ref, other_ref, own_ref, geo_ref, idx_ref,
+                 blk, cr, cc, sw, rs, s_all, c_hi, c_lo, sent_a, sent_b, sems):
     lat, lon = lax.axis_index("lat"), lax.axis_index("lon")
     n_sc = 2 * SH * NR
     moves = [
@@ -322,11 +326,12 @@
         along = jnp.where(lane == b, 1.0 - wp, jnp.where(lane == b + 1.0, wp, 0.0))
         first, second = along * (1.0 - wt), along * wt
         here = slice(N_LON * j, N_LON * j + N_LON)
+        below = slice(N_LON * (CAP + j), N_LON * (CAP + j) + N_LON)
         for k in range(NR):
             s = jnp.where(a == float(k), first, jnp.where(a == float(k - 1), second, 0.0))
             hi = s.astype(BF16)
-            s_hi[here, k * NC : (k + 1) * NC] = hi
-            s_lo[here, k * NC : (k + 1) * NC] = (s - hi.astype(F32)).astype(BF16)
+            s_all[here, k * NC : (k + 1) * NC] = hi
+            s_all[below, k * NC : (k + 1) * NC] = (s - hi.astype(F32)).astype(BF16)
     for c in copies[3:]:
         c.wait()
     at = geo_ref[G_FRAME : G_FRAME + 8, :].astype(jnp.int32)
@@ -345,10 +350,6 @@
         u = [blk[native_row(f, k), :] for f in range(8)]
         for f in range(8):
             put(own_ref, f * NR + k, u[f])
-        for first, ref in ((0, dn_ref), (NR - 2, up_ref)):
-            if k - first in (0, 1):
-                for f in range(8):
-                    put(ref, f * 2 + k - first, u[f])
         sin, cos = row_values(geo_ref, k + 2)[:2]
         c = [u[0], u[1]]
         for o in (2, 5):
@@ -363,12 +364,20 @@
         c_hi[:, k * NC : (k + 1) * NC] = hi
         c_lo[:, k * NC : (k + 1) * NC] = (c - hi.astype(F32)).astype(BF16)
 
+    last = jnp.where(is_even("lat"), NR - 2, 0)
+    for ref, k0 in ((pair_ref, last), (other_ref, NR - 2 - last)):
+        for f in range(8):
+            for j in range(2):
+                put(ref, f * 2 + j, tile(own_ref, f * NR + k0 + j))
+
     def dot(x, y):
         return lax.dot_general(
             x[...], y[...], (((1,), (1,)), ((), ())), preferred_element_type=F32
         )
 
-    sent = dot(s_hi, c_hi) + dot(s_hi, c_lo) + dot(s_lo, c_hi)
+    slots = CAP * N_LON
+    both = dot(s_all, c_hi)
+    sent = both[:slots] + both[slots:] + dot(s_all.at[:slots], c_lo)
     sent_a[...] = sent[:, 0:NC]
     sent_b[:, 0:64] = sent[:, NC : NC + 64]
     for t in range(N_LON):
@@ -380,11 +389,13 @@
         pay_ref[t, 19:28, 64:128] = part[10:19, 0:64]
 
 
-def row_of(own_ref, top_ref, bot_ref, f, e):
+def row_of(own_ref, pair_ref, other_ref, f, e):
     if isinstance(e, int) and e < 2:
-        return tile(top_ref, f * 2 + e)
+        at = f * 2 + e
+        return jnp.where(is_even("lat"), tile(other_ref, at), tile(pair_ref, at))
     if isinstance(e, int) and e >= NR + 2:
-        return tile(bot_ref, f * 2 + e - NR - 2)
+        at = f * 2 + e - NR - 2
+        return jnp.where(is_even("lat"), tile(pair_ref, at), tile(other_ref, at))
     return tile(own_ref, f * NR + e - 2)
 
 
@@ -405,7 +416,7 @@
     return lane_roll(group, first - (first + 2 * j) % 6)
 
 
-def pack_kernel(own_ref, top_ref, bot_ref, left_ref, right_ref, go_left_ref, go_right_ref):
+def pack_kernel(own_ref, top_ref, bot_ref, left_ref, right_ref, pair_ref, other_ref):
     lane = lax.broadcasted_iota(jnp.int32, (SH, NC), 1)
     place = lane % 6
     lefts, rights = [], []
@@ -424,10 +435,10 @@
         put(right_ref, f, right)
         lefts.append(left)
         rights.append(right)
-    for i, x in enumerate(dense(lefts, 2, place)):
-        put(go_left_ref, i, x)
-    for i, x in enumerate(dense(rights, 0, place)):
-        put(go_right_ref, i, x)
+    even = is_even("lon")
+    for i, (x, y) in enumerate(zip(dense(lefts, 2, place), dense(rights, 0, place))):
+        put(pair_ref, i, jnp.where(even, y, x))
+        put(other_ref, i, jnp.where(even, x, y))
 
 
 def main_kernel(own_ref, top_ref, bot_ref, geo_ref, out_hbm, near_ref, out_ref, q_ref, r_ref, sems):
@@ -448,26 +459,29 @@
             for i in range(2):
                 put(out_ref, (e - 2) * 8 + i, scal[i])
 
-    @pl.loop(3, NR + 1)
-    def _(e):
-        one(e, True)
+    def two(e):
+        vec = rows_two(q_ref, r_ref, EXT, row_geo(geo_ref, e, yang), edges, e)
+        for i in range(6):
+            put(out_ref, (e - 2) * 8 + 2 + i, vec[i])
 
     one(1, False)
     one(2, True)
-    one(NR + 1, True)
-    one(NR + 2, False)
-
     sends = []
+    quarter = NR // 4
     for part in range(4):
-        k0 = part * (NR // 4)
-
-        @pl.loop(k0 + 2, k0 + NR // 4 + 2)
+        first = 3 + part * quarter
+
+        @pl.loop(first, min(first + quarter, NR + 1))
         def _(e):
-            vec = rows_two(q_ref, r_ref, EXT, row_geo(geo_ref, e, yang), edges, e)
-            for i in range(6):
-                put(out_ref, (e - 2) * 8 + 2 + i, vec[i])
-
-        span = pl.ds(k0 * 8 * SH, NR // 4 * 8 * SH)
+            one(e, True)
+            two(e - 1)
+
+        if part == 3:
+            one(NR + 1, True)
+            two(NR)
+            one(NR + 2, False)
+            two(NR + 1)
+        span = pl.ds(part * quarter * 8 * SH, quarter * 8 * SH)
         sends.append(
             pltpu.make_async_copy(out_ref.at[span], out_hbm.at[span], sems.at[part])
         )
@@ -491,9 +505,9 @@
 STRIP = 6
 
 
-def edge_kernel(near_ref, left_ref, right_ref, fromleft_ref, fromright_ref,
+def edge_kernel(near_ref, left_ref, right_ref, pair_ref, other_ref,
                 don_ref, idx_ref, geo_ref, int_hbm, osc_hbm, ove_hbm,
-                int_ref, out_ref, bord_ref, u_ref, q_ref, r_ref, sems):
+                wide_ref, thin_ref, int_ref, out_ref, bord_ref, u_ref, q_ref, r_ref, sems):
     yang = lax.axis_index("panel").astype(F32)
     lat = lax.axis_index("lat")
     lon = lax.axis_index("lon")
@@ -505,28 +519,27 @@
     fetch.start()
     @pl.when(row_edge | col_edge)
     def _():
-        recv = jnp.transpose(don_ref[...])
+        for q in range(N_LON):
+            wide_ref[24 * q : 24 * q + 24, :] = don_ref[CHUNK * q : CHUNK * q + 24, :]
+            rest = don_ref[CHUNK * q + 16 : CHUNK * q + CHUNK, 0:64]
+            turned = don_ref[CHUNK * q + 16 : CHUNK * q + CHUNK, 64:NC]
+            thin_ref[24 * q + 16 : 24 * q + 24, :] = jnp.zeros((8, NC), F32)
+            thin_ref[24 * q : 24 * q + 10, 0:64] = rest[3:13]
+            thin_ref[24 * q + 10 : 24 * q + 19, 0:64] = turned[3:12]
+        recv = jnp.concatenate(
+            [jnp.transpose(wide_ref[...]), jnp.transpose(thin_ref[...])[0:64]], axis=0
+        )
         hi = recv.astype(BF16)
         lo = (recv - hi.astype(F32)).astype(BF16)
-        at = lax.broadcasted_iota(jnp.int32, (N_LON * CHUNK, NC), 0)
+        at = lax.broadcasted_iota(jnp.int32, (N_LON * 24, NC), 0)
         for col in range(4):
             g = idx_ref[col : col + 1, :]
             donor = jnp.floor((g.astype(F32) + 0.5) * (1.0 / CAP)).astype(jnp.int32)
-            slot = g - donor * CAP
-            first = donor * CHUNK + slot
-            here = jnp.where(g >= 0, first, -1)
-            low = jnp.where((g >= 0) & (slot < 10), first + 19, -1)
-            high = jnp.where((g >= 0) & (slot >= 10), first + 9, -1)
-
-            def pick(where, lo_row, hi_row):
-                hot = jnp.where(at == where, 1.0, 0.0).astype(BF16)
-                return jnp.dot(hi[lo_row:hi_row], hot, preferred_element_type=F32) + jnp.dot(
-                    lo[lo_row:hi_row], hot, preferred_element_type=F32
-                )
-
-            here_at = slice(col * NC, (col + 1) * NC)
-            bord_ref[0:NC, here_at] = pick(here, 0, NC)
-            bord_ref[NC : NC + 64, here_at] = pick(low, 0, 64) + pick(high, 64, NC)
+            where = jnp.where(g >= 0, g + donor * (24 - CAP), -1)
+            hot = jnp.where(at == where, 1.0, 0.0).astype(BF16)
+            bord_ref[:, col * NC : (col + 1) * NC] = jnp.dot(
+                hi, hot, preferred_element_type=F32
+            ) + jnp.dot(lo, hot, preferred_element_type=F32)
 
     def border(col, sin, cos, sphi, cphi):
         w = [bord_ref[f * SH : f * SH + SH, col * NC : (col + 1) * NC] for f in range(8)]
@@ -536,7 +549,8 @@
     place = lane % 6
     merged = None
     for side in range(2):
-        own, other = (left_ref, fromleft_ref) if side == 0 else (right_ref, fromright_ref)
+        own = left_ref if side == 0 else right_ref
+        paired = is_even("lon") if side == 1 else ~is_even("lon")
         theirs = (place < 2) if side == 0 else ((place == 2) | (place == 3))
         at = G_PACK + 4 * side
         th = [geo_ref[at + j : at + j + 1, :] for j in range(4)]
@@ -546,7 +560,8 @@
         donated = border(2 + side, th[0], th[1], ph[0], ph[1])
         u = []
         for f in range(8):
-            x = undense(tile(other, f // 3), 2 * side, f % 3)
+            x = jnp.where(paired, tile(pair_ref, f // 3), tile(other_ref, f // 3))
+            x = undense(x, 2 * side, f % 3)
             x = jnp.where(theirs, x, tile(own, f))
             u.append(jnp.where(g >= 0, donated[f], x))
         geo = Geo(geo_ref, *th, *ph, yang)
@@ -642,9 +657,10 @@
     return pltpu.VMEM((n * SH, NC), F32)
 
 
-def shifted(x, axis, step):
+def swapped(x, axis, first):
     n = lax.axis_size(axis)
-    return lax.ppermute(x, axis, [(i, (i + step) % n) for i in range(n)])
+    pairs = [(i, (i + 1) % n) for i in range(first, n, 2)]
+    return lax.ppermute(x, axis, pairs + [(b, a) for a, b in pairs])
 
 
 def body(scalars, vectors, corner_rows, corner_cols, send_weights, recv_source):
@@ -658,7 +674,7 @@
     def in_hbm(*arrays):
         return [pltpu.with_memory_space_constraint(a, pltpu.HBM) for a in arrays]
 
-    pay, up, dn, own, geo, idx = call(
+    pay, low, high, own, geo, idx = call(
         donor_kernel, [HBM] * 8,
         [
             ((N_LON, CHUNK, NC), F32, VM), halo, halo, block,
@@ -668,8 +684,7 @@
             rows(8 * NR), table, table,
             pltpu.VMEM((2, N_LON, CAP), F32),
             pltpu.VMEM((1, 1, 592), jnp.int32),
-            pltpu.VMEM((CAP * N_LON, NR * NC), BF16),
-            pltpu.VMEM((CAP * N_LON, NR * NC), BF16),
+            pltpu.VMEM((2 * CAP * N_LON, NR * NC), BF16),
             pltpu.VMEM((8 * SH, NR * NC), BF16),
             pltpu.VMEM((8 * SH, NR * NC), BF16),
             pltpu.VMEM((CAP * N_LON, NC), F32),
@@ -681,30 +696,28 @@
               jnp.asarray(lat_table()), jnp.asarray(lon_table())))
     pay = lax.ppermute(pay, "panel", [(0, 1), (1, 0)])
     don = lax.all_to_all(pay, "lon", 0, 0, tiled=True).reshape(N_LON * CHUNK, NC)
-    top = shifted(up, "lat", 1)
-    bot = shifted(dn, "lat", -1)
+    low, high = swapped(low, "lat", 0), swapped(high, "lat", 1)
     thin = ((3 * SH, NC), F32, VM)
-    left, right, go_left, go_right = call(pack_kernel, [VM] * 3, [pack, pack, thin, thin], [], "packs", 50000000000, 12)(
-        own, top, bot
+    left, right, near_lon, far_lon = call(pack_kernel, [VM] * 3, [pack, pack, thin, thin], [], "packs", 50000000000, 12)(
+        own, low, high
     )
-    from_left = shifted(go_right, "lon", 1)
-    from_right = shifted(go_left, "lon", -1)
+    near_lon, far_lon = swapped(near_lon, "lon", 0), swapped(far_lon, "lon", 1)
     inner, near = call(
         main_kernel, [VM] * 4, [block[:2] + (PINNED,), ((8 * 4 * SH, NC), F32, VM)],
         [rows(8 * NR), rows(12 * EXT), rows(4 * EXT), pltpu.SemaphoreType.DMA((4,))],
         "interior", 300000, 16,
-    )(own, top, bot, geo)
+    )(own, low, high, geo)
     osc, ove = call(
         edge_kernel, [VM] * 8 + [HBM],
         [(sc.shape, F32, HBM), (ve.shape, F32, HBM)],
         [
-            rows(8 * NR), rows(8 * NR),
+            rows(N_LON), rows(N_LON), rows(8 * NR), rows(8 * NR),
             pltpu.VMEM((8 * SH, 4 * NC), F32),
             rows(8 * STRIP + 8), rows(12 * STRIP), rows(12 * STRIP),
             pltpu.SemaphoreType.DMA((9,)),
         ],
         "edges", 10000000, 16,
-    )(near, left, right, from_left, from_right, don, idx, geo, *in_hbm(inner))
+    )(near, left, right, near_lon, far_lon, don, idx, geo, *in_hbm(inner))
     return osc.reshape(scalars.shape), ove.reshape(vectors.shape)
 
 

time: 34 us -> 33.2 us (0.976)
  Pallas kernels: 12.6 us -> 11 us
  waiting for transfers between devices: 0.46 us -> 1.5 us
    pallas_call x1, Pallas kernels: 4.55 us -> 3.48 us  [body(): call(main_kernel, [VM] * 4, [block[:2] + (PINNED,), ((8 * 4 * SH, NC), F3...]
    ppermute x4, waiting for transfers between devices: 0.01 us -> 0.7 us  [swapped(): return lax.ppermute(x, axis, pairs + [(b, a) for a, b in pairs])]
    all_to_all x1, waiting for transfers between devices: 0.45 us -> 0.8 us  [body(): lax.all_to_all(pay, 'lon', 0, 0, tiled=True).reshape(N_LON * CHUNK, NC)]
  transfers between devices with their start and end apart: 6 -> 6, of which waited for: 1 -> 2; matrix products, arithmetic and copies ran while one was open for 0% -> 0% of each run, Pallas kernels for 15% -> 13%
where the time goes in v4:
time: 33.2 us; the launch traced here: 32.9 us
  starting transfers between devices  19.7 us (59%)
  Pallas kernels  11 us (33%)
  waiting for transfers between devices  1.5 us (5%)
  between operations  0.69 us (2%)
    all_to_all x1, starting transfers between devices, body(): lax.all_to_all(pay, 'lon', 0, 0, tiled=True).reshape(N_LON * CHUNK, NC)  9.94 us
    ppermute x4, starting transfers between devices, swapped(): return lax.ppermute(x, axis, pairs + [(b, a) for a, b in pairs])  9.63 us
    pallas_call x1, Pallas kernels, body(): call(edge_kernel, [VM] * 8 + [HBM], [(sc.shape, F32, HBM), (ve.shape, F32...  3.63 us
    pallas_call x1, Pallas kernels, body(): call(main_kernel, [VM] * 4, [block[:2] + (PINNED,), ((8 * 4 * SH, NC), F3...  3.48 us
    pallas_call x1, Pallas kernels, body(): call(donor_kernel, [HBM] * 8, [((N_LON, CHUNK, NC), F32, VM), halo, halo,...  3.23 us
    all_to_all x1, waiting for transfers between devices, body(): lax.all_to_all(pay, 'lon', 0, 0, tiled=True).reshape(N_LON * CHUNK, NC)  0.8 us
    ppermute x4, waiting for transfers between devices, swapped(): return lax.ppermute(x, axis, pairs + [(b, a) for a, b in pairs])  0.7 us
    pallas_call x1, Pallas kernels, body(): call(pack_kernel, [VM] * 3, [pack, pack, thin, thin], [], 'packs', 500000...  0.69 us
  transfers between devices with their start and end apart: 6, of which 2 were waited for; matrix products, arithmetic and copies ran while one was open for 0% of the time, Pallas kernels for 13%

profile of v4, /device:TPU:8, one launch (start us, length us, event | category | flops | bytes accessed | tf_op | source)
XLA Modules:
  0.0 32.9 jit_solution(14563990035246318698)
XLA Ops:
  0.6 3.2 %donor.1 = (f32[16,32,128]{2,1,0:T(8,128)S(1)}, f32[384,128]{1,0:T(8,128)S(1)}, f32[384,128]{1,0:T(8,128)S(1)}, f32[3072,128]{1,0:T(8,128)S(1)}, f32[184,128]{1,0:T(8,128)S(1)}, /*index=5*/s32[8,128]{1,0:T(8,128)S(1)}) custom-call(f32[768,128]{1,0:T(8,128)} %bitcast.7, f32[2304,128]{1,0:T(8,128)} %bitcast.6, s32[1,1,16,19]{3,2,1,0:T(8,128)} %cr_hbm.1, ...), custom_call_target="tpu_custom_call" | custom-call | flops 400000000 | bytes 100000 | tf_op jit(solution)/shard_map/donor/pallas_call | solution.py:677
  3.9 0.1 collective-permute-start.4
  4.0 1.6 %collective-permute-start = (f32[384,128]{1,0:T(8,128)S(1)}, f32[384,128]{1,0:T(8,128)S(1)}, u32[]{:S(2)}, u32[]{:S(2)}) collective-permute-start(f32[384,128]{1,0:T(8,128)S(1)} %get-tuple-element.17), channel_id=1, source_target_pairs={{0,16},{32,48},{64,80},{96,112},{16,0},{48,32},{80,64},{112,96},{1... | collective-permute-start | bytes 589832 | tf_op jit(solution)/shard_map/ppermute | solution.py:663
  5.5 3.8 %collective-permute-start.1 = (f32[384,128]{1,0:T(8,128)S(1)}, f32[384,128]{1,0:T(8,128)S(1)}, u32[]{:S(2)}, u32[]{:S(2)}) collective-permute-start(f32[384,128]{1,0:T(8,128)S(1)} %get-tuple-element.18), channel_id=1, source_target_pairs={{16,32},{48,64},{80,96},{112,0},{32,16},{64,48},{96,80},{0,112},{1... | collective-permute-start | bytes 589832 | tf_op jit(solution)/shard_map/ppermute | solution.py:663
  9.4 0.0 collective-permute-done.4
  9.4 9.9 %all-to-all-start = ((f32[16,32,128]{2,1,0:T(8,128)}), f32[16,32,128]{2,1,0:T(8,128)S(1)}, u32[]{:S(2)}, u32[]{:S(2)}) async-start(f32[16,32,128]{2,1,0:T(8,128)} %collective-permute-done.4), calls=%async_computation | async-start | bytes 524288 | tf_op jit(solution)/shard_map/all_to_all | solution.py:698
  19.3 0.0 collective-permute-done.top_ref
  19.3 0.0 collective-permute-done.1.bot_ref
  19.3 0.7 %packs.1 = (f32[192,128]{1,0:T(8,128)S(1)}, f32[192,128]{1,0:T(8,128)S(1)}, f32[72,128]{1,0:T(8,128)S(1)}, f32[72,128]{1,0:T(8,128)S(1)}) custom-call(f32[3072,128]{1,0:T(8,128)S(1)} %get-tuple-element.16.own_ref, f32[384,128]{1,0:T(8,128)S(1)} %collective-permute-done.top_ref, f32[384,128]{1,0:T(8,128)S(1)} %collective-permute-done.1.bot_ref), custom_call_target="tpu_custom_call" | custom-call | flops 49999998976 | bytes 100000 | tf_op jit(solution)/shard_map/packs/pallas_call | solution.py:701
  20.0 1.6 %collective-permute-start.2 = (f32[72,128]{1,0:T(8,128)S(1)}, f32[72,128]{1,0:T(8,128)S(1)}, u32[]{:S(2)}, u32[]{:S(2)}) collective-permute-start(f32[72,128]{1,0:T(8,128)S(1)} %get-tuple-element.23), channel_id=1, source_target_pairs={{0,1},{2,3},{4,5},{6,7},{8,9},{10,11},{12,13},{14,15},{1,0},{3,2},... | collective-permute-start | bytes 110600 | tf_op jit(solution)/shard_map/ppermute | solution.py:663
  21.6 2.7 %collective-permute-start.3 = (f32[72,128]{1,0:T(8,128)S(1)}, f32[72,128]{1,0:T(8,128)S(1)}, u32[]{:S(2)}, u32[]{:S(2)}) collective-permute-start(f32[72,128]{1,0:T(8,128)S(1)} %get-tuple-element.24), channel_id=1, source_target_pairs={{1,2},{3,4},{5,6},{7,8},{9,10},{11,12},{13,14},{15,0},{2,1},{4,3},... | collective-permute-start | bytes 110600 | tf_op jit(solution)/shard_map/ppermute | solution.py:663
  24.3 3.5 %interior.1 = (f32[3072,128]{1,0:T(8,128)}, f32[768,128]{1,0:T(8,128)S(1)}) custom-call(f32[3072,128]{1,0:T(8,128)S(1)} %get-tuple-element.16.own_ref, f32[384,128]{1,0:T(8,128)S(1)} %collective-permute-done.top_ref, f32[384,128]{1,0:T(8,128)S(1)} %collective-permute-done.1.bot_ref, f32[184,128]{1,0:T(8,128)S(1)} %get-tuple-element.19.geo_ref), custom_call_target="tpu_custom_call" | custom-call | flops 300000 | bytes 100000 | tf_op jit(solution)/shard_map/interior/pallas_call | solution.py:705
  27.8 0.0 collective-permute-done.2.pair_ref
  27.8 0.7 %collective-permute-done.3.other_ref = f32[72,128]{1,0:T(8,128)S(1)} collective-permute-done((f32[72,128]{1,0:T(8,128)S(1)}, f32[72,128]{1,0:T(8,128)S(1)}, u32[]{:S(2)}, u32[]{:S(2)}) %collective-permute-start.3) | collective-permute-done | bytes 36896 | tf_op jit(solution)/shard_map/ppermute | solution.py:663
  28.5 0.8 %all-to-all-done = f32[16,32,128]{2,1,0:T(8,128)S(1)} async-done(((f32[16,32,128]{2,1,0:T(8,128)}), f32[16,32,128]{2,1,0:T(8,128)S(1)}, u32[]{:S(2)}, u32[]{:S(2)}) %all-to-all-start) | async-done | bytes 262176 | tf_op jit(solution)/shard_map/all_to_all | solution.py:698
  29.3 3.6 %edges.1 = (f32[768,128]{1,0:T(8,128)}, f32[2304,128]{1,0:T(8,128)}) custom-call(f32[768,128]{1,0:T(8,128)S(1)} %get-tuple-element.20.near_ref, f32[192,128]{1,0:T(8,128)S(1)} %get-tuple-element.21.left_ref, f32[192,128]{1,0:T(8,128)S(1)} %get-tuple-element.22.right_ref, f32[72,128]{1,0:T(8,128)S(1)} %collective-permute-done.2.pair_ref, ...), custom_call_target="tpu_custom_call" | custom-call | flops 10000000 | bytes 100000 | tf_op jit(solution)/shard_map/edges/pallas_call | solution.py:710
Async XLA Ops:
  3.9 5.5 %collective-permute-start.4 = (f32[16,32,128]{2,1,0:T(8,128)S(1)}, f32[16,32,128]{2,1,0:T(8,128)}, u32[]{:S(2)}, u32[]{:S(2)}) collective-permute-start(f32[16,32,128]{2,1,0:T(8,128)S(1)} %get-tuple-element.25), channel_id=1, source_target_pairs={{0,128},{128,0},{1,129},{129,1},{2,130},{130,2},{3,131},{131,3},{4... | collective-permute-start | bytes 786440 | tf_op jit(solution)/shard_map/ppermute | solution.py:697
  4.0 15.4 %collective-permute-start = (f32[384,128]{1,0:T(8,128)S(1)}, f32[384,128]{1,0:T(8,128)S(1)}, u32[]{:S(2)}, u32[]{:S(2)}) collective-permute-start(f32[384,128]{1,0:T(8,128)S(1)} %get-tuple-element.17), channel_id=1, source_target_pairs={{0,16},{32,48},{64,80},{96,112},{16,0},{48,32},{80,64},{112,96},{1... | collective-permute-start | bytes 589832 | tf_op jit(solution)/shard_map/ppermute | solution.py:663
  5.5 13.8 %collective-permute-start.1 = (f32[384,128]{1,0:T(8,128)S(1)}, f32[384,128]{1,0:T(8,128)S(1)}, u32[]{:S(2)}, u32[]{:S(2)}) collective-permute-start(f32[384,128]{1,0:T(8,128)S(1)} %get-tuple-element.18), channel_id=1, source_target_pairs={{16,32},{48,64},{80,96},{112,0},{32,16},{64,48},{96,80},{0,112},{1... | collective-permute-start | bytes 589832 | tf_op jit(solution)/shard_map/ppermute | solution.py:663
  9.4 19.9 %all-to-all-start = ((f32[16,32,128]{2,1,0:T(8,128)}), f32[16,32,128]{2,1,0:T(8,128)S(1)}, u32[]{:S(2)}, u32[]{:S(2)}) async-start(f32[16,32,128]{2,1,0:T(8,128)} %collective-permute-done.4), calls=%async_computation | async-start | bytes 524288 | tf_op jit(solution)/shard_map/all_to_all | solution.py:698
  20.0 7.7 %collective-permute-start.2 = (f32[72,128]{1,0:T(8,128)S(1)}, f32[72,128]{1,0:T(8,128)S(1)}, u32[]{:S(2)}, u32[]{:S(2)}) collective-permute-start(f32[72,128]{1,0:T(8,128)S(1)} %get-tuple-element.23), channel_id=1, source_target_pairs={{0,1},{2,3},{4,5},{6,7},{8,9},{10,11},{12,13},{14,15},{1,0},{3,2},... | collective-permute-start | bytes 110600 | tf_op jit(solution)/shard_map/ppermute | solution.py:663
  21.6 6.9 %collective-permute-start.3 = (f32[72,128]{1,0:T(8,128)S(1)}, f32[72,128]{1,0:T(8,128)S(1)}, u32[]{:S(2)}, u32[]{:S(2)}) collective-permute-start(f32[72,128]{1,0:T(8,128)S(1)} %get-tuple-element.24), channel_id=1, source_target_pairs={{1,2},{3,4},{5,6},{7,8},{9,10},{11,12},{13,14},{15,0},{2,1},{4,3},... | collective-permute-start | bytes 110600 | tf_op jit(solution)/shard_map/ppermute | solution.py:663

commit v5 on v4

--- a/solution.py
+++ b/solution.py
@@ -301,7 +301,7 @@
 
 def donor_kernel(sc_hbm, ve_hbm, cr_hbm, cc_hbm, sw_hbm, rs_hbm, lat_hbm, lon_hbm,
                  pay_ref, pair_ref, other_ref, own_ref, geo_ref, idx_ref,
-                 blk, cr, cc, sw, rs, s_all, c_hi, c_lo, sent_a, sent_b, sems):
+                 blk, cr, cc, sw, rs, s_all, c_hi, c_lo, sent_a, sent_b, chunk, sems):
     lat, lon = lax.axis_index("lat"), lax.axis_index("lon")
     n_sc = 2 * SH * NR
     moves = [
@@ -378,15 +378,17 @@
     slots = CAP * N_LON
     both = dot(s_all, c_hi)
     sent = both[:slots] + both[slots:] + dot(s_all.at[:slots], c_lo)
-    sent_a[...] = sent[:, 0:NC]
-    sent_b[:, 0:64] = sent[:, NC : NC + 64]
+    sent_a[0:slots, :] = sent[:, 0:NC]
+    sent_b[0:slots, 0:64] = sent[:, NC : NC + 64]
     for t in range(N_LON):
         mine = pl.ds(t, CAP, stride=N_LON)
         part = sent_b[mine, :]
-        pay_ref[t, 24:32, :] = jnp.zeros((8, NC), F32)
-        pay_ref[t, 0:CAP, :] = sent_a[mine, :]
-        pay_ref[t, 19:29, 0:64] = part[0:10, 0:64]
-        pay_ref[t, 19:28, 64:128] = part[10:19, 0:64]
+        at = CHUNK * t
+        chunk[at + 24 : at + 32, :] = jnp.zeros((8, NC), F32)
+        chunk[at : at + CAP, :] = sent_a[mine, :]
+        chunk[at + 19 : at + 29, 0:64] = part[0:10, 0:64]
+        chunk[at + 19 : at + 28, 64:128] = part[10:19, 0:64]
+        pay_ref[t] = chunk[at : at + CHUNK, :]
 
 
 def row_of(own_ref, pair_ref, other_ref, f, e):
@@ -527,7 +529,7 @@
             thin_ref[24 * q : 24 * q + 10, 0:64] = rest[3:13]
             thin_ref[24 * q + 10 : 24 * q + 19, 0:64] = turned[3:12]
         recv = jnp.concatenate(
-            [jnp.transpose(wide_ref[...]), jnp.transpose(thin_ref[...])[0:64]], axis=0
+            [jnp.transpose(wide_ref[...]), jnp.transpose(thin_ref[0 : 24 * N_LON, :])[0:64]], axis=0
         )
         hi = recv.astype(BF16)
         lo = (recv - hi.astype(F32)).astype(BF16)
@@ -687,8 +689,8 @@
             pltpu.VMEM((2 * CAP * N_LON, NR * NC), BF16),
             pltpu.VMEM((8 * SH, NR * NC), BF16),
             pltpu.VMEM((8 * SH, NR * NC), BF16),
-            pltpu.VMEM((CAP * N_LON, NC), F32),
-            pltpu.VMEM((CAP * N_LON, NC), F32),
+            rows(N_LON), rows(N_LON),
+            pltpu.VMEM((CHUNK * (N_LON + 1), NC), F32),
             pltpu.SemaphoreType.DMA((8,)),
         ],
         "donor", 400000000, 20,
@@ -711,7 +713,7 @@
         edge_kernel, [VM] * 8 + [HBM],
         [(sc.shape, F32, HBM), (ve.shape, F32, HBM)],
         [
-            rows(N_LON), rows(N_LON), rows(8 * NR), rows(8 * NR),
+            rows(N_LON), rows(N_LON + 1), rows(8 * NR), rows(8 * NR),
             pltpu.VMEM((8 * SH, 4 * NC), F32),
             rows(8 * STRIP + 8), rows(12 * STRIP), rows(12 * STRIP),
             pltpu.SemaphoreType.DMA((9,)),

time: 33.2 us -> 33.2 us (level)
  no operation moved by 1% of the time
where the time goes in v5:
time: 33.2 us; the launch traced here: 32.9 us
  starting transfers between devices  19.7 us (59%)
  Pallas kernels  11.1 us (33%)
  waiting for transfers between devices  1.5 us (5%)
  between operations  0.69 us (2%)
    all_to_all x1, starting transfers between devices, body(): lax.all_to_all(pay, 'lon', 0, 0, tiled=True).reshape(N_LON * CHUNK, NC)  9.94 us
    ppermute x4, starting transfers between devices, swapped(): return lax.ppermute(x, axis, pairs + [(b, a) for a, b in pairs])  9.63 us
    pallas_call x1, Pallas kernels, body(): call(edge_kernel, [VM] * 8 + [HBM], [(sc.shape, F32, HBM), (ve.shape, F32...  3.63 us
    pallas_call x1, Pallas kernels, body(): call(main_kernel, [VM] * 4, [block[:2] + (PINNED,), ((8 * 4 * SH, NC), F3...  3.48 us
    pallas_call x1, Pallas kernels, body(): call(donor_kernel, [HBM] * 8, [((N_LON, CHUNK, NC), F32, VM), halo, halo,...  3.25 us
    all_to_all x1, waiting for transfers between devices, body(): lax.all_to_all(pay, 'lon', 0, 0, tiled=True).reshape(N_LON * CHUNK, NC)  0.8 us
    ppermute x4, waiting for transfers between devices, swapped(): return lax.ppermute(x, axis, pairs + [(b, a) for a, b in pairs])  0.7 us
    pallas_call x1, Pallas kernels, body(): call(pack_kernel, [VM] * 3, [pack, pack, thin, thin], [], 'packs', 500000...  0.69 us
  transfers between devices with their start and end apart: 6, of which 2 were waited for; matrix products, arithmetic and copies ran while one was open for 0% of the time, Pallas kernels for 13%

profile of v5, /device:TPU:8, one launch (start us, length us, event | category | flops | bytes accessed | tf_op | source)
XLA Modules:
  0.0 32.9 jit_solution(7632273393650346227)
XLA Ops:
  0.6 3.3 %donor.1 = (f32[16,32,128]{2,1,0:T(8,128)S(1)}, f32[384,128]{1,0:T(8,128)S(1)}, f32[384,128]{1,0:T(8,128)S(1)}, f32[3072,128]{1,0:T(8,128)S(1)}, f32[184,128]{1,0:T(8,128)S(1)}, /*index=5*/s32[8,128]{1,0:T(8,128)S(1)}) custom-call(f32[768,128]{1,0:T(8,128)} %bitcast.7, f32[2304,128]{1,0:T(8,128)} %bitcast.6, s32[1,1,16,19]{3,2,1,0:T(8,128)} %cr_hbm.1, ...), custom_call_target="tpu_custom_call" | custom-call | flops 400000000 | bytes 100000 | tf_op jit(solution)/shard_map/donor/pallas_call | solution.py:679
  3.9 0.1 collective-permute-start.4
  4.0 1.6 %collective-permute-start = (f32[384,128]{1,0:T(8,128)S(1)}, f32[384,128]{1,0:T(8,128)S(1)}, u32[]{:S(2)}, u32[]{:S(2)}) collective-permute-start(f32[384,128]{1,0:T(8,128)S(1)} %get-tuple-element.17), channel_id=1, source_target_pairs={{0,16},{32,48},{64,80},{96,112},{16,0},{48,32},{80,64},{112,96},{1... | collective-permute-start | bytes 589832 | tf_op jit(solution)/shard_map/ppermute | solution.py:665
  5.6 3.8 %collective-permute-start.1 = (f32[384,128]{1,0:T(8,128)S(1)}, f32[384,128]{1,0:T(8,128)S(1)}, u32[]{:S(2)}, u32[]{:S(2)}) collective-permute-start(f32[384,128]{1,0:T(8,128)S(1)} %get-tuple-element.18), channel_id=1, source_target_pairs={{16,32},{48,64},{80,96},{112,0},{32,16},{64,48},{96,80},{0,112},{1... | collective-permute-start | bytes 589832 | tf_op jit(solution)/shard_map/ppermute | solution.py:665
  9.4 0.0 collective-permute-done.4
  9.4 9.9 %all-to-all-start = ((f32[16,32,128]{2,1,0:T(8,128)}), f32[16,32,128]{2,1,0:T(8,128)S(1)}, u32[]{:S(2)}, u32[]{:S(2)}) async-start(f32[16,32,128]{2,1,0:T(8,128)} %collective-permute-done.4), calls=%async_computation | async-start | bytes 524288 | tf_op jit(solution)/shard_map/all_to_all | solution.py:700
  19.4 0.0 collective-permute-done.top_ref
  19.4 0.0 collective-permute-done.1.bot_ref
  19.4 0.7 %packs.1 = (f32[192,128]{1,0:T(8,128)S(1)}, f32[192,128]{1,0:T(8,128)S(1)}, f32[72,128]{1,0:T(8,128)S(1)}, f32[72,128]{1,0:T(8,128)S(1)}) custom-call(f32[3072,128]{1,0:T(8,128)S(1)} %get-tuple-element.16.own_ref, f32[384,128]{1,0:T(8,128)S(1)} %collective-permute-done.top_ref, f32[384,128]{1,0:T(8,128)S(1)} %collective-permute-done.1.bot_ref), custom_call_target="tpu_custom_call" | custom-call | flops 49999998976 | bytes 100000 | tf_op jit(solution)/shard_map/packs/pallas_call | solution.py:703
  20.1 1.6 %collective-permute-start.2 = (f32[72,128]{1,0:T(8,128)S(1)}, f32[72,128]{1,0:T(8,128)S(1)}, u32[]{:S(2)}, u32[]{:S(2)}) collective-permute-start(f32[72,128]{1,0:T(8,128)S(1)} %get-tuple-element.23), channel_id=1, source_target_pairs={{0,1},{2,3},{4,5},{6,7},{8,9},{10,11},{12,13},{14,15},{1,0},{3,2},... | collective-permute-start | bytes 110600 | tf_op jit(solution)/shard_map/ppermute | solution.py:665
  21.6 2.7 %collective-permute-start.3 = (f32[72,128]{1,0:T(8,128)S(1)}, f32[72,128]{1,0:T(8,128)S(1)}, u32[]{:S(2)}, u32[]{:S(2)}) collective-permute-start(f32[72,128]{1,0:T(8,128)S(1)} %get-tuple-element.24), channel_id=1, source_target_pairs={{1,2},{3,4},{5,6},{7,8},{9,10},{11,12},{13,14},{15,0},{2,1},{4,3},... | collective-permute-start | bytes 110600 | tf_op jit(solution)/shard_map/ppermute | solution.py:665
  24.3 3.5 %interior.1 = (f32[3072,128]{1,0:T(8,128)}, f32[768,128]{1,0:T(8,128)S(1)}) custom-call(f32[3072,128]{1,0:T(8,128)S(1)} %get-tuple-element.16.own_ref, f32[384,128]{1,0:T(8,128)S(1)} %collective-permute-done.top_ref, f32[384,128]{1,0:T(8,128)S(1)} %collective-permute-done.1.bot_ref, f32[184,128]{1,0:T(8,128)S(1)} %get-tuple-element.19.geo_ref), custom_call_target="tpu_custom_call" | custom-call | flops 300000 | bytes 100000 | tf_op jit(solution)/shard_map/interior/pallas_call | solution.py:707
  27.8 0.0 collective-permute-done.2.pair_ref
  27.8 0.7 %collective-permute-done.3.other_ref = f32[72,128]{1,0:T(8,128)S(1)} collective-permute-done((f32[72,128]{1,0:T(8,128)S(1)}, f32[72,128]{1,0:T(8,128)S(1)}, u32[]{:S(2)}, u32[]{:S(2)}) %collective-permute-start.3) | collective-permute-done | bytes 36896 | tf_op jit(solution)/shard_map/ppermute | solution.py:665
  28.5 0.8 %all-to-all-done = f32[16,32,128]{2,1,0:T(8,128)S(1)} async-done(((f32[16,32,128]{2,1,0:T(8,128)}), f32[16,32,128]{2,1,0:T(8,128)S(1)}, u32[]{:S(2)}, u32[]{:S(2)}) %all-to-all-start) | async-done | bytes 262176 | tf_op jit(solution)/shard_map/all_to_all | solution.py:700
  29.3 3.6 %edges.1 = (f32[768,128]{1,0:T(8,128)}, f32[2304,128]{1,0:T(8,128)}) custom-call(f32[768,128]{1,0:T(8,128)S(1)} %get-tuple-element.20.near_ref, f32[192,128]{1,0:T(8,128)S(1)} %get-tuple-element.21.left_ref, f32[192,128]{1,0:T(8,128)S(1)} %get-tuple-element.22.right_ref, f32[72,128]{1,0:T(8,128)S(1)} %collective-permute-done.2.pair_ref, ...), custom_call_target="tpu_custom_call" | custom-call | flops 10000000 | bytes 100000 | tf_op jit(solution)/shard_map/edges/pallas_call | solution.py:712
Async XLA Ops:
  3.9 5.5 %collective-permute-start.4 = (f32[16,32,128]{2,1,0:T(8,128)S(1)}, f32[16,32,128]{2,1,0:T(8,128)}, u32[]{:S(2)}, u32[]{:S(2)}) collective-permute-start(f32[16,32,128]{2,1,0:T(8,128)S(1)} %get-tuple-element.25), channel_id=1, source_target_pairs={{0,128},{128,0},{1,129},{129,1},{2,130},{130,2},{3,131},{131,3},{4... | collective-permute-start | bytes 786440 | tf_op jit(solution)/shard_map/ppermute | solution.py:699
  4.0 15.4 %collective-permute-start = (f32[384,128]{1,0:T(8,128)S(1)}, f32[384,128]{1,0:T(8,128)S(1)}, u32[]{:S(2)}, u32[]{:S(2)}) collective-permute-start(f32[384,128]{1,0:T(8,128)S(1)} %get-tuple-element.17), channel_id=1, source_target_pairs={{0,16},{32,48},{64,80},{96,112},{16,0},{48,32},{80,64},{112,96},{1... | collective-permute-start | bytes 589832 | tf_op jit(solution)/shard_map/ppermute | solution.py:665
  5.6 13.8 %collective-permute-start.1 = (f32[384,128]{1,0:T(8,128)S(1)}, f32[384,128]{1,0:T(8,128)S(1)}, u32[]{:S(2)}, u32[]{:S(2)}) collective-permute-start(f32[384,128]{1,0:T(8,128)S(1)} %get-tuple-element.18), channel_id=1, source_target_pairs={{16,32},{48,64},{80,96},{112,0},{32,16},{64,48},{96,80},{0,112},{1... | collective-permute-start | bytes 589832 | tf_op jit(solution)/shard_map/ppermute | solution.py:665
  9.4 19.9 %all-to-all-start = ((f32[16,32,128]{2,1,0:T(8,128)}), f32[16,32,128]{2,1,0:T(8,128)S(1)}, u32[]{:S(2)}, u32[]{:S(2)}) async-start(f32[16,32,128]{2,1,0:T(8,128)} %collective-permute-done.4), calls=%async_computation | async-start | bytes 524288 | tf_op jit(solution)/shard_map/all_to_all | solution.py:700
  20.1 7.7 %collective-permute-start.2 = (f32[72,128]{1,0:T(8,128)S(1)}, f32[72,128]{1,0:T(8,128)S(1)}, u32[]{:S(2)}, u32[]{:S(2)}) collective-permute-start(f32[72,128]{1,0:T(8,128)S(1)} %get-tuple-element.23), channel_id=1, source_target_pairs={{0,1},{2,3},{4,5},{6,7},{8,9},{10,11},{12,13},{14,15},{1,0},{3,2},... | collective-permute-start | bytes 110600 | tf_op jit(solution)/shard_map/ppermute | solution.py:665
  21.6 6.9 %collective-permute-start.3 = (f32[72,128]{1,0:T(8,128)S(1)}, f32[72,128]{1,0:T(8,128)S(1)}, u32[]{:S(2)}, u32[]{:S(2)}) collective-permute-start(f32[72,128]{1,0:T(8,128)S(1)} %get-tuple-element.24), channel_id=1, source_target_pairs={{1,2},{3,4},{5,6},{7,8},{9,10},{11,12},{13,14},{15,0},{2,1},{4,3},... | collective-permute-start | bytes 110600 | tf_op jit(solution)/shard_map/ppermute | solution.py:665

commit v6 on v5

--- a/solution.py
+++ b/solution.py
@@ -532,16 +532,15 @@
             [jnp.transpose(wide_ref[...]), jnp.transpose(thin_ref[0 : 24 * N_LON, :])[0:64]], axis=0
         )
         hi = recv.astype(BF16)
-        lo = (recv - hi.astype(F32)).astype(BF16)
+        halves = jnp.concatenate([hi, (recv - hi.astype(F32)).astype(BF16)], axis=0)
         at = lax.broadcasted_iota(jnp.int32, (N_LON * 24, NC), 0)
         for col in range(4):
             g = idx_ref[col : col + 1, :]
             donor = jnp.floor((g.astype(F32) + 0.5) * (1.0 / CAP)).astype(jnp.int32)
             where = jnp.where(g >= 0, g + donor * (24 - CAP), -1)
             hot = jnp.where(at == where, 1.0, 0.0).astype(BF16)
-            bord_ref[:, col * NC : (col + 1) * NC] = jnp.dot(
-                hi, hot, preferred_element_type=F32
-            ) + jnp.dot(lo, hot, preferred_element_type=F32)
+            both = jnp.dot(halves, hot, preferred_element_type=F32)
+            bord_ref[:, col * NC : (col + 1) * NC] = both[: 8 * SH] + both[8 * SH :]
 
     def border(col, sin, cos, sphi, cphi):
         w = [bord_ref[f * SH : f * SH + SH, col * NC : (col + 1) * NC] for f in range(8)]

time: 33.2 us -> 33.2 us (level)
  no operation moved by 1% of the time
where the time goes in v6:
time: 33.2 us; the launch traced here: 32.9 us
  starting transfers between devices  19.7 us (59%)
  Pallas kernels  11 us (33%)
  waiting for transfers between devices  1.5 us (5%)
  between operations  0.69 us (2%)
    all_to_all x1, starting transfers between devices, body(): lax.all_to_all(pay, 'lon', 0, 0, tiled=True).reshape(N_LON * CHUNK, NC)  9.94 us
    ppermute x4, starting transfers between devices, swapped(): return lax.ppermute(x, axis, pairs + [(b, a) for a, b in pairs])  9.63 us
    pallas_call x1, Pallas kernels, body(): call(edge_kernel, [VM] * 8 + [HBM], [(sc.shape, F32, HBM), (ve.shape, F32...  3.61 us
    pallas_call x1, Pallas kernels, body(): call(main_kernel, [VM] * 4, [block[:2] + (PINNED,), ((8 * 4 * SH, NC), F3...  3.48 us
    pallas_call x1, Pallas kernels, body(): call(donor_kernel, [HBM] * 8, [((N_LON, CHUNK, NC), F32, VM), halo, halo,...  3.25 us
    all_to_all x1, waiting for transfers between devices, body(): lax.all_to_all(pay, 'lon', 0, 0, tiled=True).reshape(N_LON * CHUNK, NC)  0.8 us
    ppermute x4, waiting for transfers between devices, swapped(): return lax.ppermute(x, axis, pairs + [(b, a) for a, b in pairs])  0.7 us
    pallas_call x1, Pallas kernels, body(): call(pack_kernel, [VM] * 3, [pack, pack, thin, thin], [], 'packs', 500000...  0.69 us
  transfers between devices with their start and end apart: 6, of which 2 were waited for; matrix products, arithmetic and copies ran while one was open for 0% of the time, Pallas kernels for 13%

profile of v6, /device:TPU:8, one launch (start us, length us, event | category | flops | bytes accessed | tf_op | source)
XLA Modules:
  0.0 32.9 jit_solution(7972914638605537766)
XLA Ops:
  0.6 3.3 %donor.1 = (f32[16,32,128]{2,1,0:T(8,128)S(1)}, f32[384,128]{1,0:T(8,128)S(1)}, f32[384,128]{1,0:T(8,128)S(1)}, f32[3072,128]{1,0:T(8,128)S(1)}, f32[184,128]{1,0:T(8,128)S(1)}, /*index=5*/s32[8,128]{1,0:T(8,128)S(1)}) custom-call(f32[768,128]{1,0:T(8,128)} %bitcast.7, f32[2304,128]{1,0:T(8,128)} %bitcast.6, s32[1,1,16,19]{3,2,1,0:T(8,128)} %cr_hbm.1, ...), custom_call_target="tpu_custom_call" | custom-call | flops 400000000 | bytes 100000 | tf_op jit(solution)/shard_map/donor/pallas_call | solution.py:678
  3.9 0.1 collective-permute-start.4
  4.0 1.6 %collective-permute-start = (f32[384,128]{1,0:T(8,128)S(1)}, f32[384,128]{1,0:T(8,128)S(1)}, u32[]{:S(2)}, u32[]{:S(2)}) collective-permute-start(f32[384,128]{1,0:T(8,128)S(1)} %get-tuple-element.17), channel_id=1, source_target_pairs={{0,16},{32,48},{64,80},{96,112},{16,0},{48,32},{80,64},{112,96},{1... | collective-permute-start | bytes 589832 | tf_op jit(solution)/shard_map/ppermute | solution.py:664
  5.6 3.8 %collective-permute-start.1 = (f32[384,128]{1,0:T(8,128)S(1)}, f32[384,128]{1,0:T(8,128)S(1)}, u32[]{:S(2)}, u32[]{:S(2)}) collective-permute-start(f32[384,128]{1,0:T(8,128)S(1)} %get-tuple-element.18), channel_id=1, source_target_pairs={{16,32},{48,64},{80,96},{112,0},{32,16},{64,48},{96,80},{0,112},{1... | collective-permute-start | bytes 589832 | tf_op jit(solution)/shard_map/ppermute | solution.py:664
  9.4 0.0 collective-permute-done.4
  9.4 9.9 %all-to-all-start = ((f32[16,32,128]{2,1,0:T(8,128)}), f32[16,32,128]{2,1,0:T(8,128)S(1)}, u32[]{:S(2)}, u32[]{:S(2)}) async-start(f32[16,32,128]{2,1,0:T(8,128)} %collective-permute-done.4), calls=%async_computation | async-start | bytes 524288 | tf_op jit(solution)/shard_map/all_to_all | solution.py:699
  19.4 0.0 collective-permute-done.top_ref
  19.4 0.0 collective-permute-done.1.bot_ref
  19.4 0.7 %packs.1 = (f32[192,128]{1,0:T(8,128)S(1)}, f32[192,128]{1,0:T(8,128)S(1)}, f32[72,128]{1,0:T(8,128)S(1)}, f32[72,128]{1,0:T(8,128)S(1)}) custom-call(f32[3072,128]{1,0:T(8,128)S(1)} %get-tuple-element.16.own_ref, f32[384,128]{1,0:T(8,128)S(1)} %collective-permute-done.top_ref, f32[384,128]{1,0:T(8,128)S(1)} %collective-permute-done.1.bot_ref), custom_call_target="tpu_custom_call" | custom-call | flops 49999998976 | bytes 100000 | tf_op jit(solution)/shard_map/packs/pallas_call | solution.py:702
  20.1 1.6 %collective-permute-start.2 = (f32[72,128]{1,0:T(8,128)S(1)}, f32[72,128]{1,0:T(8,128)S(1)}, u32[]{:S(2)}, u32[]{:S(2)}) collective-permute-start(f32[72,128]{1,0:T(8,128)S(1)} %get-tuple-element.23), channel_id=1, source_target_pairs={{0,1},{2,3},{4,5},{6,7},{8,9},{10,11},{12,13},{14,15},{1,0},{3,2},... | collective-permute-start | bytes 110600 | tf_op jit(solution)/shard_map/ppermute | solution.py:664
  21.6 2.7 %collective-permute-start.3 = (f32[72,128]{1,0:T(8,128)S(1)}, f32[72,128]{1,0:T(8,128)S(1)}, u32[]{:S(2)}, u32[]{:S(2)}) collective-permute-start(f32[72,128]{1,0:T(8,128)S(1)} %get-tuple-element.24), channel_id=1, source_target_pairs={{1,2},{3,4},{5,6},{7,8},{9,10},{11,12},{13,14},{15,0},{2,1},{4,3},... | collective-permute-start | bytes 110600 | tf_op jit(solution)/shard_map/ppermute | solution.py:664
  24.3 3.5 %interior.1 = (f32[3072,128]{1,0:T(8,128)}, f32[768,128]{1,0:T(8,128)S(1)}) custom-call(f32[3072,128]{1,0:T(8,128)S(1)} %get-tuple-element.16.own_ref, f32[384,128]{1,0:T(8,128)S(1)} %collective-permute-done.top_ref, f32[384,128]{1,0:T(8,128)S(1)} %collective-permute-done.1.bot_ref, f32[184,128]{1,0:T(8,128)S(1)} %get-tuple-element.19.geo_ref), custom_call_target="tpu_custom_call" | custom-call | flops 300000 | bytes 100000 | tf_op jit(solution)/shard_map/interior/pallas_call | solution.py:706
  27.8 0.0 collective-permute-done.2.pair_ref
  27.8 0.7 %collective-permute-done.3.other_ref = f32[72,128]{1,0:T(8,128)S(1)} collective-permute-done((f32[72,128]{1,0:T(8,128)S(1)}, f32[72,128]{1,0:T(8,128)S(1)}, u32[]{:S(2)}, u32[]{:S(2)}) %collective-permute-start.3) | collective-permute-done | bytes 36896 | tf_op jit(solution)/shard_map/ppermute | solution.py:664
  28.5 0.8 %all-to-all-done = f32[16,32,128]{2,1,0:T(8,128)S(1)} async-done(((f32[16,32,128]{2,1,0:T(8,128)}), f32[16,32,128]{2,1,0:T(8,128)S(1)}, u32[]{:S(2)}, u32[]{:S(2)}) %all-to-all-start) | async-done | bytes 262176 | tf_op jit(solution)/shard_map/all_to_all | solution.py:699
  29.3 3.6 %edges.1 = (f32[768,128]{1,0:T(8,128)}, f32[2304,128]{1,0:T(8,128)}) custom-call(f32[768,128]{1,0:T(8,128)S(1)} %get-tuple-element.20.near_ref, f32[192,128]{1,0:T(8,128)S(1)} %get-tuple-element.21.left_ref, f32[192,128]{1,0:T(8,128)S(1)} %get-tuple-element.22.right_ref, f32[72,128]{1,0:T(8,128)S(1)} %collective-permute-done.2.pair_ref, ...), custom_call_target="tpu_custom_call" | custom-call | flops 10000000 | bytes 100000 | tf_op jit(solution)/shard_map/edges/pallas_call | solution.py:711
Async XLA Ops:
  3.9 5.5 %collective-permute-start.4 = (f32[16,32,128]{2,1,0:T(8,128)S(1)}, f32[16,32,128]{2,1,0:T(8,128)}, u32[]{:S(2)}, u32[]{:S(2)}) collective-permute-start(f32[16,32,128]{2,1,0:T(8,128)S(1)} %get-tuple-element.25), channel_id=1, source_target_pairs={{0,128},{128,0},{1,129},{129,1},{2,130},{130,2},{3,131},{131,3},{4... | collective-permute-start | bytes 786440 | tf_op jit(solution)/shard_map/ppermute | solution.py:698
  4.0 15.4 %collective-permute-start = (f32[384,128]{1,0:T(8,128)S(1)}, f32[384,128]{1,0:T(8,128)S(1)}, u32[]{:S(2)}, u32[]{:S(2)}) collective-permute-start(f32[384,128]{1,0:T(8,128)S(1)} %get-tuple-element.17), channel_id=1, source_target_pairs={{0,16},{32,48},{64,80},{96,112},{16,0},{48,32},{80,64},{112,96},{1... | collective-permute-start | bytes 589832 | tf_op jit(solution)/shard_map/ppermute | solution.py:664
  5.6 13.8 %collective-permute-start.1 = (f32[384,128]{1,0:T(8,128)S(1)}, f32[384,128]{1,0:T(8,128)S(1)}, u32[]{:S(2)}, u32[]{:S(2)}) collective-permute-start(f32[384,128]{1,0:T(8,128)S(1)} %get-tuple-element.18), channel_id=1, source_target_pairs={{16,32},{48,64},{80,96},{112,0},{32,16},{64,48},{96,80},{0,112},{1... | collective-permute-start | bytes 589832 | tf_op jit(solution)/shard_map/ppermute | solution.py:664
  9.4 19.9 %all-to-all-start = ((f32[16,32,128]{2,1,0:T(8,128)}), f32[16,32,128]{2,1,0:T(8,128)S(1)}, u32[]{:S(2)}, u32[]{:S(2)}) async-start(f32[16,32,128]{2,1,0:T(8,128)} %collective-permute-done.4), calls=%async_computation | async-start | bytes 524288 | tf_op jit(solution)/shard_map/all_to_all | solution.py:699
  20.1 7.7 %collective-permute-start.2 = (f32[72,128]{1,0:T(8,128)S(1)}, f32[72,128]{1,0:T(8,128)S(1)}, u32[]{:S(2)}, u32[]{:S(2)}) collective-permute-start(f32[72,128]{1,0:T(8,128)S(1)} %get-tuple-element.23), channel_id=1, source_target_pairs={{0,1},{2,3},{4,5},{6,7},{8,9},{10,11},{12,13},{14,15},{1,0},{3,2},... | collective-permute-start | bytes 110600 | tf_op jit(solution)/shard_map/ppermute | solution.py:664
  21.6 6.9 %collective-permute-start.3 = (f32[72,128]{1,0:T(8,128)S(1)}, f32[72,128]{1,0:T(8,128)S(1)}, u32[]{:S(2)}, u32[]{:S(2)}) collective-permute-start(f32[72,128]{1,0:T(8,128)S(1)} %get-tuple-element.24), channel_id=1, source_target_pairs={{1,2},{3,4},{5,6},{7,8},{9,10},{11,12},{13,14},{15,0},{2,1},{4,3},... | collective-permute-start | bytes 110600 | tf_op jit(solution)/shard_map/ppermute | solution.py:664
